TPU v7x, 32 devices: a whole 2x2x4 slice. The times are simulated.
32 devices in a mesh: rep: 8 (over y, x, core), fsdp: 4 (over z).
Axes of the slice: x: 2, y: 2, z: 4, core: 2. Of those that a mesh axis runs over, the one named last changes fastest.
Arguments:
- tokens: bfloat16 [4096, 1600], P(('rep', 'fsdp')), may hold values from -6 to 6
- cotangent: bfloat16 [4096, 1600], P(('rep', 'fsdp')), may hold values from -6 to 6
- lengths: int32 [32, 3], P(('rep', 'fsdp')), may hold values from 1 to 96, 128 in all within a row
- source_slot: int32 [32, 128], P(('rep', 'fsdp')), may hold values from 0 to 127, each once within a row
- norm_in: float32 [1600], replicated, may hold values from 0.5 to 1.5
- w_qkv: bfloat16 [1600, 2240], P('fsdp'), may hold values from -0.15625 to 0.15625
- w_mamba_in: bfloat16 [1600, 6400], P('fsdp'), may hold values from -0.15625 to 0.15625
- conv_weight: float32 [4, 3200], replicated, may hold values from -3 to 3
- conv_bias: float32 [3200], replicated, may hold values from -3 to 3
- x_proj: float32 [3200, 132], replicated, may hold values from -0.109375 to 0.109375
- dt_proj: float32 [100, 3200], replicated, may hold values from -0.625 to 0.625
- dt_bias: float32 [3200], replicated, may hold values from -5 to -1
- a_log: float32 [16, 3200], replicated, may hold values from 0 to 2.8
- d_skip: float32 [3200], replicated, may hold values from 0.5 to 1.5
- w_mamba_out: bfloat16 [3200, 1600], P('fsdp'), may hold values from -0.109375 to 0.109375
- norm_attn: float32 [1600], replicated, may hold values from 0.5 to 1.5
- norm_ssm: float32 [1600], replicated, may hold values from 0.5 to 1.5
- w_mix_out: bfloat16 [1600, 1600], P('fsdp'), may hold values from -0.15625 to 0.15625
- norm_ffn: float32 [1600], replicated, may hold values from 0.5 to 1.5
- w_gate: bfloat16 [1600, 5504], P('fsdp'), may hold values from -0.15625 to 0.15625
- w_up: bfloat16 [1600, 5504], P('fsdp'), may hold values from -0.15625 to 0.15625
- w_down: bfloat16 [5504, 1600], P('fsdp'), may hold values from -0.078125 to 0.078125
Outputs:
- mixed_out: bfloat16 [4096, 1600], P(('rep', 'fsdp'))
- grad_tokens: bfloat16 [4096, 1600], P(('rep', 'fsdp'))
- grad_norm_in: float32 [1600], replicated
- grad_w_qkv: float32 [1600, 2240], P('fsdp')
- grad_w_mamba_in: float32 [1600, 6400], P('fsdp')
- grad_conv_weight: float32 [4, 3200], replicated
- grad_conv_bias: float32 [3200], replicated
- grad_x_proj: float32 [3200, 132], replicated
- grad_dt_proj: float32 [100, 3200], replicated
- grad_dt_bias: float32 [3200], replicated
- grad_a_log: float32 [16, 3200], replicated
- grad_d_skip: float32 [3200], replicated
- grad_w_mamba_out: float32 [3200, 1600], P('fsdp')
- grad_norm_attn: float32 [1600], replicated
- grad_norm_ssm: float32 [1600], replicated
- grad_w_mix_out: float32 [1600, 1600], P('fsdp')
- grad_norm_ffn: float32 [1600], replicated
- grad_w_gate: float32 [1600, 5504], P('fsdp')
- grad_w_up: float32 [1600, 5504], P('fsdp')
- grad_w_down: float32 [5504, 1600], P('fsdp')
Inputs may be any that keep to these rules, and one draw needn't show every extreme that they name: Each device's 3 lengths sum to 128, and the longest is exactly 96. `source_slot`: each row is a permutation of 0 to 127.
All inputs are finite; a program needn't handle non-finite values.
Results may differ from a plain program's by a relative error of at most 0.018.
Values may be sent and summed in bfloat16 or wider, within the bound.
A program may use at most 448 MiB of HBM per device.

v0:
```python
import jax
import jax.numpy as jnp
from jax import lax
from jax.sharding import PartitionSpec as P

HEADS = 25
KV_HEADS = 5
HEAD_DIM = 64
INNER = 3200
STATE = 16
DT_RANK = 100
CONV = 4
WINDOW = 1024
SPAN = 8


epsilon = 1e-06
highest_precision = lax.Precision.HIGHEST


def matmul_high(left, right):
    return jnp.dot(left, right, precision=highest_precision, preferred_element_type=jnp.float32)


def rms_norm(value_rows, gain):
    return (
        value_rows
        * lax.rsqrt(jnp.mean(value_rows * value_rows, axis=-1, keepdims=True) + epsilon)
        * gain
    )


def mix_branches(attended_values, ssm_out, norm_attn, norm_ssm):
    return (rms_norm(attended_values, norm_attn) + rms_norm(ssm_out, norm_ssm)) * 0.5


def swiglu(gate_val, up_val):
    return jax.nn.silu(gate_val) * up_val


def segment_info(length_row, count):
    ends = jnp.cumsum(length_row, dtype=jnp.int32)
    positions = jnp.arange(count, dtype=jnp.int32)
    seg_ids = jnp.sum((positions[:, None] >= ends[None, :-1]).astype(jnp.int32), axis=1)
    starts = ends - length_row
    first_flag = jnp.any(positions[:, None] == starts[None, :], axis=1).astype(jnp.float32)
    distance = positions[:, None] - positions[None, :]
    allowed = (seg_ids[:, None] == seg_ids[None, :]) & (distance >= 0) & (distance < WINDOW)
    return (seg_ids, first_flag, allowed)


def span_scan(inner_act, step_size, input_mix, output_mix, decay_rate, first_flag):
    count, channels = inner_act.shape
    blocks = count // SPAN

    def block_step(carry_state, block_data):
        act_b, step_b, input_b, output_b, flag_b = block_data
        outputs = []
        for row in range(SPAN):
            carry_state = (
                jnp.exp(step_b[row][None, :] * decay_rate) * carry_state * (1.0 - flag_b[row])
                + input_b[row][:, None] * (step_b[row] * act_b[row])[None, :]
            )
            outputs.append(jnp.sum(carry_state * output_b[row][:, None], axis=0))
        return (carry_state, jnp.stack(outputs, axis=0))

    checked = jax.checkpoint(block_step)
    block_data = tuple(
        (
            jnp.reshape(item_arr, (blocks, SPAN) + item_arr.shape[1:])
            for item_arr in (inner_act, step_size, input_mix, output_mix, first_flag)
        )
    )
    zero_state = jnp.zeros((decay_rate.shape[0], channels), jnp.float32)
    unused, scanned = lax.scan(checked, zero_state, block_data)
    return scanned.reshape(count, channels)


def mamba_core(xs_in, gate_z, mamba_params, seg_ids, first_flag):
    conv_weight, conv_bias, x_proj, dt_proj, dt_bias, a_log, d_skip = mamba_params
    count = xs_in.shape[0]
    conv_sum = xs_in * conv_weight[CONV - 1] + conv_bias
    for shift_steps in range(1, CONV):
        shifted = jnp.concatenate(
            [jnp.zeros((shift_steps, xs_in.shape[1]), jnp.float32), xs_in[: count - shift_steps]],
            axis=0,
        )
        earlier = jnp.concatenate(
            [jnp.full((shift_steps,), -1, jnp.int32), seg_ids[: count - shift_steps]], axis=0
        )
        same_seq = (earlier == seg_ids)[:, None]
        conv_sum = (
            conv_sum + jnp.where(same_seq, shifted, 0.0) * conv_weight[CONV - 1 - shift_steps]
        )
    inner_act = jax.nn.silu(conv_sum)
    projected = matmul_high(inner_act, x_proj)
    step_size = jax.nn.softplus(matmul_high(projected[:, :DT_RANK], dt_proj) + dt_bias)
    input_mix = projected[:, DT_RANK : DT_RANK + STATE]
    output_mix = projected[:, DT_RANK + STATE :]
    decay_rate = -jnp.exp(a_log)
    scanned = span_scan(inner_act, step_size, input_mix, output_mix, decay_rate, first_flag)
    return (scanned + d_skip * inner_act) * jax.nn.silu(gate_z)


def split_heads(qkv_low):
    count = qkv_low.shape[0]
    group_size = HEADS // KV_HEADS
    query_width = HEADS * HEAD_DIM
    kv_width = KV_HEADS * HEAD_DIM
    query_rows = qkv_low[:, :query_width].reshape(count, KV_HEADS, group_size, HEAD_DIM)
    key_rows = qkv_low[:, query_width : query_width + kv_width].reshape(count, KV_HEADS, HEAD_DIM)
    value_rows = qkv_low[:, query_width + kv_width :].reshape(count, KV_HEADS, HEAD_DIM)
    return (query_rows, key_rows, value_rows)


def masked_scores(query_rows, key_rows, allowed):
    attention_scores = jnp.einsum(
        "jzhx,kzx->zhjk", query_rows, key_rows, preferred_element_type=jnp.float32
    ) * HEAD_DIM ** (-0.5)
    return jnp.where(allowed[None, None], attention_scores, -1e30)


def attention_forward(qkv_low, allowed):
    count = qkv_low.shape[0]
    query_rows, key_rows, value_rows = split_heads(qkv_low)
    attention_scores = masked_scores(query_rows, key_rows, allowed)
    row_max = jnp.max(attention_scores, axis=-1, keepdims=True)
    weights_exp = jnp.exp(attention_scores - row_max)
    row_total = jnp.sum(weights_exp, axis=-1, keepdims=True)
    lowered_probabilities = (weights_exp / row_total).astype(jnp.bfloat16)
    attended_values = jnp.einsum(
        "lpho,ole->hlpe", lowered_probabilities, value_rows, preferred_element_type=jnp.float32
    )
    return (attended_values.reshape(count, HEADS * HEAD_DIM), row_max + jnp.log(row_total))


def attention_backward(qkv_low, grad_low, log_total, allowed):
    count = qkv_low.shape[0]
    query_rows, key_rows, value_rows = split_heads(qkv_low)
    probabilities = jnp.exp(masked_scores(query_rows, key_rows, allowed) - log_total)
    head_gradient = grad_low.reshape(count, KV_HEADS, HEADS // KV_HEADS, HEAD_DIM)
    grad_probs = jnp.einsum(
        "jzhx,kzx->zhjk", head_gradient, value_rows, preferred_element_type=jnp.float32
    )
    score_gradient = (
        probabilities * (grad_probs - jnp.sum(grad_probs * probabilities, axis=-1, keepdims=True))
    ).astype(jnp.bfloat16)
    scale_factor_scores = HEAD_DIM ** (-0.5)
    grad_queries = (
        jnp.einsum("lpho,ole->hlpe", score_gradient, key_rows, preferred_element_type=jnp.float32)
        * scale_factor_scores
    )
    grad_keys = (
        jnp.einsum("wniv,iwne->vwe", score_gradient, query_rows, preferred_element_type=jnp.float32)
        * scale_factor_scores
    )
    grad_values = jnp.einsum(
        "wniv,iwne->vwe",
        probabilities.astype(jnp.bfloat16),
        head_gradient,
        preferred_element_type=jnp.float32,
    )
    return jnp.concatenate(
        [
            grad_queries.reshape(count, -1),
            grad_keys.reshape(count, -1),
            grad_values.reshape(count, -1),
        ],
        axis=1,
    )


def owned_grad(left_low, right_low, own_rows):
    own_start = lax.axis_index("fsdp") * own_rows
    zero_total = jnp.zeros((own_rows, right_low.shape[1]), jnp.float32)
    column_part = lax.dynamic_slice_in_dim(
        lax.all_gather(left_low, "fsdp", axis=0, tiled=True), own_start, own_rows, 1
    )
    return zero_total + jnp.einsum(
        "tf,tc->fc",
        column_part,
        lax.all_gather(right_low, "fsdp", axis=0, tiled=True),
        preferred_element_type=jnp.float32,
    )


def per_device(
    tokens,
    cotangent,
    lengths,
    source_slot,
    norm_in,
    w_qkv,
    w_mamba_in,
    conv_weight,
    conv_bias,
    x_proj,
    dt_proj,
    dt_bias,
    a_log,
    d_skip,
    w_mamba_out,
    norm_attn,
    norm_ssm,
    w_mix_out,
    norm_ffn,
    w_gate,
    w_up,
    w_down,
):
    arrived, cot_arrived = (
        lax.all_to_all(tokens, "fsdp", split_axis=0, concat_axis=0, tiled=True),
        lax.all_to_all(cotangent, "fsdp", split_axis=0, concat_axis=0, tiled=True),
    )
    slot_order = source_slot[0]
    hidden_in = jnp.take(arrived, slot_order, axis=0).astype(jnp.float32)
    cot_rows = jnp.take(cot_arrived, slot_order, axis=0).astype(jnp.float32)
    seg_ids, first_flag, allowed = segment_info(lengths[0], hidden_in.shape[0])
    full_qkv, full_min, full_mout, full_mix, full_gate, full_up, full_down = (
        lax.all_gather(w_qkv, "fsdp", axis=0, tiled=True),
        lax.all_gather(w_mamba_in, "fsdp", axis=0, tiled=True),
        lax.all_gather(w_mamba_out, "fsdp", axis=0, tiled=True),
        lax.all_gather(w_mix_out, "fsdp", axis=0, tiled=True),
        lax.all_gather(w_gate, "fsdp", axis=0, tiled=True),
        lax.all_gather(w_up, "fsdp", axis=0, tiled=True),
        lax.all_gather(w_down, "fsdp", axis=0, tiled=True),
    )
    normed, norm_in_pull = jax.vjp(rms_norm, hidden_in, norm_in)
    normed_low = normed.astype(jnp.bfloat16)
    qkv_low = jnp.dot(normed_low, full_qkv, preferred_element_type=jnp.float32).astype(jnp.bfloat16)
    attended_values, log_total = attention_forward(qkv_low, allowed)
    mamba_pair = jnp.dot(normed_low, full_min, preferred_element_type=jnp.float32)

    def mamba_local(xs_in, gate_z, mamba_params):
        return mamba_core(xs_in, gate_z, mamba_params, seg_ids, first_flag)

    mamba_params = (conv_weight, conv_bias, x_proj, dt_proj, dt_bias, a_log, d_skip)
    mixer_out, mamba_pull = jax.vjp(
        mamba_local, mamba_pair[:, :INNER], mamba_pair[:, INNER:], mamba_params
    )
    mixer_low = mixer_out.astype(jnp.bfloat16)
    ssm_out = jnp.dot(mixer_low, full_mout, preferred_element_type=jnp.float32)
    mixed, mix_pull = jax.vjp(mix_branches, attended_values, ssm_out, norm_attn, norm_ssm)
    mixed_low = mixed.astype(jnp.bfloat16)
    middle = hidden_in + jnp.dot(mixed_low, full_mix, preferred_element_type=jnp.float32)
    ffn_in, ffn_pull = jax.vjp(rms_norm, middle, norm_ffn)
    ffn_low = ffn_in.astype(jnp.bfloat16)
    gate_val = jnp.dot(ffn_low, full_gate, preferred_element_type=jnp.float32)
    up_val = jnp.dot(ffn_low, full_up, preferred_element_type=jnp.float32)
    hidden_ffn, swiglu_pull = jax.vjp(swiglu, gate_val, up_val)
    hidden_low = hidden_ffn.astype(jnp.bfloat16)
    result = middle + jnp.dot(hidden_low, full_down, preferred_element_type=jnp.float32)
    cot_low = cot_rows.astype(jnp.bfloat16)
    grad_down = owned_grad(hidden_low, cot_low, w_down.shape[0])
    grad_hidden = jnp.einsum("td,fd->tf", cot_low, full_down, preferred_element_type=jnp.float32)
    grad_gate_val, grad_up_val = swiglu_pull(grad_hidden)
    gate_up_low = jnp.concatenate([grad_gate_val, grad_up_val], axis=1).astype(jnp.bfloat16)
    grad_gate_up = owned_grad(ffn_low, gate_up_low, w_gate.shape[0])
    ff_width = w_gate.shape[1]
    grad_ffn_in = jnp.einsum(
        "tf,df->td", gate_up_low[:, :ff_width], full_gate, preferred_element_type=jnp.float32
    ) + jnp.einsum(
        "tf,df->td", gate_up_low[:, ff_width:], full_up, preferred_element_type=jnp.float32
    )
    grad_middle_norm, grad_norm_ffn = ffn_pull(grad_ffn_in)
    grad_middle = cot_rows + grad_middle_norm
    middle_low = grad_middle.astype(jnp.bfloat16)
    grad_mix_weight = owned_grad(mixed_low, middle_low, w_mix_out.shape[0])
    grad_mixed = jnp.einsum("td,ed->te", middle_low, full_mix, preferred_element_type=jnp.float32)
    grad_attended, grad_ssm, grad_norm_attn, grad_norm_ssm = mix_pull(grad_mixed)
    ssm_low = grad_ssm.astype(jnp.bfloat16)
    grad_mout = owned_grad(mixer_low, ssm_low, w_mamba_out.shape[0])
    grad_mixer = jnp.einsum("td,id->ti", ssm_low, full_mout, preferred_element_type=jnp.float32)
    grad_xs, grad_gate_z, grad_mamba_params = mamba_pull(grad_mixer)
    (
        grad_conv_weight,
        grad_conv_bias,
        grad_x_proj,
        grad_dt_proj,
        grad_dt_bias,
        grad_a_log,
        grad_d_skip,
    ) = grad_mamba_params
    pair_low = jnp.concatenate([grad_xs, grad_gate_z], axis=1).astype(jnp.bfloat16)
    qkv_grad_low = attention_backward(
        qkv_low, grad_attended.astype(jnp.bfloat16), log_total, allowed
    ).astype(jnp.bfloat16)
    input_low = jnp.concatenate([qkv_grad_low, pair_low], axis=1)
    grad_inputs = owned_grad(normed_low, input_low, w_qkv.shape[0])
    grad_normed = jnp.einsum(
        "tc,dc->td", qkv_grad_low, full_qkv, preferred_element_type=jnp.float32
    ) + jnp.einsum("tc,dc->td", pair_low, full_min, preferred_element_type=jnp.float32)
    grad_hidden_norm, grad_norm_in = norm_in_pull(grad_normed)
    grad_hidden_in = grad_middle + grad_hidden_norm
    sum_inputs, sum_mout, sum_mix, sum_gate_up, sum_down = (
        lax.psum(grad_inputs.astype(jnp.bfloat16), "rep").astype(jnp.float32),
        lax.psum(grad_mout.astype(jnp.bfloat16), "rep").astype(jnp.float32),
        lax.psum(grad_mix_weight.astype(jnp.bfloat16), "rep").astype(jnp.float32),
        lax.psum(grad_gate_up.astype(jnp.bfloat16), "rep").astype(jnp.float32),
        lax.psum(grad_down.astype(jnp.bfloat16), "rep").astype(jnp.float32),
    )
    (
        sum_norm_in,
        sum_norm_attn,
        sum_norm_ssm,
        sum_norm_ffn,
        sum_conv_weight,
        sum_conv_bias,
        sum_x_proj,
        sum_dt_proj,
        sum_dt_bias,
        sum_a_log,
        sum_d_skip,
    ) = lax.psum(
        (
            grad_norm_in,
            grad_norm_attn,
            grad_norm_ssm,
            grad_norm_ffn,
            grad_conv_weight,
            grad_conv_bias,
            grad_x_proj,
            grad_dt_proj,
            grad_dt_bias,
            grad_a_log,
            grad_d_skip,
        ),
        ("rep", "fsdp"),
    )
    out_buffer = jnp.zeros_like(arrived).at[slot_order].set(result.astype(jnp.bfloat16))
    grad_buffer = jnp.zeros_like(arrived).at[slot_order].set(grad_hidden_in.astype(jnp.bfloat16))
    mixed_out, grad_tokens = (
        lax.all_to_all(out_buffer, "fsdp", split_axis=0, concat_axis=0, tiled=True),
        lax.all_to_all(grad_buffer, "fsdp", split_axis=0, concat_axis=0, tiled=True),
    )
    qkv_width = w_qkv.shape[1]
    return (
        mixed_out,
        grad_tokens,
        sum_norm_in,
        sum_inputs[:, :qkv_width],
        sum_inputs[:, qkv_width:],
        sum_conv_weight,
        sum_conv_bias,
        sum_x_proj,
        sum_dt_proj,
        sum_dt_bias,
        sum_a_log,
        sum_d_skip,
        sum_mout,
        sum_norm_attn,
        sum_norm_ssm,
        sum_mix,
        sum_norm_ffn,
        sum_gate_up[:, :ff_width],
        sum_gate_up[:, ff_width:],
        sum_down,
    )


def solution(mesh):
    placed = (
        P(("rep", "fsdp"), None),
        P(("rep", "fsdp"), None),
        P(("rep", "fsdp"), None),
        P(("rep", "fsdp"), None),
        P(),
        P("fsdp", None),
        P("fsdp", None),
        P(),
        P(),
        P(),
        P(),
        P(),
        P(),
        P(),
        P("fsdp", None),
        P(),
        P(),
        P("fsdp", None),
        P(),
        P("fsdp", None),
        P("fsdp", None),
        P("fsdp", None),
    )
    return jax.shard_map(
        per_device,
        mesh=mesh,
        in_specs=placed,
        out_specs=(
            P(("rep", "fsdp"), None),
            P(("rep", "fsdp"), None),
            P(),
            P("fsdp", None),
            P("fsdp", None),
            P(),
            P(),
            P(),
            P(),
            P(),
            P(),
            P(),
            P("fsdp", None),
            P(),
            P(),
            P("fsdp", None),
            P(),
            P("fsdp", None),
            P("fsdp", None),
            P("fsdp", None),
        ),
        check_vma=False,
    )
```

profile of v0, /device:TPU:0, one launch (start us, length us, event | category | flops | bytes accessed | tf_op | source)
XLA Modules:
  0.0 3150.7 jit_solution(12248176181959829494)
XLA Ops:
  22.4 17.3 all-to-all-done
  39.7 8.2 all-to-all-start.2
  52.4 20.1 all-to-all-done.2
  76.7 82.8 %all-gather.19.cloned.1.call-done = bf16[1600,2240]{1,0:T(8,128)(2,1)} async-done(((bf16[400,2240]{1,0:T(8,128)(2,1)}), bf16[1600,2240]{1,0:T(8,128)(2,1)}) %all-gather.19.cloned.1.call-update) | async-done | bytes 7168016 | tf_op jit(solution)/shard_map/all_gather | solution.py:220
  167.9 301.2 %all-gather.51.cloned.1.call-done = bf16[4,1376,1600]{1,2,0:T(8,128)(2,1)} async-done(((bf16[1,1376,1600]{1,2,0:T(8,128)(2,1)}), bf16[4,1376,1600]{1,2,0:T(8,128)(2,1)}) %all-gather.51.cloned.1.call-update) | async-done | bytes 17612816 | tf_op jit(solution)/shard_map/all_gather | solution.py:226
  469.0 24.6 copy.108
  493.6 324.8 %all-gather.21.cloned.1.call-done = bf16[1600,6400]{1,0:T(8,128)(2,1)} async-done(((bf16[400,6400]{1,0:T(8,128)(2,1)}), bf16[1600,6400]{1,0:T(8,128)(2,1)}) %all-gather.21.cloned.1.call-update) | async-done | bytes 20480016 | tf_op jit(solution)/shard_map/all_gather | solution.py:221
  818.4 8.8 fusion.103
  842.6 201.6 %while.40 = (s32[]{:T(128)}, f32[16,3200]{1,0:T(8,128)S(1)}, f32[16,8,3200]{2,1,0:T(8,128)}, f32[16,16,3200]{2,1,0:T(8,128)}, f32[16,8,3200]{2,1,0:T(8,128)}, /*...) while((s32[]{:T(128)}, f32[16,3200]{1,0:T(8,128)S(1)}, ...), condition=%wide.region_16.18_spmd.clone, body=%wide.region_7.17_spmd.clone.sunk | while | flops 4044818 | bytes 5023581 | solution.py:75
  1048.5 8.6 multiply_reduce_fusion.59
  1059.5 44.6 %all-gather.25.cloned.1.call-done = bf16[1600,1600]{1,0:T(8,128)(2,1)} async-done(((bf16[400,1600]{1,0:T(8,128)(2,1)}), bf16[1600,1600]{1,0:T(8,128)(2,1)}) %all-gather.25.cloned.1.call-update) | async-done | bytes 5120016 | tf_op jit(solution)/shard_map/all_gather | solution.py:223
  1110.1 295.9 %all-gather.29.cloned.1.call-done = bf16[1600,5504]{1,0:T(8,128)(2,1)} async-done(((bf16[400,5504]{1,0:T(8,128)(2,1)}), bf16[1600,5504]{1,0:T(8,128)(2,1)}) %all-gather.29.cloned.1.call-update) | async-done | bytes 17612816 | tf_op jit(solution)/shard_map/all_gather | solution.py:225
  1406.0 10.6 fusion.105
  1416.6 292.1 %all-gather.27.cloned.1.call-done = bf16[1600,5504]{1,0:T(8,128)(2,1)} async-done(((bf16[400,5504]{1,0:T(8,128)(2,1)}), bf16[1600,5504]{1,0:T(8,128)(2,1)}) %all-gather.27.cloned.1.call-update) | async-done | bytes 17612816 | tf_op jit(solution)/shard_map/all_gather | solution.py:224
  1708.6 10.6 fusion.104
  1719.2 11.7 multiply_convert_fusion
  1730.9 9.5 fusion.106
  1740.4 10.8 multiply_reduce_fusion.53
  1770.3 7.5 fusion.107
  1783.4 322.4 %while.41 = (s32[]{:T(128)}, f32[16,3200]{1,0:T(8,128)}, f32[16,3200]{1,0:T(8,128)}, f32[16,8,3200]{2,1,0:T(8,128)}, f32[16,8,3200]{2,1,0:T(8,128)}, /*index=5*/...) while((s32[]{:T(128)}, f32[16,3200]{1,0:T(8,128)}, ...), condition=%wide.region_57.59_spmd.clone, body=%wide.region_24.58_spmd.clone.sunk | while | flops 17742348 | bytes 14277292 | solution.py:75
  2131.6 8.1 multiply_reduce_fusion.48
  2166.2 136.7 %all-gather.33.cloned.1.call-done = bf16[512,8640]{1,0:T(8,128)(2,1)} async-done(((bf16[128,8640]{1,0:T(8,128)(2,1)}), bf16[512,8640]{1,0:T(8,128)(2,1)}) %all-gather.33.cloned.1.call-update) | async-done | bytes 8847376 | tf_op jit(solution)/shard_map/all_gather | solution.py:182
  2303.0 10.4 convolution_convert_fusion.1
  2313.3 28.6 all-gather.43.cloned.1.call-done
  2342.0 197.0 %all-gather.45.cloned.1.call-done = bf16[512,11008]{1,0:T(8,128)(2,1)} async-done(((bf16[128,11008]{1,0:T(8,128)(2,1)}), bf16[512,11008]{1,0:T(8,128)(2,1)}) %all-gather.45.cloned.1.call-update) | async-done | bytes 11272208 | tf_op jit(solution)/shard_map/all_gather | solution.py:182
  2539.0 12.6 convolution_convert_fusion
  2553.0 12.5 fusion.5
  2577.7 12.7 fusion.37
  2614.8 236.2 %all-reduce.66.cloned.1.call-done = (bf16[400,8640]{1,0:T(8,128)(2,1)}, bf16[400,11008]{1,0:T(8,128)(2,1)}, bf16[800,1600]{1,0:T(8,128)(2,1)}, bf16[400,1600]{1,0:T(8,128)(2,1)}, bf16[1376,1600]{0,1:T(8,128)(2,1)}) async-done(((bf16[400,8640]{1,0:T(8,128)(2,1)}, bf16[400,11008]{1,0:T(8,128)(2,1)}, bf16[800,1600]{1,0:T(8,128)(2,1)}, bf16[400,1600]{1,0:T(8,128)(2,1)}, bf16[1376,1600]{0,1:T(8,128)(2,1)}), ...) | async-done | bytes 23961616 | tf_op jit(solution)/shard_map/psum | solution.py:296
  2871.0 11.2 fusion.99
  2882.2 100.4 %all-reduce.62.cloned.1.call-done = (f32[1600]{0:T(1024)}, f32[4,3200]{1,0:T(4,128)}, f32[3200]{0:T(1024)}, f32[3200]{0:T(1024)}, f32[3200]{0:T(1024)}, /*index=5*/f32[1600]{0:T(1024)}, f32[1600]{0:T(1024)}, f32[1600]{0:T(1024)}) async-done(((f32[1600]{0:T(1024)}, f32[4,3200]{1,0:T(4,128)}, f32[3200]{0:T(1024)}, f32[3200]{0:T(1024)}, f32[3200]{0:T(1024)}, /*index=5*/f32[1600]{0:T(1024)}, f32[1600]{0:T(1024)}, ...) | async-done | bytes 115216 | tf_op jit(solution)/shard_map/psum | solution.py:314
  2982.5 149.1 %all-reduce.64.cloned.1.call-done = (f32[3200,132]{0,1:T(8,128)}, f32[100,3200]{1,0:T(8,128)}, f32[16,3200]{1,0:T(8,128)}) async-done(((f32[3200,132]{0,1:T(8,128)}, f32[100,3200]{1,0:T(8,128)}, f32[16,3200]{1,0:T(8,128)}), (f32[3200,132]{0,1:T(8,128)}, f32[100,3200]{1,0:T(8,128)}, f32[16,3200]{1,0:T(8,128)})) %all-reduce.64.cloned.1.call-update) | async-done | bytes 3174416 | tf_op jit(solution)/shard_map/psum | solution.py:314
  (1493 shorter events, 560.1 us)
Async XLA Ops:
  7.2 825.7 %copy-start = (f32[3200,132]{0,1:T(8,128)S(1)}, f32[3200,132]{0,1:T(8,128)}, u32[]{:S(2)}) copy-start(f32[3200,132]{0,1:T(8,128)} %param.37) | copy-start | bytes 5068804
  7.2 152.3 %all-gather.19.cloned.1.call-start = ((), (), s32[]{:S(2)}) async-start(), calls=%async_computation.4 | async-start | bytes 9216000 | tf_op jit(solution)/shard_map/all_gather | solution.py:220
  7.9 461.1 %all-gather.51.cloned.1.call-start = ((), (), s32[]{:S(2)}) async-start(), calls=%async_computation.20 | async-start | bytes 22528000 | tf_op jit(solution)/shard_map/all_gather | solution.py:226
  8.7 809.7 %all-gather.21.cloned.1.call-start = ((), (), s32[]{:S(2)}) async-start(), calls=%async_computation.5 | async-start | bytes 25600000 | tf_op jit(solution)/shard_map/all_gather | solution.py:221
  9.4 1039.0 %all-gather.23.cloned.1.call-start = ((), (), s32[]{:S(2)}) async-start(), calls=%async_computation.6 | async-start | bytes 13312000 | tf_op jit(solution)/shard_map/all_gather | solution.py:222
  10.0 1094.2 %all-gather.25.cloned.1.call-start = ((), (), s32[]{:S(2)}) async-start(), calls=%async_computation.7 | async-start | bytes 6656000 | tf_op jit(solution)/shard_map/all_gather | solution.py:223
  10.6 1395.4 %all-gather.29.cloned.1.call-start = ((), (), s32[]{:S(2)}) async-start(), calls=%async_computation.9 | async-start | bytes 22016000 | tf_op jit(solution)/shard_map/all_gather | solution.py:225
  12.6 27.1 all-to-all-start
  18.9 1689.7 %all-gather.27.cloned.1.call-start = ((), (), s32[]{:S(2)}) async-start(), calls=%async_computation.8 | async-start | bytes 22016000 | tf_op jit(solution)/shard_map/all_gather | solution.py:224
  19.9 56.5 %copy-start.80 = (pred[128]{0:T(512)(128)(4,1)}, pred[128]{0:T(512)(128)(4,1)S(1)}, u32[]{:S(2)}) copy-start(pred[128]{0:T(512)(128)(4,1)S(1)} %compare_and_fusion) | copy-start | bytes 388
  20.8 806.8 %copy-start.62 = (f32[3200]{0:T(1024)}, f32[3200]{0:T(1024)S(1)}, u32[]{:S(2)}) copy-start(f32[3200]{0:T(1024)S(1)} %get-tuple-element.685) | copy-start | bytes 38404
  22.4 805.3 %copy-start.94 = (pred[128]{0:T(512)(128)(4,1)}, pred[128]{0:T(512)(128)(4,1)S(1)}, u32[]{:S(2)}) copy-start(pred[128]{0:T(512)(128)(4,1)S(1)} %get-tuple-element.861) | copy-start | bytes 388
  22.4 805.3 %copy-start.97 = (pred[128]{0:T(512)(128)(4,1)}, pred[128]{0:T(512)(128)(4,1)S(1)}, u32[]{:S(2)}) copy-start(pred[128]{0:T(512)(128)(4,1)S(1)} %get-tuple-element.862) | copy-start | bytes 388
  39.7 32.9 %all-to-all-start.2 = ((bf16[4,32,1600]{2,1,0:T(8,128)(2,1)}), bf16[4,32,1600]{2,1,0:T(8,128)(2,1)S(1)}, u32[]{:S(2)}, u32[]{:S(2)}) async-start(bf16[4,32,1600]{2,1,0:T(8,128)(2,1)} %bitcast.28), calls=%async_computation.2 | async-start | bytes 851968 | tf_op jit(solution)/shard_map/all_to_all | solution.py:213
  47.8 2102.1 %all-gather.39.cloned.1.call-start = ((), (), s32[]{:S(2)}) async-start(), calls=%async_computation.14 | async-start | bytes 2048000 | tf_op jit(solution)/shard_map/all_gather | solution.py:177
  76.7 741.7 %copy-start.36 = (bf16[128,1600]{0,1:T(8,128)(2,1)}, bf16[128,1600]{0,1:T(8,128)(2,1)S(1)}, u32[]{:S(2)}) copy-start(bf16[128,1600]{0,1:T(8,128)(2,1)S(1)} %fusion.36) | copy-start | bytes 1228804
  842.6 201.6 %copy-start.70 = (f32[3200]{0:T(1024)S(1)}, f32[3200]{0:T(1024)}, u32[]{:S(2)}) copy-start(f32[3200]{0:T(1024)} %param.41) | copy-start | bytes 38404
  1059.5 1090.5 %all-gather.41.cloned.1.call-start = ((), (), s32[]{:S(2)}) async-start(), calls=%async_computation.15 | async-start | bytes 2048000 | tf_op jit(solution)/shard_map/all_gather | solution.py:182
  1109.0 642.2 %copy-start.92 = (f32[128]{0:T(128)}, f32[128]{0:T(128)S(1)}, u32[]{:S(2)}) copy-start(f32[128]{0:T(128)S(1)} %fusion.84) | copy-start | bytes 1540
  1753.2 400.5 %all-gather.37.cloned.1.call-start = ((), (), s32[]{:S(2)}) async-start(), calls=%async_computation.13 | async-start | bytes 2048000 | tf_op jit(solution)/shard_map/all_gather | solution.py:182
  1760.7 393.0 %all-gather.35.cloned.1.call-start = ((), (), s32[]{:S(2)}) async-start(), calls=%async_computation.12 | async-start | bytes 4096000 | tf_op jit(solution)/shard_map/all_gather | solution.py:177
  1761.5 397.9 %all-gather.49.cloned.1.call-start = ((), (), s32[]{:S(2)}) async-start(), calls=%async_computation.19 | async-start | bytes 2048000 | tf_op jit(solution)/shard_map/all_gather | solution.py:182
  1762.0 397.3 %all-gather.47.cloned.1.call-start = ((), (), s32[]{:S(2)}) async-start(), calls=%async_computation.18 | async-start | bytes 7045120 | tf_op jit(solution)/shard_map/all_gather | solution.py:177
  1762.8 403.4 %all-gather.31.cloned.1.call-start = ((), (), s32[]{:S(2)}) async-start(), calls=%async_computation.10 | async-start | bytes 2048000 | tf_op jit(solution)/shard_map/all_gather | solution.py:177
  1764.7 538.2 %all-gather.33.cloned.1.call-start = ((), (), s32[]{:S(2)}) async-start(), calls=%async_computation.11 | async-start | bytes 11141120 | tf_op jit(solution)/shard_map/all_gather | solution.py:182
  2145.2 196.8 %all-gather.43.cloned.1.call-start = ((), (), s32[]{:S(2)}) async-start(), calls=%async_computation.16 | async-start | bytes 2048000 | tf_op jit(solution)/shard_map/all_gather | solution.py:177
  2145.8 393.2 %all-gather.45.cloned.1.call-start = ((), (), s32[]{:S(2)}) async-start(), calls=%async_computation.17 | async-start | bytes 14090240 | tf_op jit(solution)/shard_map/all_gather | solution.py:182
  2149.7 701.4 %all-reduce.66.cloned.1.call-start = ((), (), s32[]{:S(2)}) async-start(), calls=%async_computation.23 | async-start | bytes 48537600 | tf_op jit(solution)/shard_map/psum | solution.py:296
  2567.8 28.8 all-to-all-start.1
  2572.0 410.6 %all-reduce.62.cloned.1.call-start = ((), (), s32[]{:S(2)}) async-start(), calls=%async_computation.21 | async-start | bytes 266240 | tf_op jit(solution)/shard_map/psum | solution.py:314
  2596.6 17.3 all-to-all-start.3
  2601.6 530.0 %all-reduce.64.cloned.1.call-start = ((), (), s32[]{:S(2)}) async-start(), calls=%async_computation.22 | async-start | bytes 6553600 | tf_op jit(solution)/shard_map/psum | solution.py:314
  (138 other events, 703.3 us)
Sparse Core Ops, SparseCore 0:
  9.6 149.8 all-gather.18
  161.1 307.8 all-gather.50
  470.6 347.7 all-gather.20
  819.8 185.2 all-gather.22
  1006.5 97.5 all-gather.24
  1105.6 300.3 all-gather.28
  1407.6 300.9 all-gather.26
  1710.7 37.7 all-gather.38
  1753.4 37.9 all-gather.40
  1792.7 36.9 all-gather.36
  1831.3 63.8 all-gather.34
  1896.7 37.3 all-gather.48
  1935.7 102.7 all-gather.46
  2039.9 37.0 all-gather.30
  2145.3 157.5 all-gather.32
  2304.9 36.9 all-gather.42
  2344.0 195.0 all-gather.44
  2551.8 299.1 all-reduce.65
  2859.2 123.3 all-reduce.61
  2989.4 142.1 all-reduce.63
where the time goes:
time: 3170 us; the launch traced here: 3150 us
  waiting for transfers between devices  2240 us (71%)
  local copies, waits for them, and re-layouts  280 us (9%)
  other arithmetic  231 us (7%)
  matrix products  192 us (6%)
  loops' own time  169 us (5%)
    all_gather x5, waiting for transfers between devices, owned_grad(): lax.all_gather(right_low, 'fsdp', axis=0, tiled=True)  334 us
    all_gather x1, waiting for transfers between devices, per_device(): lax.all_gather(w_mamba_in, 'fsdp', axis=0, tiled=True)  325 us
    all_gather x1, waiting for transfers between devices, per_device(): lax.all_gather(w_down, 'fsdp', axis=0, tiled=True)  301 us
    all_gather x1, waiting for transfers between devices, per_device(): lax.all_gather(w_up, 'fsdp', axis=0, tiled=True)  296 us
    all_gather x1, waiting for transfers between devices, per_device(): lax.all_gather(w_gate, 'fsdp', axis=0, tiled=True)  292 us
    psum x2, waiting for transfers between devices, per_device(): lax.psum((grad_norm_in, grad_norm_attn, grad_norm_ssm, grad_norm_ffn, gra...  249 us
    psum x1, waiting for transfers between devices, per_device(): lax.psum(grad_inputs.astype(jnp.bfloat16), 'rep').astype(jnp.float32)  236 us
    another operation x2, loops' own time, span_scan(): unused, scanned = lax.scan(checked, zero_state, block_data)  169 us
  transfers between devices with their start and end apart: 24, of which 15 were waited for; matrix products, arithmetic and copies ran while one was open for 21% of the time, Pallas kernels for 0%

commit v1 on v0

v1 whole, which is shorter than its diff:
```python
import functools

import jax
import jax.numpy as jnp
from jax import lax
from jax.experimental import pallas as pl
from jax.experimental.pallas import tpu as pltpu
from jax.sharding import PartitionSpec as P

HEADS = 25
KV_HEADS = 5
HEAD_DIM = 64
INNER = 3200
STATE = 16
DT_RANK = 100
CONV = 4
WINDOW = 1024
LANES = 128
PACKS = 8
LOG2_E = 1.4426950408889634

epsilon = 1e-06
bf16 = jnp.bfloat16
f32 = jnp.float32


def dot(left, right, precision=None):
    return jnp.dot(left, right, precision=precision, preferred_element_type=f32)


def dot_right_t(left, right):
    return lax.dot_general(left, right, (((1,), (1,)), ((), ())), preferred_element_type=f32)


def dot_left_t(left, right):
    return lax.dot_general(left, right, (((0,), (0,)), ((), ())), preferred_element_type=f32)


def rms_norm(value_rows, gain):
    return (
        value_rows
        * lax.rsqrt(jnp.mean(value_rows * value_rows, axis=-1, keepdims=True) + epsilon)
        * gain
    )


def mix_branches(attended_values, ssm_out, norm_attn, norm_ssm):
    return (rms_norm(attended_values, norm_attn) + rms_norm(ssm_out, norm_ssm)) * 0.5


def swiglu(gate_val, up_val):
    return jax.nn.silu(gate_val) * up_val


def hbm_spec():
    return pl.BlockSpec(memory_space=pl.ANY)


def vmem_spec():
    return pl.BlockSpec(memory_space=pltpu.VMEM)


SMALL_COST = pl.CostEstimate(flops=0, bytes_accessed=10**4, transcendentals=0)


def send(src, dst, sems, axis, target):
    copy = pltpu.make_async_remote_copy(
        src_ref=src,
        dst_ref=dst,
        send_sem=sems[0],
        recv_sem=sems[1],
        device_id={axis: target},
        device_id_type=pl.DeviceIdType.MESH,
    )
    copy.start()
    return copy


def meet(axis, others):
    barrier = pltpu.get_barrier_semaphore()
    for other in others:
        pl.semaphore_signal(
            barrier, inc=1, device_id={axis: other}, device_id_type=pl.DeviceIdType.MESH
        )
    pl.semaphore_wait(barrier, len(others))


def rep_kernel(rep, counts, square, *refs):
    n_gather, n_sum, n_all, n_trade = counts
    chips = rep // 2
    refs = list(refs)

    def take(n):
        taken = refs[:n]
        del refs[:n]
        return taken

    gathers, sums, alls, trades = (take(n) for n in counts)
    gathered, summed, all_summed, traded = (take(n) for n in counts)
    reduced = sums + alls
    buffers = [take(3) for _ in reduced]
    totals = summed + take(n_all)
    local, far, near, direct = refs

    me = lax.axis_index("rep")
    core = lax.rem(me, 2)
    chip = (me - core) // 2
    partner = 2 * chip + 1 - core
    ahead = [lax.rem(chip + k, chips) for k in range(chips)]
    behind = [lax.rem(chip + chips - k, chips) for k in range(chips)]
    if square:
        along_x, along_y = chip + 1 - 2 * lax.rem(chip, 2), lax.rem(chip + 2, 4)
        first = along_x + core * (along_y - along_x)
        second = along_y + core * (along_x - along_y)
        across = 3 - chip
        linked = [2 * first + core, 2 * second + core]
    else:
        linked = [2 * ahead[k] + core for k in range(1, chips)]
    if n_trade:
        meet("rep", [lax.rem(me + k, rep) for k in range(1, rep)])
    else:
        meet("rep", linked + [partner])

    kept, sent = [], []

    def keep(src, dst):
        copy = pltpu.make_async_copy(src, dst, local.at[len(kept)])
        copy.start()
        kept.append(copy)

    def far_send(src, dst, slot, k, target):
        copy = send(src, dst, (far.at[0, slot, k], far.at[1, slot, k]), "rep", 2 * target + core)
        sent.append(copy)
        return copy

    def near_send(src, dst, slot, k):
        copy = send(src, dst, (near.at[0, slot, k], near.at[1, slot, k]), "rep", partner)
        sent.append(copy)
        return copy

    def start_gather(source, out, slot):
        if square:
            far_copies = [
                far_send(source, out.at[me], slot, 1, first),
                far_send(source, out.at[me], slot, 2, second),
            ]
        else:
            far_copies = [
                far_send(source, out.at[me], slot, k, ahead[k]) for k in range(1, chips)
            ]
        near_copies = [near_send(source, out.at[me], slot, 0)]
        keep(source, out.at[me])
        return out, slot, far_copies, near_copies

    def pass_on(states):
        if square:
            for out, slot, far_copies, near_copies in states:
                block = out.at[2 * first + core]
                far_copies[0].wait_recv()
                far_copies.append(far_send(block, block, slot, 3, second))
                near_copies.append(near_send(block, block, slot, 1))
            for out, slot, far_copies, near_copies in states:
                for k, source in ((2, second), (3, across)):
                    block = out.at[2 * source + core]
                    far_copies[k - 1].wait_recv()
                    near_copies.append(near_send(block, block, slot, k))
        else:
            for out, slot, far_copies, near_copies in states:
                for k in range(1, chips):
                    block = out.at[2 * behind[k] + core]
                    far_copies[k - 1].wait_recv()
                    near_copies.append(near_send(block, block, slot, k))
        for _, _, _, near_copies in states:
            for copy in near_copies:
                copy.wait_recv()

    dests = [chip, first, across, second] if square else ahead
    partner_dests = [chip, second, across, first] if square else ahead
    order = [1, 2, 3, 0] if square else [*range(1, chips), 0]
    crossing = []
    for i, source in enumerate(reduced):
        from_partner = buffers[i][1]
        crossing.append(
            {
                k: near_send(source.at[2 * partner_dests[k] + 1 - core], from_partner.at[k], i, k)
                for k in order
            }
        )
    states = [
        start_gather(source, gathered[i], len(reduced) + n_all + i)
        for i, source in enumerate(gathers)
    ]
    trading = []
    for i, source in enumerate(trades):
        keep(source.at[me], traded[i].at[me])
        for k in range(1, rep):
            target = lax.rem(me + k, rep)
            copy = send(
                source.at[target],
                traded[i].at[me],
                (direct.at[0, i, k], direct.at[1, i, k]),
                "rep",
                target,
            )
            trading.append(copy)

    def of_chip(i, k):
        crossing[i][k].wait_recv()
        own = reduced[i][2 * dests[k] + core]
        return own.astype(f32) + buffers[i][1][k].astype(f32)

    crossed = []
    for i in range(len(reduced)):
        low, _, arrived = buffers[i]
        copies = []
        for k in (1, 2) if square else range(1, chips):
            low[k - 1] = of_chip(i, k).astype(low.dtype)
            target = first if square else ahead[k]
            copies.append(far_send(low.at[k - 1], arrived.at[k - 1], i, k, target))
        crossed.append(copies)
    if square:
        for i in range(len(reduced)):
            low, _, arrived = buffers[i]
            value = of_chip(i, 3)
            crossed[i][1].wait_recv()
            low[2] = (value + arrived[1].astype(f32)).astype(low.dtype)
            crossed[i].append(far_send(low.at[2], arrived.at[2], i, 3, second))
    for i in range(len(reduced)):
        arrived = buffers[i][2]
        total = of_chip(i, 0)
        for k in (1, 3) if square else range(1, chips):
            crossed[i][k - 1].wait_recv()
            total = total + arrived[k - 1].astype(f32)
        totals[i][...] = total
        if i >= n_sum:
            states.append(start_gather(totals[i], all_summed[i - n_sum], n_all + i))
    pass_on(states)
    for copy in trading:
        copy.wait()
    for copy in sent:
        copy.wait_send()
    for copy in kept:
        copy.wait()


def rep_exchange(rep, collective_id, gathers=(), sums=(), alls=(), trades=()):
    chips = rep // 2
    square = rep == 8 and not alls
    counts = (len(gathers), len(sums), len(alls), len(trades))
    reduced = (*sums, *alls)
    out_shape = [jax.ShapeDtypeStruct((rep,) + x.shape, x.dtype) for x in gathers]
    out_shape += [jax.ShapeDtypeStruct(x.shape[1:], f32) for x in sums]
    out_shape += [jax.ShapeDtypeStruct(x.shape, f32) for x in alls]
    out_shape += [jax.ShapeDtypeStruct(x.shape, x.dtype) for x in trades]
    scratch = []
    for x in reduced:
        scratch += [
            pltpu.VMEM((n,) + x.shape[1:], x.dtype) for n in (chips - 1, chips, chips - 1)
        ]
    scratch += [pltpu.VMEM(x.shape[1:], f32) for x in alls]
    n_local = sum(counts) - len(sums) + 1
    n_slots = len(reduced) + len(alls) + len(gathers) + 1
    scratch += [
        pltpu.SemaphoreType.DMA((n_local,)),
        pltpu.SemaphoreType.DMA((2, n_slots, chips)),
        pltpu.SemaphoreType.DMA((2, n_slots, chips)),
        pltpu.SemaphoreType.DMA((2, len(trades) + 1, rep)),
    ]
    return pl.pallas_call(
        functools.partial(rep_kernel, rep, counts, square),
        out_shape=out_shape,
        in_specs=[vmem_spec()] * sum(counts),
        out_specs=[hbm_spec()] * len(gathers)
        + [vmem_spec()] * len(sums)
        + [hbm_spec()] * (len(alls) + len(trades)),
        scratch_shapes=scratch,
        compiler_params=pltpu.CompilerParams(
            collective_id=collective_id,
            has_side_effects=True,
            vmem_limit_bytes=40 * 1024 * 1024,
        ),
        cost_estimate=SMALL_COST,
    )(*gathers, *sums, *alls, *trades)


def line_kernel(count, n_gather, n_trade, *refs):
    n_in = n_gather + n_trade
    ins, outs, (local, remote) = refs[:n_in], refs[n_in : 2 * n_in], refs[2 * n_in :]
    me = lax.axis_index("fsdp")
    others = [lax.rem(me + k, count) for k in range(1, count)]
    meet("fsdp", others)
    copies = []
    for i in range(n_in):
        own = ins[i] if i < n_gather else ins[i].at[me]
        copy = pltpu.make_async_copy(own, outs[i].at[me], local.at[i])
        copy.start()
        copies.append(copy)
        for k, other in enumerate(others):
            block = ins[i] if i < n_gather else ins[i].at[other]
            sems = (remote.at[0, i, k], remote.at[1, i, k])
            copies.append(send(block, outs[i].at[me], sems, "fsdp", other))
    for copy in copies:
        copy.wait()


def line_exchange(count, collective_id, gathers=(), trades=()):
    arrays = (*gathers, *trades)
    out_shape = [jax.ShapeDtypeStruct((count,) + x.shape, x.dtype) for x in gathers]
    out_shape += [jax.ShapeDtypeStruct(x.shape, x.dtype) for x in trades]
    return pl.pallas_call(
        functools.partial(line_kernel, count, len(gathers), len(trades)),
        out_shape=out_shape,
        in_specs=[vmem_spec()] * len(arrays),
        out_specs=[hbm_spec()] * len(arrays),
        scratch_shapes=[
            pltpu.SemaphoreType.DMA((len(arrays),)),
            pltpu.SemaphoreType.DMA((2, len(arrays), count)),
        ],
        compiler_params=pltpu.CompilerParams(collective_id=collective_id, has_side_effects=True),
        cost_estimate=SMALL_COST,
    )(*arrays)


def pair_kernel(own_ref, out_ref, local, send_sem, recv_sem):
    me = lax.axis_index("rep")
    core = lax.rem(me, 2)
    partner = me + 1 - 2 * core
    meet("rep", [partner])
    keep = pltpu.make_async_copy(own_ref, out_ref.at[:, core], local)
    keep.start()
    copy = send(own_ref, out_ref.at[:, core], (send_sem, recv_sem), "rep", partner)
    copy.wait()
    keep.wait()


def pair_gather(collective_id, own):
    groups, rows, width = own.shape
    return pl.pallas_call(
        pair_kernel,
        out_shape=jax.ShapeDtypeStruct((groups, 2, rows, width), own.dtype),
        in_specs=[vmem_spec()],
        out_specs=hbm_spec(),
        scratch_shapes=[pltpu.SemaphoreType.DMA] * 3,
        compiler_params=pltpu.CompilerParams(collective_id=collective_id, has_side_effects=True),
        cost_estimate=SMALL_COST,
    )(own)


def windows(width, pieces, start, step, rest):
    wide = min(-(-(rest + LANES - 1) // LANES) * LANES, width)
    me = lax.axis_index("rep")
    for i in range(pieces):
        at = start + i * step + me * rest
        aligned = jnp.minimum((at // LANES) * LANES, (width - wide) // LANES * LANES)
        yield pl.multiple_of(aligned, LANES), at - aligned, wide


def up16(size):
    return -(-size // 16) * 16


def copy_parts(rep, fsdp, source, out, place, start, total):
    rest = total // (rep * fsdp)
    rows = source.shape[0]
    for aligned, shift, wide in windows(source.shape[1], fsdp, start, rep * rest, rest):
        value = source[:, pl.ds(aligned, wide)].astype(f32)
        value = pltpu.roll(value, lax.rem(wide - shift, wide), 1)[:, :rest]
        if up16(rest) > rest:
            value = jnp.concatenate([value, jnp.zeros((rows, up16(rest) - rest), f32)], axis=1)
        out[:, place : place + up16(rest)] = value.astype(bf16)
        place += up16(rest)


def part_in_kernel(rep, fsdp, spots, qkv_ref, min_ref, out_ref):
    _, qkv_at, gate_at = spots
    rows, qkv_width = qkv_ref.shape
    qkv_part = qkv_width // rep
    out_ref[...] = jnp.zeros_like(out_ref)
    copy_parts(rep, fsdp, min_ref, out_ref, 0, 0, INNER)
    copy_parts(rep, fsdp, min_ref, out_ref, gate_at, INNER, INNER)
    value = qkv_ref[...].astype(f32)
    padded = -(-qkv_width // LANES) * LANES
    value = jnp.concatenate([value, jnp.zeros((rows, padded - qkv_width), f32)], axis=1)
    shift = padded - lax.axis_index("rep") * qkv_part
    value = pltpu.roll(value, lax.rem(shift, padded), 1)
    out_ref[:, qkv_at : qkv_at + qkv_part] = value[:, :qkv_part].astype(bf16)


def part_gate_up_kernel(rep, fsdp, gate_ref, up_ref, out_ref):
    copy_parts(rep, fsdp, gate_ref, out_ref, 0, 0, gate_ref.shape[1])
    copy_parts(rep, fsdp, up_ref, out_ref, out_ref.shape[1] // 2, 0, up_ref.shape[1])


def by_rows(kernel, sources, width):
    rows = sources[0].shape[0]
    block = 80 if rows % 80 == 0 else rows
    return pl.pallas_call(
        kernel,
        grid=(rows // block,),
        in_specs=[pl.BlockSpec((block, x.shape[1]), lambda i: (i, 0)) for x in sources],
        out_specs=pl.BlockSpec((block, width), lambda i: (i, 0)),
        out_shape=jax.ShapeDtypeStruct((rows, width), bf16),
        compiler_params=pltpu.CompilerParams(vmem_limit_bytes=40 * 1024 * 1024),
        cost_estimate=SMALL_COST,
    )(*sources)


def join_kernel(rep, layout, *refs):
    sources, outs = refs[: len(refs) - len(layout)], refs[len(refs) - len(layout) :]
    for out, entries in zip(outs, layout):
        for index, first, rest, place, pieces in entries:
            for i in range(pieces):
                start = first + i * up16(rest)
                for r in range(rep):
                    at = place + (i * rep + r) * rest
                    piece = sources[index][r, :, start : start + rest]
                    out[:, at : at + rest] = piece.astype(f32)


def join_rows_kernel(rep, pieces, rest, *refs):
    for source, out, rows in zip(refs[: len(rest)], refs[len(rest) :], rest):
        for i in range(pieces):
            for r in range(rep):
                at, start = (i * rep + r) * rows, i * up16(rows)
                out[at : at + rows, :] = source[r, start : start + rows, :].astype(f32)


def join_rows(rep, sources, totals, pieces=1):
    width = sources[0].shape[2]
    block = min(2 * LANES, width)
    return pl.pallas_call(
        functools.partial(join_rows_kernel, rep, pieces, tuple(n // rep // pieces for n in totals)),
        grid=(pl.cdiv(width, block),),
        in_specs=[
            pl.BlockSpec((rep, x.shape[1], block), lambda i: (0, 0, i)) for x in sources
        ],
        out_specs=[pl.BlockSpec((n, block), lambda i: (0, i)) for n in totals],
        out_shape=[jax.ShapeDtypeStruct((n, width), f32) for n in totals],
        compiler_params=pltpu.CompilerParams(vmem_limit_bytes=40 * 1024 * 1024),
        cost_estimate=SMALL_COST,
    )(*sources)


def join_columns(rep, sources, widths, layout):
    rows = sources[0].shape[1]
    block = next(n for n in (80, 40, 64, rows) if rows % n == 0)
    return pl.pallas_call(
        functools.partial(join_kernel, rep, layout),
        grid=(rows // block,),
        in_specs=[
            pl.BlockSpec((rep, block, x.shape[2]), lambda i: (0, i, 0)) for x in sources
        ],
        out_specs=[pl.BlockSpec((block, width), lambda i: (i, 0)) for width in widths],
        out_shape=[jax.ShapeDtypeStruct((rows, width), f32) for width in widths],
        compiler_params=pltpu.CompilerParams(vmem_limit_bytes=48 * 1024 * 1024),
        cost_estimate=SMALL_COST,
    )(*sources)


def spread_maps(maps_ref, wide_ref):
    count, packs, columns = maps_ref.shape

    def spread(i, _):
        for u in range(2):
            t = 2 * i + u
            maps = maps_ref[t]
            for n in range(columns):
                wide_ref[n, t] = jnp.broadcast_to(maps[:, n : n + 1], (packs, LANES))
        return 0

    lax.fori_loop(0, count // 2, spread, 0)


def scan_kernel(decay_step_ref, input_ref, maps_ref, rate_ref, out_ref, wide_ref):
    count, packs, _ = decay_step_ref.shape

    @pl.when(pl.program_id(1) == 0)
    def _():
        spread_maps(maps_ref, wide_ref)

    def step(i, states):
        for u in range(2):
            t = 2 * i + u
            decay_step, inputs = decay_step_ref[t], input_ref[t]
            out = jnp.zeros((packs, LANES), f32)
            new_states = []
            for n in range(STATE):
                decay = jnp.exp2(decay_step * rate_ref[n : n + 1, :])
                state = decay * states[n] + wide_ref[n, t] * inputs
                out = out + state * wide_ref[STATE + n, t]
                new_states.append(state)
            out_ref[t] = out
            states = tuple(new_states)
        return states

    lax.fori_loop(0, count // 2, step, (jnp.zeros((packs, LANES), f32),) * STATE)


def scan_forward(decay_step, inputs, maps, rate2):
    count, packs, channels = inputs.shape
    wide = pl.BlockSpec((count, PACKS, LANES), lambda g, i: (0, g, i))
    return pl.pallas_call(
        scan_kernel,
        grid=(packs // PACKS, pl.cdiv(channels, LANES)),
        in_specs=[
            wide,
            wide,
            pl.BlockSpec((count, PACKS, 2 * STATE), lambda g, i: (0, g, 0)),
            pl.BlockSpec((STATE, LANES), lambda g, i: (0, i)),
        ],
        out_specs=wide,
        out_shape=jax.ShapeDtypeStruct(inputs.shape, f32),
        scratch_shapes=[pltpu.VMEM((2 * STATE, count, PACKS, LANES), f32)],
        compiler_params=pltpu.CompilerParams(vmem_limit_bytes=40 * 1024 * 1024),
        cost_estimate=SMALL_COST,
    )(decay_step, inputs, maps, rate2)


def scan_back_kernel(
    channels,
    decay_step_ref,
    step_ref,
    input_ref,
    maps_ref,
    grad_ref,
    rate2_ref,
    rate_ref,
    grad_input_ref,
    grad_step_ref,
    grad_rate_ref,
    grad_maps_ref,
    states_ref,
    in_sum_ref,
    out_sum_ref,
    wide_ref,
):
    count, packs, _ = decay_step_ref.shape
    at = pl.program_id(1)
    valid = lax.broadcasted_iota(jnp.int32, (packs, LANES), 1) < channels - at * LANES
    valid_row = valid[:1]
    rate2 = [jnp.where(valid_row, rate2_ref[n : n + 1, :], 0.0) for n in range(STATE)]
    rate = [jnp.where(valid_row, rate_ref[n : n + 1, :], 0.0) for n in range(STATE)]

    @pl.when(at == 0)
    def _():
        spread_maps(maps_ref, wide_ref)
        in_sum_ref[...] = jnp.zeros_like(in_sum_ref)
        out_sum_ref[...] = jnp.zeros_like(out_sum_ref)

    def forward(i, states):
        for u in range(2):
            t = 2 * i + u
            decay_step = jnp.where(valid, decay_step_ref[t], 0.0)
            inputs = jnp.where(valid, input_ref[t], 0.0)
            new_states = []
            for n in range(STATE):
                state = jnp.exp2(decay_step * rate2[n]) * states[n] + wide_ref[n, t] * inputs
                states_ref[n, t] = state
                new_states.append(state)
            states = tuple(new_states)
        return states

    zero = jnp.zeros((packs, LANES), f32)
    lax.fori_loop(0, count // 2, forward, (zero,) * STATE)

    def backward(back_t, carried):
        grad_states, grad_rates = carried
        t = count - 1 - back_t
        decay_step = jnp.where(valid, decay_step_ref[t], 0.0)
        step = jnp.where(valid, step_ref[t], 0.0)
        inputs = jnp.where(valid, input_ref[t], 0.0)
        grad = jnp.where(valid, grad_ref[t], 0.0)
        grad_input, grad_step = zero, zero
        new_states, new_rates = [], []
        for n in range(STATE):
            state, in_map = states_ref[n, t], wide_ref[n, t]
            grad_state = grad * wide_ref[STATE + n, t] + grad_states[n]
            out_sum_ref[n, t] += grad * state
            in_sum_ref[n, t] += grad_state * inputs
            grad_input = grad_input + grad_state * in_map
            through = grad_state * (state - in_map * inputs)
            grad_step = grad_step + through * rate[n]
            new_rates.append(grad_rates[n] + through * step)
            new_states.append(jnp.exp2(decay_step * rate2[n]) * grad_state)
        grad_input_ref[t] = grad_input
        grad_step_ref[t] = grad_step
        return (tuple(new_states), tuple(new_rates))

    _, grad_rates = lax.fori_loop(0, count, backward, ((zero,) * STATE, (zero,) * STATE))
    for n in range(STATE):
        grad_rate_ref[n : n + 1, :] = jnp.sum(grad_rates[n], axis=0, keepdims=True)

    @pl.when(at == pl.num_programs(1) - 1)
    def _():
        column = lax.broadcasted_iota(jnp.int32, (LANES, LANES), 1)
        total = jnp.zeros((count * packs, LANES), f32)
        for n in range(STATE):
            for sums, place in ((in_sum_ref, n), (out_sum_ref, STATE + n)):
                total = total + jnp.dot(
                    sums[n].reshape(count * packs, LANES).astype(bf16),
                    (column == place).astype(bf16),
                    preferred_element_type=f32,
                )
        grad_maps_ref[...] = total.reshape(count, packs, LANES)


def scan_backward(decay_step, step, inputs, maps, grad, rate2, rate):
    count, packs, channels = inputs.shape
    groups = packs // PACKS
    wide = pl.BlockSpec((count, PACKS, LANES), lambda g, i: (0, g, i))
    row = pl.BlockSpec((STATE, LANES), lambda g, i: (0, i))
    scratch = pltpu.VMEM((STATE, count, PACKS, LANES), f32)
    grad_inputs, grad_step, grad_rate, grad_maps = pl.pallas_call(
        functools.partial(scan_back_kernel, channels),
        grid=(groups, pl.cdiv(channels, LANES)),
        in_specs=[
            wide,
            wide,
            wide,
            pl.BlockSpec((count, PACKS, 2 * STATE), lambda g, i: (0, g, 0)),
            wide,
            row,
            row,
        ],
        out_specs=[
            wide,
            wide,
            pl.BlockSpec((STATE, LANES), lambda g, i: (g, i)),
            pl.BlockSpec((count, PACKS, LANES), lambda g, i: (0, g, 0)),
        ],
        out_shape=[
            jax.ShapeDtypeStruct(inputs.shape, f32),
            jax.ShapeDtypeStruct(inputs.shape, f32),
            jax.ShapeDtypeStruct((groups * STATE, channels), f32),
            jax.ShapeDtypeStruct((count, packs, LANES), f32),
        ],
        scratch_shapes=[
            scratch,
            scratch,
            scratch,
            pltpu.VMEM((2 * STATE, count, PACKS, LANES), f32),
        ],
        compiler_params=pltpu.CompilerParams(vmem_limit_bytes=58 * 1024 * 1024),
        cost_estimate=SMALL_COST,
    )(decay_step, step, inputs, maps, grad, rate2, rate)
    grad_rate = jnp.sum(grad_rate.reshape(groups, STATE, channels), axis=0)
    return grad_inputs, grad_step, grad_rate, grad_maps.reshape(count * packs, LANES)


def split_heads(qkv_low):
    count = qkv_low.shape[0]
    group_size = HEADS // KV_HEADS
    query_width = HEADS * HEAD_DIM
    kv_width = KV_HEADS * HEAD_DIM
    query_rows = qkv_low[:, :query_width].reshape(count, KV_HEADS, group_size, HEAD_DIM)
    key_rows = qkv_low[:, query_width : query_width + kv_width].reshape(count, KV_HEADS, HEAD_DIM)
    value_rows = qkv_low[:, query_width + kv_width :].reshape(count, KV_HEADS, HEAD_DIM)
    return (query_rows, key_rows, value_rows)


def masked_scores(query_rows, key_rows, allowed):
    attention_scores = jnp.einsum(
        "jzhx,kzx->zhjk", query_rows, key_rows, preferred_element_type=f32
    ) * HEAD_DIM ** (-0.5)
    return jnp.where(allowed[None, None], attention_scores, -1e30)


def attention_forward(qkv_low, allowed):
    count = qkv_low.shape[0]
    query_rows, key_rows, value_rows = split_heads(qkv_low)
    attention_scores = masked_scores(query_rows, key_rows, allowed)
    row_max = jnp.max(attention_scores, axis=-1, keepdims=True)
    weights_exp = jnp.exp(attention_scores - row_max)
    row_total = jnp.sum(weights_exp, axis=-1, keepdims=True)
    lowered_probabilities = (weights_exp / row_total).astype(bf16)
    attended_values = jnp.einsum(
        "lpho,ole->hlpe", lowered_probabilities, value_rows, preferred_element_type=f32
    )
    return (attended_values.reshape(count, HEADS * HEAD_DIM), row_max + jnp.log(row_total))


def attention_backward(qkv_low, grad_low, log_total, allowed):
    count = qkv_low.shape[0]
    query_rows, key_rows, value_rows = split_heads(qkv_low)
    probabilities = jnp.exp(masked_scores(query_rows, key_rows, allowed) - log_total)
    head_gradient = grad_low.reshape(count, KV_HEADS, HEADS // KV_HEADS, HEAD_DIM)
    grad_probs = jnp.einsum(
        "jzhx,kzx->zhjk", head_gradient, value_rows, preferred_element_type=f32
    )
    score_gradient = (
        probabilities * (grad_probs - jnp.sum(grad_probs * probabilities, axis=-1, keepdims=True))
    ).astype(bf16)
    scale_factor_scores = HEAD_DIM ** (-0.5)
    grad_queries = (
        jnp.einsum("lpho,ole->hlpe", score_gradient, key_rows, preferred_element_type=f32)
        * scale_factor_scores
    )
    grad_keys = (
        jnp.einsum("wniv,iwne->vwe", score_gradient, query_rows, preferred_element_type=f32)
        * scale_factor_scores
    )
    grad_values = jnp.einsum(
        "wniv,iwne->vwe", probabilities.astype(bf16), head_gradient, preferred_element_type=f32
    )
    return jnp.concatenate(
        [
            grad_queries.reshape(count, -1),
            grad_keys.reshape(count, -1),
            grad_values.reshape(count, -1),
        ],
        axis=1,
    )


def tied(value, *others):
    return lax.optimization_barrier((value,) + others)[0]


def silu_and_slope(value):
    gate = jax.nn.sigmoid(value)
    return value * gate, gate * (1.0 + value * (1.0 - gate))


def shift_down(rows, amount):
    return jnp.concatenate([jnp.zeros((amount,) + rows.shape[1:], rows.dtype), rows[:-amount]], 0)


def shift_up(rows, amount):
    return jnp.concatenate([rows[amount:], jnp.zeros((amount,) + rows.shape[1:], rows.dtype)], 0)


def per_device(
    rep,
    fsdp,
    tokens,
    cotangent,
    lengths,
    source_slot,
    norm_in,
    w_qkv,
    w_mamba_in,
    conv_weight,
    conv_bias,
    x_proj,
    dt_proj,
    dt_bias,
    a_log,
    d_skip,
    w_mamba_out,
    norm_attn,
    norm_ssm,
    w_mix_out,
    norm_ffn,
    w_gate,
    w_up,
    w_down,
):
    count, width = tokens.shape
    block_rows = count // fsdp
    piece, ff_piece = INNER // (rep * fsdp), w_gate.shape[1] // (rep * fsdp)
    channels, ff_part = fsdp * up16(piece), fsdp * up16(ff_piece)
    qkv_part = w_qkv.shape[1] // rep
    group = rep * count
    high = lax.Precision.HIGH
    me, line = lax.axis_index("rep"), lax.axis_index("fsdp")

    def my_part(value, axis):
        rest = value.shape[axis] // (rep * fsdp)
        spare = [(0, up16(rest) - rest if i == axis else 0) for i in range(value.ndim)]
        return jnp.concatenate(
            [
                jnp.pad(lax.dynamic_slice_in_dim(value, (i * rep + me) * rest, rest, axis), spare)
                for i in range(fsdp)
            ],
            axis=axis,
        )

    def my_rows(value):
        rest = value.shape[0] // rep
        part = lax.dynamic_slice_in_dim(value, me * rest, rest, 0)
        return jnp.pad(part, ((0, up16(rest) - rest), (0, 0)))

    def line_gather(value):
        return lax.all_gather(value, "fsdp", axis=0, tiled=True)

    def line_scatter(value):
        return lax.psum_scatter(value, "fsdp", scatter_dimension=0, tiled=True)

    def swapped(rows):
        lead = count if rows.shape[0] == count else rep
        return rows.transpose(1, 0, 2).reshape(group, rows.shape[2])

    early_width = -(-(qkv_part + channels) // LANES) * LANES
    gate_at = -(-(channels + qkv_part) // LANES) * LANES
    in_width = -(-(gate_at + channels) // LANES) * LANES
    part_in = by_rows(
        functools.partial(part_in_kernel, rep, fsdp, (0, channels, gate_at)),
        (w_qkv, w_mamba_in),
        in_width,
    )
    full_in = line_gather(part_in)
    half = w_mix_out.shape[0] // 2
    part_mix = lax.dynamic_slice_in_dim(w_mix_out, lax.rem(me, 2) * half, half, 0)
    part_mout, part_down = my_rows(w_mamba_out), my_rows(w_down)

    received, cot_received = line_exchange(
        fsdp,
        0,
        trades=(
            tied(tokens, part_in).reshape(fsdp, block_rows, width),
            cotangent.reshape(fsdp, block_rows, width),
        ),
    )
    w_gate, w_up, part_mout, part_mix, part_down, received = lax.optimization_barrier(
        (w_gate, w_up, part_mout, part_mix, part_down, received)
    )
    full_mout, half_mix = line_gather(part_mout), line_gather(part_mix)
    part_gate_up = by_rows(
        functools.partial(part_gate_up_kernel, rep, fsdp), (w_gate, w_up), 2 * ff_part
    )
    full_gate_up, full_down = line_gather(part_gate_up), line_gather(part_down)
    slots = source_slot[0]
    picks = (slots[:, None] == jnp.arange(count, dtype=jnp.int32)[None, :]).astype(bf16)
    hidden_in = dot(picks, received.reshape(count, width))
    cot_rows = dot(picks, cot_received.reshape(count, width))
    cot_low = cot_rows.astype(bf16)

    ends = jnp.cumsum(lengths[0], dtype=jnp.int32)
    positions = jnp.arange(count, dtype=jnp.int32)
    passed = positions[:, None] >= ends[None, :-1]
    seg_ids = jnp.sum(passed.astype(jnp.int32), axis=1)
    in_seq = positions - jnp.max(jnp.where(passed, ends[None, :-1], 0), axis=1)
    distance = positions[:, None] - positions[None, :]
    allowed = (seg_ids[:, None] == seg_ids[None, :]) & (distance >= 0) & (distance < WINDOW)

    normed, norm_in_pull = jax.vjp(rms_norm, hidden_in, norm_in)
    marks = jnp.broadcast_to(in_seq[:, None].astype(bf16), (count, 64))
    normed_marked = jnp.concatenate([normed.astype(bf16), marks], axis=1)
    normed_sent, cot_all = rep_exchange(rep, 1, gathers=(normed_marked, cot_low))
    cot_all = cot_all.reshape(group, width)
    normed_all = normed_sent[:, :, :width].reshape(group, width)
    in_seq_all = normed_sent[:, :, width].astype(f32).T.reshape(group, 1)

    in_out = dot(swapped(normed_all.reshape(rep, count, width)), full_in)
    xs, gate_z = in_out[:, :channels], in_out[:, gate_at : gate_at + channels]
    qkv_sent = in_out[:, channels : channels + qkv_part].astype(bf16)
    qkv_sent = swapped(qkv_sent.reshape(count, rep, qkv_part))

    conv_w, conv_b = my_part(conv_weight, 1), my_part(conv_bias, 0)
    part_x_proj, part_dt_proj = my_part(x_proj, 0), my_part(dt_proj, 1)
    part_dt_bias, part_skip = my_part(dt_bias, 0), my_part(d_skip, 0)
    rate = -jnp.exp(my_part(a_log, 1))
    rate2 = rate * LOG2_E
    conv_sum = xs * conv_w[CONV - 1] + conv_b
    for k in range(1, CONV):
        earlier = jnp.where(in_seq_all >= k, shift_down(xs, k * rep), 0.0)
        conv_sum = conv_sum + earlier * conv_w[CONV - 1 - k]
    act, act_slope = silu_and_slope(conv_sum)
    proj_sent = dot(act, part_x_proj, high).reshape(count, rep, -1).transpose(1, 0, 2)
    proj, qkv_back = rep_exchange(
        rep, 2, alls=(proj_sent,), trades=(qkv_sent.reshape(rep, count, qkv_part),)
    )
    qkv_low = qkv_back.transpose(1, 0, 2).reshape(count, rep * qkv_part)
    proj = proj.transpose(1, 0, 2)
    dt_in = proj.reshape(group, -1)[:, :DT_RANK]
    maps = proj[:, :, DT_RANK:]
    dt_sum = dot(dt_in, part_dt_proj, high) + part_dt_bias
    step = jax.nn.softplus(dt_sum)
    decay_step = jnp.where(in_seq_all == 0.0, 1e30, step)
    inputs = step * act
    cube = (count, rep, channels)
    scanned = scan_forward(decay_step.reshape(cube), inputs.reshape(cube), maps, rate2)
    scanned = scanned.reshape(group, channels)
    silu_z, z_slope = silu_and_slope(gate_z)
    before_gate = scanned + part_skip * act
    mixer_low = swapped((before_gate * silu_z).astype(bf16).reshape(cube))
    ssm_part = dot(mixer_low, full_mout).astype(bf16).reshape(rep, count, width)
    (ssm_out,) = rep_exchange(rep, 3, sums=(ssm_part,))

    attended_values, log_total = attention_forward(qkv_low, allowed)
    half_mix, qkv_low = lax.optimization_barrier((half_mix, qkv_low))
    full_mix = pair_gather(9, half_mix.reshape(fsdp, half, width)).reshape(width, width)
    mixed, mix_pull = jax.vjp(mix_branches, attended_values, ssm_out, norm_attn, norm_ssm)
    mixed_low = mixed.astype(bf16)
    middle = hidden_in + dot(mixed_low, full_mix)
    ffn_in, ffn_pull = jax.vjp(rms_norm, middle, norm_ffn)
    ffn_all, mixed_all = rep_exchange(rep, 4, gathers=(ffn_in.astype(bf16), mixed_low))
    ffn_all, mixed_all = ffn_all.reshape(group, width), mixed_all.reshape(group, width)

    gate_up = dot(ffn_all, full_gate_up)
    hidden, swiglu_pull = jax.vjp(swiglu, gate_up[:, :ff_part], gate_up[:, ff_part:])
    hidden_low = hidden.astype(bf16)
    grad_hidden = dot_right_t(cot_all, full_down)
    grad_gate_up = jnp.concatenate(swiglu_pull(grad_hidden), axis=1).astype(bf16)
    ffn_sent = dot_right_t(grad_gate_up, full_gate_up).astype(bf16).reshape(rep, count, width)
    down_sent = dot(hidden_low, full_down).astype(bf16).reshape(rep, count, width)
    grad_ffn, down_out = rep_exchange(rep, 5, sums=(ffn_sent, down_sent))
    result = middle + down_out
    part_gate_up = dot_left_t(ffn_all, grad_gate_up).astype(bf16)
    part_down = dot_left_t(hidden_low, cot_all).astype(bf16)
    grad_ffn = tied(grad_ffn, part_gate_up, part_down)
    own_gate_up, own_down = line_scatter(part_gate_up), line_scatter(part_down)

    grad_middle_norm, grad_norm_ffn = ffn_pull(grad_ffn)
    grad_middle = cot_rows + grad_middle_norm
    middle_low = grad_middle.astype(bf16)
    grad_mixed = dot_right_t(middle_low, full_mix)
    grad_attended, grad_ssm, grad_norm_attn, grad_norm_ssm = mix_pull(grad_mixed)
    middle_sent = middle_low.reshape(count, rep, -1).transpose(1, 0, 2)
    qkv_grad = attention_backward(qkv_low, grad_attended.astype(bf16), log_total, allowed)
    qkv_grad = qkv_grad.astype(bf16).reshape(count, rep, -1).transpose(1, 0, 2)
    ssm_all, middle_cols, qkv_cols = rep_exchange(
        rep, 6, gathers=(grad_ssm.astype(bf16),), trades=(middle_sent, qkv_grad)
    )
    qkv_cols = qkv_cols.reshape(group, qkv_part)
    ssm_all = ssm_all.reshape(group, width)
    grad_mixer = dot_right_t(ssm_all, full_mout).reshape(rep, count, channels)
    grad_mixer = swapped(grad_mixer)
    part_mout = dot_left_t(mixer_low, ssm_all).astype(bf16)
    part_mix = dot_left_t(mixed_all, middle_cols.reshape(group, -1)).astype(bf16)

    grad_z = (grad_mixer * before_gate * z_slope).astype(bf16)
    grad_z = swapped(grad_z.reshape(cube))
    spare = early_width - qkv_part - channels
    early_grad = jnp.concatenate([qkv_cols, jnp.zeros((group, spare), bf16), grad_z], axis=1)
    part_early = dot_left_t(normed_all, early_grad).astype(bf16)
    grad_mixer = tied(grad_mixer, part_mout, part_mix, part_early)
    own_mout, own_mix = line_scatter(part_mout), line_scatter(part_mix)
    own_early = line_scatter(part_early)
    grad_before = grad_mixer * silu_z
    grad_skip = jnp.sum(grad_before * act, axis=0)
    grad_inputs, grad_step, grad_rate, grad_maps = scan_backward(
        *(item.reshape(cube) for item in (decay_step, step, inputs)),
        maps,
        grad_before.reshape(cube),
        rate2,
        rate,
    )
    grad_inputs = grad_inputs.reshape(group, channels)
    grad_step = grad_step.reshape(group, channels)
    grad_a_log = grad_rate * rate
    grad_step = grad_step + grad_inputs * act
    grad_dt = grad_step * jax.nn.sigmoid(dt_sum)
    grad_dt_bias = jnp.sum(grad_dt, axis=0)
    grad_dt_proj = dot_left_t(dt_in, grad_dt)
    proj_sent = jnp.concatenate(
        [dot_right_t(grad_dt, part_dt_proj), grad_maps[:, : 2 * STATE]], axis=1
    )
    proj_sent = proj_sent.reshape(count, rep, -1).transpose(1, 0, 2)
    (grad_proj,) = rep_exchange(rep, 7, alls=(proj_sent,))
    grad_proj = swapped(grad_proj)
    grad_x_proj = dot_left_t(act, grad_proj)
    grad_act = grad_before * part_skip + grad_inputs * step + dot_right_t(grad_proj, part_x_proj)
    grad_conv = grad_act * act_slope
    grad_conv_b = jnp.sum(grad_conv, axis=0)
    grad_conv_w = [jnp.sum(grad_conv * xs, axis=0)]
    grad_xs = grad_conv * conv_w[CONV - 1]
    for k in range(1, CONV):
        reached = jnp.where(in_seq_all >= k, grad_conv, 0.0)
        grad_conv_w.insert(0, jnp.sum(reached * shift_down(xs, k * rep), axis=0))
        grad_xs = grad_xs + shift_up(reached, k * rep) * conv_w[CONV - 1 - k]
    small = jnp.concatenate(
        [jnp.stack(grad_conv_w), grad_conv_b[None], grad_dt_bias[None], grad_skip[None]]
        + [grad_a_log, grad_dt_proj],
        axis=0,
    )
    small = jnp.pad(small, ((0, up16(small.shape[0]) - small.shape[0]), (0, 0))).astype(bf16)
    grad_xs = swapped(grad_xs.astype(bf16).reshape(cube))
    gap = jnp.zeros((group, gate_at - channels - qkv_part), bf16)
    end = jnp.zeros((group, in_width - gate_at - channels), bf16)
    in_grad = jnp.concatenate([grad_xs, qkv_cols, gap, grad_z, end], axis=1)
    normed_part = dot_right_t(in_grad, full_in).astype(bf16).reshape(rep, count, width)
    own_late = line_scatter(dot_left_t(normed_all, grad_xs).astype(bf16))
    (grad_normed,) = rep_exchange(rep, 8, sums=(normed_part,))
    grad_hidden_norm, grad_norm_in = norm_in_pull(grad_normed)
    grad_hidden_in = grad_middle + grad_hidden_norm

    def given_back(rows):
        return dot_left_t(picks, rows.astype(bf16)).astype(bf16).reshape(fsdp, block_rows, width)

    gains = jnp.stack([grad_norm_in, grad_norm_attn, grad_norm_ssm, grad_norm_ffn])
    gains = jnp.concatenate([gains, jnp.zeros((4, width), f32)], axis=0)
    gains, small, x_small, mixed_out, grad_tokens = line_exchange(
        fsdp,
        10,
        gathers=(gains, small, grad_x_proj.astype(bf16)),
        trades=(given_back(result), given_back(grad_hidden_in)),
    )
    gains, small, x_small = (
        jnp.sum(item.astype(f32), axis=0) for item in (gains, small, x_small)
    )

    own_gate_up = tied(own_gate_up, mixed_out)
    all_down, all_gate_up, all_mout, all_mix, all_early = rep_exchange(
        rep, 11, gathers=(own_down, own_gate_up, own_mout, own_mix, own_early)
    )
    own_late = tied(own_late, all_down)
    all_late, small, x_small, gains = rep_exchange(
        rep, 12, gathers=(own_late, small, x_small, gains)
    )
    gains = jnp.sum(gains, axis=0)
    sum_gate, sum_up = join_columns(
        rep,
        (all_gate_up,),
        (w_gate.shape[1], w_up.shape[1]),
        (((0, 0, ff_piece, 0, fsdp),), ((0, ff_part, ff_piece, 0, fsdp),)),
    )
    sum_mamba_in, sum_qkv, sum_mix = join_columns(
        rep,
        (all_late, all_early, all_mix),
        (w_mamba_in.shape[1], w_qkv.shape[1], width),
        (
            ((0, 0, piece, 0, fsdp), (1, early_width - channels, piece, INNER, fsdp)),
            ((1, 0, qkv_part, 0, 1),),
            ((2, 0, width // rep, 0, 1),),
        ),
    )
    (sum_down,) = join_rows(rep, (all_down,), (w_down.shape[0],))
    (sum_mout,) = join_rows(rep, (all_mout,), (w_mamba_out.shape[0],))

    (sum_x_proj,) = join_rows(rep, (x_small,), (x_proj.shape[0],), fsdp)
    (small,) = join_columns(rep, (small,), (INNER,), (((0, 0, piece, 0, fsdp),),))
    ends = [CONV, CONV + 1, CONV + 2, CONV + 3, CONV + 3 + STATE, CONV + 3 + STATE + DT_RANK]
    return (
        mixed_out.reshape(count, width),
        grad_tokens.reshape(count, width),
        gains[0],
        sum_qkv,
        sum_mamba_in,
        small[: ends[0]],
        small[ends[0]],
        sum_x_proj,
        small[ends[4] : ends[5]],
        small[ends[1]],
        small[ends[3] : ends[4]],
        small[ends[2]],
        sum_mout,
        gains[1],
        gains[2],
        sum_mix,
        gains[3],
        sum_gate,
        sum_up,
        sum_down,
    )


def solution(mesh):
    rows = P(("rep", "fsdp"), None)
    cut = P("fsdp", None)
    whole = P()
    return jax.shard_map(
        functools.partial(per_device, mesh.shape["rep"], mesh.shape["fsdp"]),
        mesh=mesh,
        in_specs=(rows,) * 4
        + (whole, cut, cut)
        + (whole,) * 7
        + (cut, whole, whole, cut, whole, cut, cut, cut),
        out_specs=(rows, rows, whole, cut, cut)
        + (whole,) * 7
        + (cut, whole, whole, cut, whole, cut, cut, cut),
        check_vma=False,
    )
```

time: 3170 us -> 979 us (0.31)
  waiting for transfers between devices: 2240 us -> 43.9 us
  Pallas kernels: 0 us -> 595 us
  other arithmetic: 231 us -> 34.8 us
  loops' own time: 169 us -> 0 us
  local copies, waits for them, and re-layouts: 280 us -> 154 us
  matrix products: 192 us -> 127 us
    all_gather x17 -> x5, waiting for transfers between devices: 1700 us -> 41.7 us  [line_gather(): return lax.all_gather(value, 'fsdp', axis=0, tiled=True)]
    pallas_call x0 -> x23, Pallas kernels: none -> 595 us  [the longest x10 367 us: rep_exchange(): pl.pallas_call(functools.partial(rep_kernel, rep, counts, square), out_sh...]
    psum x3 -> x0, waiting for transfers between devices: 486 us -> none  [the longest x2 249 us: per_device(): lax.psum((grad_norm_in, grad_norm_attn, grad_norm_ssm, grad_norm_ffn, gra...]
    another operation x2 -> x0, loops' own time: 169 us -> none  [span_scan(): unused, scanned = lax.scan(checked, zero_state, block_data)]
    reduce_sum x163 -> x8, other arithmetic: 87.3 us -> 7.49 us  [the longest x1 4.16 us: per_device(): grad_dt_bias = jnp.sum(grad_dt, axis=0)]
    slice x74 -> x15, local copies, waits for them, and re-layouts: 85.8 us -> 10.1 us  [the longest x1 3.99 us: per_device(): normed_all = normed_sent[:, :, :width].reshape(group, width)]
    squeeze x80 -> x0, local copies, waits for them, and re-layouts: 67.3 us -> none  [span_scan(): unused, scanned = lax.scan(checked, zero_state, block_data)]
    dot_general x26 -> x27, matrix products: 185 us -> 123 us  [the longest x7 46.8 us: dot_right_t(): lax.dot_general(left, right, (((1,), (1,)), ((), ())), preferred_element_...]
  transfers between devices with their start and end apart: 24 -> 11, of which waited for: 15 -> 2; matrix products, arithmetic and copies ran while one was open for 21% -> 23% of each run, Pallas kernels for 0% -> 54%
where the time goes in v1:
time: 979 us; the launch traced here: 973 us
  Pallas kernels  595 us (61%)
  local copies, waits for them, and re-layouts  154 us (16%)
  matrix products  127 us (13%)
  waiting for transfers between devices  43.9 us (4%)
  other arithmetic  34.8 us (4%)
  between operations  16.1 us (2%)
    pallas_call x10, Pallas kernels, rep_exchange(): pl.pallas_call(functools.partial(rep_kernel, rep, counts, square), out_sh...  367 us
    pallas_call x2, Pallas kernels, line_exchange(): pl.pallas_call(functools.partial(line_kernel, count, len(gathers), len(tr...  98.6 us
    unnamed x306, local copies, waits for them, and re-layouts  81.6 us
    pallas_call x1, Pallas kernels, scan_backward(): pl.pallas_call(functools.partial(scan_back_kernel, channels), grid=(group...  63.6 us
    dot_general x7, matrix products, dot_right_t(): lax.dot_general(left, right, (((1,), (1,)), ((), ())), preferred_element_...  46.8 us
    all_gather x5, waiting for transfers between devices, line_gather(): return lax.all_gather(value, 'fsdp', axis=0, tiled=True)  41.7 us
    dot_general x9, matrix products, dot(): return jnp.dot(left, right, precision=precision, preferred_element_type=f32)  39.5 us
    dot_general x10, matrix products, dot_left_t(): lax.dot_general(left, right, (((0,), (0,)), ((), ())), preferred_element_...  36.3 us
  transfers between devices with their start and end apart: 11, of which 2 were waited for; matrix products, arithmetic and copies ran while one was open for 23% of the time, Pallas kernels for 54%

profile of v1, /device:TPU:0, one launch (start us, length us, event | category | flops | bytes accessed | tf_op | source)
XLA Modules:
  0.0 972.6 jit_solution(3203483697741739293)
XLA Ops:
  23.1 41.3 %shard_map.366 = (bf16[4,32,1600]{2,1,0:T(8,128)(2,1)}, bf16[4,32,1600]{2,1,0:T(8,128)(2,1)}) custom-call(bf16[4,32,1600]{2,1,0:T(8,128)(2,1)} %bitcast.300, bf16[4,32,1600]{2,1,0:T(8,128)(2,1)} %bitcast.301), custom_call_target="tpu_custom_call" | custom-call | bytes 10000 | tf_op jit(solution)/shard_map/pallas_call | solution.py:310
  77.9 32.8 %shard_map.367 = (bf16[8,128,1664]{2,1,0:T(8,128)(2,1)S(1)}, bf16[8,128,1600]{2,1,0:T(8,128)(2,1)S(1)}) custom-call(bf16[128,1664]{1,0:T(8,128)(2,1)S(1)} %pad_maximum_fusion.5.refs_0_, bf16[128,1600]{1,0:T(8,128)(2,1)S(1)} %copy.292.refs_1_), custom_call_target="tpu_custom_call" | custom-call | bytes 10000 | tf_op jit(solution)/shard_map/pallas_call | solution.py:269
  125.5 9.2 fusion
  143.0 27.0 %shard_map.368 = (f32[8,128,132]{2,1,0:T(8,128)S(1)}, bf16[8,128,280]{2,1,0:T(8,128)(2,1)S(1)}) custom-call(f32[8,128,132]{2,1,0:T(8,128)S(1)} %bitcast.259, bf16[8,128,280]{2,1,0:T(8,128)(2,1)S(1)} %bitcast.261), custom_call_target="tpu_custom_call" | custom-call | bytes 10000 | tf_op jit(solution)/shard_map/pallas_call | solution.py:269
  176.5 22.9 %shard_map.369 = f32[128,8,448]{2,1,0:T(8,128)S(1)} custom-call(f32[128,8,448]{2,1,0:T(8,128)S(1)} %get-tuple-element.263.decay_step_ref, f32[128,8,448]{2,1,0:T(8,128)S(1)} %get-tuple-element.261.input_ref, f32[128,8,32]{2,1,0:T(8,128)S(1)} %slice.174.maps_ref, f32[16,448]{1,0:T(8,128)S(1)} %get-tuple-element.254.rate_ref.rate2_ref), custom_call_target="tpu_custom_call" | custom-call | bytes 10000 | tf_op jit(solution)/shard_map/pallas_call | solution.py:502
  211.6 5.6 copy.307
  219.5 22.0 %shard_map.370 = f32[128,1600]{1,0:T(8,128)S(1)} custom-call(bf16[8,128,1600]{2,1,0:T(8,128)(2,1)S(1)} %bitcast.255), custom_call_target="tpu_custom_call" | custom-call | bytes 10000 | tf_op jit(solution)/shard_map/pallas_call | solution.py:269
  245.1 7.2 shard_map.371
  257.3 32.3 %shard_map.372 = (bf16[8,128,1600]{2,1,0:T(8,128)(2,1)S(1)}, bf16[8,128,1600]{2,1,0:T(8,128)(2,1)S(1)}) custom-call(bf16[128,1600]{1,0:T(8,128)(2,1)S(1)} %multiply_convert_fusion.4.refs_0_, bf16[128,1600]{1,0:T(8,128)(2,1)S(1)} %multiply_convert_fusion.5.refs_1_), custom_call_target="tpu_custom_call" | custom-call | bytes 10000 | tf_op jit(solution)/shard_map/pallas_call | solution.py:269
  294.6 10.0 %fusion.110 = f32[1024,1408]{0,1:T(8,128)} fusion(bf16[1024,1600]{1,0:T(8,128)(2,1)} %bitcast.270, bf16[1600,1408]{1,0:T(8,128)(2,1)} %all-gather.14.cloned.1.call-done), kind=kOutput, calls=%fused_computation.295 | convolution fusion | flops 4613734400 | bytes 13549568 | tf_op jit(solution)/shard_map/dot_general | solution.py:28
  304.7 40.1 %all-gather.6.cloned.1.call-done = bf16[704,1600]{1,0:T(8,128)(2,1)} async-done(((bf16[176,1600]{1,0:T(8,128)(2,1)}), bf16[704,1600]{1,0:T(8,128)(2,1)}) %all-gather.6.cloned.1.call-update) | async-done | bytes 2252816 | tf_op jit(solution)/shard_map/all_gather | solution.py:784
  344.8 9.4 fusion.6
  355.3 8.0 convolution_convert_fusion
  367.0 7.4 convolution_convert_fusion.2
  374.4 5.9 copy.313
  380.3 9.2 convolution_convert_fusion.1
  389.5 5.4 copy.312
  398.8 35.8 %shard_map.374 = (f32[128,1600]{1,0:T(8,128)S(1)}, f32[128,1600]{1,0:T(8,128)S(1)}) custom-call(bf16[8,128,1600]{2,1,0:T(8,128)(2,1)S(1)} %bitcast.258, bf16[8,128,1600]{2,1,0:T(8,128)(2,1)S(1)} %bitcast.257), custom_call_target="tpu_custom_call" | custom-call | bytes 10000 | tf_op jit(solution)/shard_map/pallas_call | solution.py:269
  457.2 33.1 %shard_map.375 = (bf16[8,128,1600]{2,1,0:T(8,128)(2,1)S(1)}, bf16[8,128,200]{2,1,0:T(8,128)(2,1)S(1)}, bf16[8,128,280]{2,1,0:T(8,128)(2,1)S(1)}) custom-call(bf16[128,1600]{1,0:T(8,128)(2,1)S(1)} %get-tuple-element.281.refs_0_, bf16[8,128,200]{2,1,0:T(8,128)(2,1)S(1)} %bitcast.263, bf16[8,128,280]{2,1,0:T(8,128)(2,1)S(1)} %bitcast.262), custom_call_target="tpu_custom_call" | custom-call | bytes 10000 | tf_op jit(solution)/shard_map/pallas_call | solution.py:269
  520.1 6.4 convolution_convert_fusion.5
  531.5 63.6 %shard_map.376 = (f32[128,8,448]{2,1,0:T(8,128)}, f32[128,8,448]{2,1,0:T(8,128)}, f32[16,448]{1,0:T(8,128)}, f32[128,8,128]{2,1,0:T(8,128)}) custom-call(f32[128,8,448]{2,1,0:T(8,128)} %copy-done.4, f32[128,8,448]{2,1,0:T(8,128)} %get-tuple-element.262.step_ref, f32[128,8,448]{2,1,0:T(8,128)} %copy-done.3, f32[128,8,32]{2,1,0:T(8,128)} %copy-done.13, ...), custom_call_target="tpu_custom_call" | custom-call | bytes 10000 | tf_op jit(solution)/shard_map/pallas_call | solution.py:613
  602.4 20.1 %shard_map.377 = f32[8,128,132]{2,1,0:T(8,128)S(1)} custom-call(f32[8,128,132]{2,1,0:T(8,128)S(1)} %bitcast.260), custom_call_target="tpu_custom_call" | custom-call | bytes 10000 | tf_op jit(solution)/shard_map/pallas_call | solution.py:269
  622.6 8.4 multiply_reduce_fusion
  646.5 9.2 convolution_convert_fusion.4
  655.7 5.4 copy.342
  663.1 22.0 %shard_map.378 = f32[128,1600]{1,0:T(8,128)S(1)} custom-call(bf16[8,128,1600]{2,1,0:T(8,128)(2,1)S(1)} %bitcast.256), custom_call_target="tpu_custom_call" | custom-call | bytes 10000 | tf_op jit(solution)/shard_map/pallas_call | solution.py:269
  695.5 57.2 %shard_map.379 = (f32[4,8,1600]{2,1,0:T(8,128)}, bf16[4,128,448]{2,1,0:T(8,128)(2,1)}, bf16[4,448,132]{2,1,0:T(8,128)(2,1)}, bf16[4,32,1600]{2,1,0:T(8,128)(2,1)}, bf16[4,32,1600]{2,1,0:T(8,128)(2,1)}) custom-call(f32[8,1600]{1,0:T(8,128)} %concatenate.88.refs_0_, bf16[128,448]{1,0:T(8,128)(2,1)} %pad.138.refs_1_, bf16[448,132]{1,0:T(8,128)(2,1)} %copy.348.refs_2_, ...), custom_call_target="tpu_custom_call" | custom-call | bytes 10000 | tf_op jit(solution)/shard_map/pallas_call | solution.py:310
  763.4 99.2 %shard_map.380 = (bf16[8,176,1600]{2,1,0:T(8,128)(2,1)S(1)}, bf16[8,400,1408]{2,1,0:T(8,128)(2,1)}, bf16[8,112,1600]{2,1,0:T(8,128)(2,1)S(1)}, bf16[8,400,200]{2,1,0:T(8,128)(2,1)S(1)}, bf16[8,400,768]{2,1,0:T(8,128)(2,1)}) custom-call(bf16[176,1600]{1,0:T(8,128)(2,1)S(1)} %copy-done.34, bf16[400,1408]{1,0:T(8,128)(2,1)S(1)} %copy-done.28, ...), custom_call_target="tpu_custom_call" | custom-call | bytes 10000 | tf_op jit(solution)/shard_map/pallas_call | solution.py:269
  871.1 43.0 %shard_map.381 = (bf16[8,400,448]{2,1,0:T(8,128)(2,1)S(1)}, f32[8,128,448]{2,1,0:T(8,128)S(1)}, f32[8,448,132]{2,1,0:T(8,128)S(1)}, f32[8,8,1600]{2,1,0:T(8,128)S(1)}) custom-call(bf16[400,448]{1,0:T(8,128)(2,1)S(1)} %copy-done.35, f32[128,448]{1,0:T(8,128)S(1)} %convert_reduce_fusion.1.refs_1_, f32[448,132]{1,0:T(8,128)S(1)} %convert_reduce_fusion.refs_2_, ...), custom_call_target="tpu_custom_call" | custom-call | bytes 10000 | tf_op jit(solution)/shard_map/pallas_call | solution.py:269
  922.1 10.3 %copy.354 = f32[1376,1600]{0,1:T(8,128)} copy(f32[1376,1600]{1,0:T(8,128)} %copy-done.2) | data formatting | bytes 17612800
  932.4 11.7 %shard_map.386 = (f32[400,5504]{1,0:T(8,128)}, f32[400,5504]{1,0:T(8,128)}) custom-call(bf16[8,400,1408]{2,1,0:T(8,128)(2,1)} %get-tuple-element.115.refs_0_), custom_call_target="tpu_custom_call" | custom-call | bytes 10000 | tf_op jit(solution)/shard_map/pallas_call | solution.py:447
  956.2 9.7 shard_map.382
  (492 shorter events, 225.5 us)
Async XLA Ops:
  7.2 118.3 %all-gather.8.cloned.1.call-start = ((), (), s32[]{:S(2)}) async-start(), calls=%async_computation.7 | async-start | bytes 5120000 | tf_op jit(solution)/shard_map/all_gather | solution.py:784
  15.5 191.1 %all-gather.10.cloned.1.call-start = ((), (), s32[]{:S(2)}) async-start(), calls=%async_computation.8 | async-start | bytes 1863680 | tf_op jit(solution)/shard_map/all_gather | solution.py:784
  18.4 46.0 %copy-start.82 = (bf16[400,1600]{1,0:T(8,128)(2,1)S(1)}, bf16[400,1600]{1,0:T(8,128)(2,1)}, u32[]{:S(2)}) copy-start(bf16[400,1600]{1,0:T(8,128)(2,1)} %param.39) | copy-start | bytes 3840004
  65.4 179.6 %all-gather.12.cloned.1.call-start = ((), (), s32[]{:S(2)}) async-start(), calls=%async_computation.9 | async-start | bytes 3328000 | tf_op jit(solution)/shard_map/all_gather | solution.py:784
  66.1 228.5 %all-gather.14.cloned.1.call-start = ((), (), s32[]{:S(2)}) async-start(), calls=%async_computation.10 | async-start | bytes 5632000 | tf_op jit(solution)/shard_map/all_gather | solution.py:784
  74.3 270.5 %all-gather.6.cloned.1.call-start = ((), (), s32[]{:S(2)}) async-start(), calls=%async_computation.6 | async-start | bytes 2928640 | tf_op jit(solution)/shard_map/all_gather | solution.py:784
  74.9 683.0 %reduce-scatter.11.cloned.1.call-start = ((), (), s32[]{:S(2)}) async-start(), calls=%async_computation.13 | async-start | bytes 5632000 | tf_op jit(solution)/shard_map/reduce_scatter | solution.py:787
  122.4 49.0 %copy-start.84 = (f32[100,100]{1,0:T(8,128)}, f32[100,100]{1,0:T(8,128)S(1)}, u32[]{:S(2)}) copy-start(f32[100,100]{1,0:T(8,128)S(1)} %get-tuple-element.274) | copy-start | bytes 120004
  122.4 49.0 %copy-start.86 = (f32[100,100]{1,0:T(8,128)}, f32[100,100]{1,0:T(8,128)S(1)}, u32[]{:S(2)}) copy-start(f32[100,100]{1,0:T(8,128)S(1)} %get-tuple-element.275) | copy-start | bytes 120004
  122.4 49.0 %copy-start.88 = (f32[100,100]{1,0:T(8,128)}, f32[100,100]{1,0:T(8,128)S(1)}, u32[]{:S(2)}) copy-start(f32[100,100]{1,0:T(8,128)S(1)} %get-tuple-element.276) | copy-start | bytes 120004
  122.4 49.0 %copy-start.90 = (f32[100,100]{1,0:T(8,128)}, f32[100,100]{1,0:T(8,128)S(1)}, u32[]{:S(2)}) copy-start(f32[100,100]{1,0:T(8,128)S(1)} %get-tuple-element.277) | copy-start | bytes 120004
  125.4 51.1 %copy-start.37 = (f32[16,448]{1,0:T(8,128)}, f32[16,448]{1,0:T(8,128)S(1)}, u32[]{:S(2)}) copy-start(f32[16,448]{1,0:T(8,128)S(1)} %get-tuple-element.254.rate_ref.rate2_ref) | copy-start | bytes 86020
  125.5 74.0 %copy-start.109 = (f32[448]{0:T(512)}, f32[448]{0:T(512)S(1)}, u32[]{:S(2)}) copy-start(f32[448]{0:T(512)S(1)} %select_maximum_fusion.12) | copy-start | bytes 5380
  176.5 23.0 %copy-start.3 = (f32[128,8,448]{2,1,0:T(8,128)}, f32[128,8,448]{2,1,0:T(8,128)S(1)}, u32[]{:S(2)}) copy-start(f32[128,8,448]{2,1,0:T(8,128)S(1)} %get-tuple-element.261.input_ref) | copy-start | bytes 5505028
  176.5 23.0 %copy-start.4 = (f32[128,8,448]{2,1,0:T(8,128)}, f32[128,8,448]{2,1,0:T(8,128)S(1)}, u32[]{:S(2)}) copy-start(f32[128,8,448]{2,1,0:T(8,128)S(1)} %get-tuple-element.263.decay_step_ref) | copy-start | bytes 5505028
  257.1 47.6 %copy-start.138 = (f32[128]{0:T(128)}, f32[128]{0:T(128)S(1)}, u32[]{:S(2)}) copy-start(f32[128]{0:T(128)S(1)} %get-tuple-element.318) | copy-start | bytes 1540
  257.1 183.9 %copy-start.53 = (f32[128,1600]{1,0:T(8,128)}, f32[128,1600]{1,0:T(8,128)S(1)}, u32[]{:S(2)}) copy-start(f32[128,1600]{1,0:T(8,128)S(1)} %get-tuple-element.319) | copy-start | bytes 2457604
  257.1 47.6 %copy-start.123 = (f32[128]{0:T(128)}, f32[128]{0:T(128)S(1)}, u32[]{:S(2)}) copy-start(f32[128]{0:T(128)S(1)} %fusion.86) | copy-start | bytes 1540
  363.3 394.7 %reduce-scatter.15.cloned.1.call-start = ((), (), s32[]{:S(2)}) async-start(), calls=%async_computation.15 | async-start | bytes 1024000 | tf_op jit(solution)/shard_map/reduce_scatter | solution.py:787
  398.8 35.8 %copy-start.40 = (bf16[8,128,1600]{2,1,0:T(8,128)(2,1)S(1)}, bf16[8,128,1600]{2,1,0:T(8,128)(2,1)}, u32[]{:S(2)}) copy-start(bf16[8,128,1600]{2,1,0:T(8,128)(2,1)} %copy-done.39) | copy-start | bytes 9830404
  398.8 35.8 %copy-start.143 = (bf16[1024,704]{0,1:T(8,128)(2,1)S(1)}, bf16[1024,704]{0,1:T(8,128)(2,1)}, u32[]{:S(2)}) copy-start(bf16[1024,704]{0,1:T(8,128)(2,1)} %get-tuple-element.258) | copy-start | bytes 4325380
  496.4 261.6 %reduce-scatter.13.cloned.1.call-start = ((), (), s32[]{:S(2)}) async-start(), calls=%async_computation.14 | async-start | bytes 1863680 | tf_op jit(solution)/shard_map/reduce_scatter | solution.py:787
  501.8 256.2 %reduce-scatter.9.cloned.1.call-start = ((), (), s32[]{:S(2)}) async-start(), calls=%async_computation.12 | async-start | bytes 2928640 | tf_op jit(solution)/shard_map/reduce_scatter | solution.py:787
  502.6 255.5 %reduce-scatter.17.cloned.1.call-start = ((), (), s32[]{:S(2)}) async-start(), calls=%async_computation.16 | async-start | bytes 3072000 | tf_op jit(solution)/shard_map/reduce_scatter | solution.py:787
  526.5 343.6 %reduce-scatter.7.cloned.1.call-start = ((), (), s32[]{:S(2)}) async-start(), calls=%async_computation.11 | async-start | bytes 2048000 | tf_op jit(solution)/shard_map/reduce_scatter | solution.py:787
  531.5 64.9 %copy-start.47 = (f32[1024,448]{1,0:T(8,128)S(1)}, f32[1024,448]{1,0:T(8,128)}, u32[]{:S(2)}) copy-start(f32[1024,448]{1,0:T(8,128)} %copy-done.45) | copy-start | bytes 5505028
  663.1 22.1 %copy-start.52 = (f32[128,1600]{1,0:T(8,128)S(1)}, f32[128,1600]{1,0:T(8,128)}, u32[]{:S(2)}) copy-start(f32[128,1600]{1,0:T(8,128)} %copy-done.50) | copy-start | bytes 2457604
  663.1 22.1 %copy-start.94 = (f32[1600]{0:T(1024)S(1)}, f32[1600]{0:T(1024)}, u32[]{:S(2)}) copy-start(f32[1600]{0:T(1024)} %param.26) | copy-start | bytes 19204
  663.1 22.1 %copy-start.122 = (f32[128]{0:T(128)S(1)}, f32[128]{0:T(128)}, u32[]{:S(2)}) copy-start(f32[128]{0:T(128)} %copy-done.121) | copy-start | bytes 1540
  663.1 22.4 %copy-start.135 = (f32[128]{0:T(128)S(1)}, f32[128]{0:T(128)}, u32[]{:S(2)}) copy-start(f32[128]{0:T(128)} %copy-done.134) | copy-start | bytes 1540
  663.1 22.4 %copy-start.73 = (f32[128,1600]{1,0:T(8,128)S(1)}, f32[128,1600]{1,0:T(8,128)}, u32[]{:S(2)}) copy-start(f32[128,1600]{1,0:T(8,128)} %get-tuple-element.253) | copy-start | bytes 2457604
  663.1 22.4 %copy-start.120 = (s32[1,128]{1,0:T(1,128)S(1)}, s32[1,128]{1,0:T(1,128)}, u32[]{:S(2)}) copy-start(s32[1,128]{1,0:T(1,128)} %param.25) | copy-start | bytes 1540
  (126 other events, 735.3 us)
Sparse Core Ops, SparseCore 0:
  15.7 99.2 all-gather.7
  117.0 34.8 all-gather.9
  153.5 54.3 all-gather.11
  209.9 84.6 all-gather.13
  296.0 48.6 all-gather.5
  363.4 80.7 reduce-scatter.10
  496.5 21.5 reduce-scatter.14
  520.5 33.4 reduce-scatter.12
  556.9 46.8 reduce-scatter.8
  606.6 49.0 reduce-scatter.16
  658.6 35.8 reduce-scatter.6

commit v2 on v1

--- a/solution.py
+++ b/solution.py
@@ -4,6 +4,7 @@
 import jax.numpy as jnp
 from jax import lax
 from jax.experimental import pallas as pl
+from jax.experimental.layout import Layout, with_layout_constraint
 from jax.experimental.pallas import tpu as pltpu
 from jax.sharding import PartitionSpec as P
 
@@ -283,42 +284,214 @@
     )(*gathers, *sums, *alls, *trades)
 
 
-def line_kernel(count, n_gather, n_trade, *refs):
-    n_in = n_gather + n_trade
-    ins, outs, (local, remote) = refs[:n_in], refs[n_in : 2 * n_in], refs[2 * n_in :]
+def line_kernel(count, counts, *refs):
+    n_gather, n_all, n_trade = counts
+    n_in = sum(counts)
+    ins, outs, scratch = refs[:n_in], refs[n_in : 2 * n_in], refs[2 * n_in :]
+    arrived, totals = scratch[:n_all], scratch[n_all : 2 * n_all]
+    local, remote = scratch[2 * n_all :]
     me = lax.axis_index("fsdp")
     others = [lax.rem(me + k, count) for k in range(1, count)]
     meet("fsdp", others)
-    copies = []
-    for i in range(n_in):
-        own = ins[i] if i < n_gather else ins[i].at[me]
-        copy = pltpu.make_async_copy(own, outs[i].at[me], local.at[i])
+    copies, coming = [], []
+
+    def push(block, out, slot):
+        return [
+            send(block(other), out, (remote.at[0, slot, k], remote.at[1, slot, k]), "fsdp", other)
+            for k, other in enumerate(others)
+        ]
+
+    def keep(block, out, slot):
+        copy = pltpu.make_async_copy(block, out, local.at[slot])
         copy.start()
         copies.append(copy)
-        for k, other in enumerate(others):
-            block = ins[i] if i < n_gather else ins[i].at[other]
-            sems = (remote.at[0, i, k], remote.at[1, i, k])
-            copies.append(send(block, outs[i].at[me], sems, "fsdp", other))
+
+    for i in range(n_all):
+        source = ins[n_gather + i]
+        coming.append(push(lambda other: source.at[other], arrived[i].at[me], n_in + i))
+    for i in range(n_in):
+        if i < n_gather:
+            keep(ins[i], outs[i].at[me], i)
+            copies += push(lambda other: ins[i], outs[i].at[me], i)
+        elif i >= n_gather + n_all:
+            keep(ins[i].at[me], outs[i].at[me], i)
+            copies += push(lambda other: ins[i].at[other], outs[i].at[me], i)
+    for i in range(n_all):
+        for copy in coming[i]:
+            copy.wait()
+        total = ins[n_gather + i][me].astype(f32)
+        for other in others:
+            total = total + arrived[i][other].astype(f32)
+        totals[i][...] = total.astype(totals[i].dtype)
+        out = outs[n_gather + i]
+        keep(totals[i], out.at[me], n_gather + i)
+        copies += push(lambda other: totals[i], out.at[me], n_gather + i)
     for copy in copies:
         copy.wait()
 
 
-def line_exchange(count, collective_id, gathers=(), trades=()):
-    arrays = (*gathers, *trades)
+def line_exchange(count, collective_id, gathers=(), alls=(), trades=()):
+    arrays = (*gathers, *alls, *trades)
     out_shape = [jax.ShapeDtypeStruct((count,) + x.shape, x.dtype) for x in gathers]
-    out_shape += [jax.ShapeDtypeStruct(x.shape, x.dtype) for x in trades]
+    out_shape += [jax.ShapeDtypeStruct(x.shape, x.dtype) for x in (*alls, *trades)]
     return pl.pallas_call(
-        functools.partial(line_kernel, count, len(gathers), len(trades)),
+        functools.partial(line_kernel, count, (len(gathers), len(alls), len(trades))),
         out_shape=out_shape,
         in_specs=[vmem_spec()] * len(arrays),
         out_specs=[hbm_spec()] * len(arrays),
-        scratch_shapes=[
+        scratch_shapes=[pltpu.VMEM(x.shape, x.dtype) for x in alls]
+        + [pltpu.VMEM(x.shape[1:], x.dtype) for x in alls]
+        + [
             pltpu.SemaphoreType.DMA((len(arrays),)),
-            pltpu.SemaphoreType.DMA((2, len(arrays), count)),
+            pltpu.SemaphoreType.DMA((2, len(arrays) + len(alls), count)),
         ],
         compiler_params=pltpu.CompilerParams(collective_id=collective_id, has_side_effects=True),
         cost_estimate=SMALL_COST,
     )(*arrays)
+
+
+def last_kernel(rep, fsdp, square, n_gather, *refs):
+    chips = rep // 2
+    gathers, refs = refs[:n_gather], refs[n_gather:]
+    small, gains, trades, refs = refs[0], refs[1], refs[2:4], refs[4:]
+    gathered, refs = refs[:n_gather], refs[n_gather:]
+    small_out, gains_out, traded, refs = refs[0], refs[1], refs[2:4], refs[4:]
+    arrived, total, lined, gains_in, gains_sum, local, far, near, remote = refs
+
+    me, line = lax.axis_index("rep"), lax.axis_index("fsdp")
+    core = lax.rem(me, 2)
+    chip = (me - core) // 2
+    partner = 2 * chip + 1 - core
+    if square:
+        along_x, along_y = chip + 1 - 2 * lax.rem(chip, 2), lax.rem(chip + 2, 4)
+        first = along_x + core * (along_y - along_x)
+        second = along_y + core * (along_x - along_y)
+        hops, sources = [first, second], [first, second, 3 - chip]
+    else:
+        hops = [lax.rem(chip + k, chips) for k in range(1, chips)]
+        sources = [lax.rem(chip + chips - k, chips) for k in range(1, chips)]
+    others = [lax.rem(line + k, fsdp) for k in range(1, fsdp)]
+    barrier = pltpu.get_barrier_semaphore()
+    for axis, indices in (("rep", [2 * hop + core for hop in hops] + [partner]), ("fsdp", others)):
+        for index in indices:
+            pl.semaphore_signal(
+                barrier, inc=1, device_id={axis: index}, device_id_type=pl.DeviceIdType.MESH
+            )
+    pl.semaphore_wait(barrier, len(hops) + 1 + len(others))
+
+    kept, sent, waited = [], [], []
+
+    def keep(src, dst):
+        copy = pltpu.make_async_copy(src, dst, local.at[len(kept)])
+        copy.start()
+        kept.append(copy)
+
+    def push(block, out, slot):
+        copies = [
+            send(block(other), out, (remote.at[0, slot, k], remote.at[1, slot, k]), "fsdp", other)
+            for k, other in enumerate(others)
+        ]
+        return copies
+
+    def hop_send(src, dst, slot, k, target):
+        copy = send(src, dst, (far.at[0, slot, k], far.at[1, slot, k]), "rep", 2 * target + core)
+        sent.append(copy)
+        return copy
+
+    def cross_send(src, dst, slot, k):
+        copy = send(src, dst, (near.at[0, slot, k], near.at[1, slot, k]), "rep", partner)
+        sent.append(copy)
+        waited.append(copy)
+
+    def start_gather(source, out, slot):
+        far_copies = [
+            hop_send(source, out.at[me], slot, k, hop) for k, hop in enumerate(hops)
+        ]
+        cross_send(source, out.at[me], slot, chips - 1)
+        keep(source, out.at[me])
+        return out, slot, far_copies
+
+    def pass_on(state):
+        out, slot, far_copies = state
+        for k, source in enumerate(sources):
+            block = out.at[2 * source + core]
+            far_copies[k].wait_recv()
+            if square and k == 0:
+                far_copies.append(hop_send(block, block, slot, 2, second))
+            cross_send(block, block, slot, k)
+
+    small_copies = push(lambda other: small.at[other], arrived.at[line], 0)
+    states = [start_gather(gains, gains_in, 0)]
+    for i in range(n_gather):
+        states.append(start_gather(gathers[i], gathered[i], 1 + i))
+    for i in range(2):
+        keep(trades[i].at[line], traded[i].at[line])
+        waited += push(lambda other: trades[i].at[other], traded[i].at[line], 1 + i)
+        sent += waited[-len(others) :]
+    for copy in small_copies:
+        copy.wait()
+    value = small[line].astype(f32)
+    for other in others:
+        value = value + arrived[other].astype(f32)
+    total[...] = value.astype(total.dtype)
+    small_copies = push(lambda other: total, lined.at[line], 3)
+    lined[line] = total[...]
+
+    gains_state, states = states[0], states[1:]
+    crossed = len(waited)
+    pass_on(gains_state)
+    for copy in waited[crossed:]:
+        copy.wait_recv()
+    for state in states:
+        pass_on(state)
+    for copy in small_copies:
+        copy.wait()
+    small_state = start_gather(lined, small_out, 1 + n_gather)
+    kept[0].wait()
+    waited.pop(0).wait_recv()
+    gains_sum[...] = jnp.sum(gains_in[...], axis=0)
+    keep(gains_sum, gains_out.at[line])
+    gains_copies = push(lambda other: gains_sum, gains_out.at[line], 4)
+    pass_on(small_state)
+    for copy in waited[: crossed - 1] + waited[crossed - 1 + chips - 1 :]:
+        copy.wait_recv()
+    for copy in sent:
+        copy.wait_send()
+    for copy in gains_copies:
+        copy.wait()
+    for copy in kept[1:]:
+        copy.wait()
+
+
+def last_exchange(rep, fsdp, collective_id, gathers, small, gains, trades):
+    n_gather, chips = len(gathers), rep // 2
+    out_shape = [jax.ShapeDtypeStruct((rep,) + x.shape, x.dtype) for x in gathers]
+    out_shape.append(jax.ShapeDtypeStruct((rep,) + small.shape, small.dtype))
+    out_shape.append(jax.ShapeDtypeStruct((fsdp,) + gains.shape, gains.dtype))
+    out_shape += [jax.ShapeDtypeStruct(x.shape, x.dtype) for x in trades]
+    return pl.pallas_call(
+        functools.partial(last_kernel, rep, fsdp, rep == 8, n_gather),
+        out_shape=out_shape,
+        in_specs=[vmem_spec()] * (n_gather + 4),
+        out_specs=[hbm_spec()] * (n_gather + 4),
+        scratch_shapes=[
+            pltpu.VMEM(small.shape, small.dtype),
+            pltpu.VMEM(small.shape[1:], small.dtype),
+            pltpu.VMEM(small.shape, small.dtype),
+            pltpu.VMEM((rep,) + gains.shape, gains.dtype),
+            pltpu.VMEM(gains.shape, gains.dtype),
+            pltpu.SemaphoreType.DMA((n_gather + 5,)),
+            pltpu.SemaphoreType.DMA((2, n_gather + 2, chips)),
+            pltpu.SemaphoreType.DMA((2, n_gather + 2, chips)),
+            pltpu.SemaphoreType.DMA((2, 5, fsdp)),
+        ],
+        compiler_params=pltpu.CompilerParams(
+            collective_id=collective_id,
+            has_side_effects=True,
+            vmem_limit_bytes=40 * 1024 * 1024,
+        ),
+        cost_estimate=SMALL_COST,
+    )(*gathers, small, gains, *trades)
 
 
 def pair_kernel(own_ref, out_ref, local, send_sem, recv_sem):
@@ -417,28 +590,30 @@
                     out[:, at : at + rest] = piece.astype(f32)
 
 
-def join_rows_kernel(rep, pieces, rest, *refs):
-    for source, out, rows in zip(refs[: len(rest)], refs[len(rest) :], rest):
-        for i in range(pieces):
-            for r in range(rep):
-                at, start = (i * rep + r) * rows, i * up16(rows)
-                out[at : at + rows, :] = source[r, start : start + rows, :].astype(f32)
-
-
-def join_rows(rep, sources, totals, pieces=1):
-    width = sources[0].shape[2]
-    block = min(2 * LANES, width)
+def join_rows_kernel(rep, rows, flip, source, out):
+    for r in range(rep):
+        if flip:
+            out[:, r * rows : (r + 1) * rows] = source[r].astype(f32).T[:, :rows]
+        else:
+            out[r * rows : (r + 1) * rows, :] = source[r, :rows, :].astype(f32)
+
+
+def join_rows(rep, source, total, width, flip=False):
+    block = 2 * LANES
+    shape = (total, width)
+    out_spec = pl.BlockSpec((total, block), lambda i: (0, i))
+    if flip:
+        shape = (width, total)
+        out_spec = pl.BlockSpec((block, total), lambda i: (i, 0))
     return pl.pallas_call(
-        functools.partial(join_rows_kernel, rep, pieces, tuple(n // rep // pieces for n in totals)),
+        functools.partial(join_rows_kernel, rep, total // rep, flip),
         grid=(pl.cdiv(width, block),),
-        in_specs=[
-            pl.BlockSpec((rep, x.shape[1], block), lambda i: (0, 0, i)) for x in sources
-        ],
-        out_specs=[pl.BlockSpec((n, block), lambda i: (0, i)) for n in totals],
-        out_shape=[jax.ShapeDtypeStruct((n, width), f32) for n in totals],
+        in_specs=[pl.BlockSpec((rep, source.shape[1], block), lambda i: (0, 0, i))],
+        out_specs=out_spec,
+        out_shape=jax.ShapeDtypeStruct(shape, f32),
         compiler_params=pltpu.CompilerParams(vmem_limit_bytes=40 * 1024 * 1024),
         cost_estimate=SMALL_COST,
-    )(*sources)
+    )(source)
 
 
 def join_columns(rep, sources, widths, layout):
@@ -457,7 +632,7 @@
     )(*sources)
 
 
-def spread_maps(maps_ref, wide_ref):
+def spread_maps(maps_ref, wide_ref, start):
     count, packs, columns = maps_ref.shape
 
     def spread(i, _):
@@ -465,29 +640,47 @@
             t = 2 * i + u
             maps = maps_ref[t]
             for n in range(columns):
-                wide_ref[n, t] = jnp.broadcast_to(maps[:, n : n + 1], (packs, LANES))
+                wide_ref[n, start + t] = jnp.broadcast_to(maps[:, n : n + 1], (packs, LANES))
         return 0
 
     lax.fori_loop(0, count // 2, spread, 0)
 
 
-def scan_kernel(decay_step_ref, input_ref, maps_ref, rate_ref, out_ref, wide_ref):
+def scan_kernel(
+    channels,
+    decay_step_ref,
+    input_ref,
+    maps_ref,
+    rate_ref,
+    _handed_ref,
+    out_ref,
+    decayed_ref,
+    _handed_on_ref,
+    wide_ref,
+):
     count, packs, _ = decay_step_ref.shape
+    valid = (
+        lax.broadcasted_iota(jnp.int32, (packs, LANES), 1)
+        < channels - pl.program_id(1) * LANES
+    )
+    rate = jnp.where(valid[:1], rate_ref[...], 0.0)
 
     @pl.when(pl.program_id(1) == 0)
     def _():
-        spread_maps(maps_ref, wide_ref)
+        spread_maps(maps_ref, wide_ref, 0)
 
     def step(i, states):
         for u in range(2):
             t = 2 * i + u
-            decay_step, inputs = decay_step_ref[t], input_ref[t]
+            decay_step = jnp.where(valid, decay_step_ref[t], 0.0)
+            inputs = jnp.where(valid, input_ref[t], 0.0)
             out = jnp.zeros((packs, LANES), f32)
             new_states = []
             for n in range(STATE):
-                decay = jnp.exp2(decay_step * rate_ref[n : n + 1, :])
-                state = decay * states[n] + wide_ref[n, t] * inputs
+                decayed = jnp.exp2(decay_step * rate[n : n + 1]) * states[n]
+                state = decayed + wide_ref[n, t] * inputs
                 out = out + state * wide_ref[STATE + n, t]
+                decayed_ref[n, t] = decayed
                 new_states.append(state)
             out_ref[t] = out
             states = tuple(new_states)
@@ -496,155 +689,275 @@
     lax.fori_loop(0, count // 2, step, (jnp.zeros((packs, LANES), f32),) * STATE)
 
 
-def scan_forward(decay_step, inputs, maps, rate2):
+def scan_forward(decay_step, inputs, maps, rate, handed):
     count, packs, channels = inputs.shape
     wide = pl.BlockSpec((count, PACKS, LANES), lambda g, i: (0, g, i))
     return pl.pallas_call(
-        scan_kernel,
+        functools.partial(scan_kernel, channels),
         grid=(packs // PACKS, pl.cdiv(channels, LANES)),
         in_specs=[
             wide,
             wide,
             pl.BlockSpec((count, PACKS, 2 * STATE), lambda g, i: (0, g, 0)),
             pl.BlockSpec((STATE, LANES), lambda g, i: (0, i)),
+            hbm_spec(),
         ],
-        out_specs=wide,
-        out_shape=jax.ShapeDtypeStruct(inputs.shape, f32),
+        out_specs=[
+            wide,
+            pl.BlockSpec((STATE, count, PACKS, LANES), lambda g, i: (0, 0, g, i)),
+            hbm_spec(),
+        ],
+        input_output_aliases={4: 2},
+        out_shape=[
+            jax.ShapeDtypeStruct(inputs.shape, f32),
+            jax.ShapeDtypeStruct(
+                (STATE, count, packs, pl.cdiv(channels, LANES) * LANES), f32
+            ),
+            jax.ShapeDtypeStruct(handed.shape, handed.dtype),
+        ],
         scratch_shapes=[pltpu.VMEM((2 * STATE, count, PACKS, LANES), f32)],
-        compiler_params=pltpu.CompilerParams(vmem_limit_bytes=40 * 1024 * 1024),
+        compiler_params=pltpu.CompilerParams(vmem_limit_bytes=48 * 1024 * 1024),
         cost_estimate=SMALL_COST,
-    )(decay_step, inputs, maps, rate2)
+    )(decay_step, inputs, maps, rate, handed)
+
+
+def spread_beside(rep, steps, source, out, local, far, near):
+    chips, square = rep // 2, rep == 8
+    me = lax.axis_index("rep")
+    core = lax.rem(me, 2)
+    chip = (me - core) // 2
+    partner = 2 * chip + 1 - core
+    if square:
+        along_x, along_y = chip + 1 - 2 * lax.rem(chip, 2), lax.rem(chip + 2, 4)
+        first = along_x + core * (along_y - along_x)
+        second = along_y + core * (along_x - along_y)
+        hops, sources = [first, second], [first, second, 3 - chip]
+    else:
+        hops = [lax.rem(chip + k, chips) for k in range(1, chips)]
+        sources = [lax.rem(chip + chips - k, chips) for k in range(1, chips)]
+
+    def copy_to(src, dst, sems, k, target):
+        return pltpu.make_async_remote_copy(
+            src_ref=src,
+            dst_ref=dst,
+            send_sem=sems.at[0, k],
+            recv_sem=sems.at[1, k],
+            device_id={"rep": target},
+            device_id_type=pl.DeviceIdType.MESH,
+        )
+
+    def block(k):
+        return out.at[2 * sources[k] + core]
+
+    own = [copy_to(source, out.at[me], far, k, 2 * hop + core) for k, hop in enumerate(hops)]
+    if square:
+        own.append(copy_to(block(0), block(0), far, 2, 2 * second + core))
+    crossing = [copy_to(block(k), block(k), near, k, partner) for k in range(chips - 1)]
+    crossing.append(copy_to(source, out.at[me], near, chips - 1, partner))
+    keep = pltpu.make_async_copy(source, out.at[me], local)
+
+    @pl.when(steps[0])
+    def _():
+        meet("rep", [2 * hop + core for hop in hops] + [partner])
+        for copy in own[: len(hops)]:
+            copy.start()
+        crossing[-1].start()
+        keep.start()
+
+    @pl.when(steps[1])
+    def _():
+        own[0].wait_recv()
+        if square:
+            own[2].start()
+        crossing[0].start()
+
+    @pl.when(steps[2])
+    def _():
+        for k in range(1, len(hops)):
+            own[k].wait_recv()
+            crossing[k].start()
+
+    @pl.when(steps[3])
+    def _():
+        if square:
+            own[2].wait_recv()
+            crossing[2].start()
+        for copy in crossing:
+            copy.wait()
+        for copy in own:
+            copy.wait_send()
+        keep.wait()
 
 
 def scan_back_kernel(
+    rep,
     channels,
     decay_step_ref,
     step_ref,
     input_ref,
     maps_ref,
     grad_ref,
-    rate2_ref,
+    decayed_ref,
     rate_ref,
+    beside_ref,
     grad_input_ref,
     grad_step_ref,
     grad_rate_ref,
     grad_maps_ref,
-    states_ref,
+    beside_out_ref,
+    carry_ref,
+    rates_ref,
     in_sum_ref,
     out_sum_ref,
+    both_sum_ref,
     wide_ref,
+    local,
+    far,
+    near,
 ):
     count, packs, _ = decay_step_ref.shape
-    at = pl.program_id(1)
-    valid = lax.broadcasted_iota(jnp.int32, (packs, LANES), 1) < channels - at * LANES
-    valid_row = valid[:1]
-    rate2 = [jnp.where(valid_row, rate2_ref[n : n + 1, :], 0.0) for n in range(STATE)]
-    rate = [jnp.where(valid_row, rate_ref[n : n + 1, :], 0.0) for n in range(STATE)]
-
-    @pl.when(at == 0)
+    at = (pl.program_id(0) * pl.num_programs(1) + pl.program_id(1)) * pl.num_programs(2)
+    at = at + pl.program_id(2)
+    last = pl.num_programs(0) * pl.num_programs(1) * pl.num_programs(2) - 1
+    steps = [at == step for step in (0, 9 * last // 16, 11 * last // 16, last)]
+    spread_beside(rep, steps, beside_ref, beside_out_ref, local, far, near)
+    tile, chunk = pl.program_id(1), pl.program_id(2)
+    start = (pl.num_programs(2) - 1 - chunk) * count
+    valid = lax.broadcasted_iota(jnp.int32, (packs, LANES), 1) < channels - tile * LANES
+
+    @pl.when(tile == 0)
     def _():
-        spread_maps(maps_ref, wide_ref)
-        in_sum_ref[...] = jnp.zeros_like(in_sum_ref)
-        out_sum_ref[...] = jnp.zeros_like(out_sum_ref)
-
-    def forward(i, states):
-        for u in range(2):
-            t = 2 * i + u
-            decay_step = jnp.where(valid, decay_step_ref[t], 0.0)
-            inputs = jnp.where(valid, input_ref[t], 0.0)
-            new_states = []
-            for n in range(STATE):
-                state = jnp.exp2(decay_step * rate2[n]) * states[n] + wide_ref[n, t] * inputs
-                states_ref[n, t] = state
-                new_states.append(state)
-            states = tuple(new_states)
-        return states
-
-    zero = jnp.zeros((packs, LANES), f32)
-    lax.fori_loop(0, count // 2, forward, (zero,) * STATE)
+        spread_maps(maps_ref, wide_ref, start)
+        zeros = jnp.zeros((STATE, count, packs, LANES), f32)
+        in_sum_ref[:, pl.ds(start, count)] = zeros
+        out_sum_ref[:, pl.ds(start, count)] = zeros
+        both_sum_ref[pl.ds(start, count)] = zeros[0]
+
+    @pl.when(chunk == 0)
+    def _():
+        carry_ref[...] = jnp.zeros_like(carry_ref)
+        for n in range(STATE):
+            rates_ref[n] = jnp.where(
+                valid, jnp.broadcast_to(rate_ref[n : n + 1, :], (packs, LANES)), 0.0
+            )
 
     def backward(back_t, carried):
         grad_states, grad_rates = carried
         t = count - 1 - back_t
+        at = start + t
         decay_step = jnp.where(valid, decay_step_ref[t], 0.0)
         step = jnp.where(valid, step_ref[t], 0.0)
         inputs = jnp.where(valid, input_ref[t], 0.0)
         grad = jnp.where(valid, grad_ref[t], 0.0)
-        grad_input, grad_step = zero, zero
+        both_sum_ref[at] += grad * inputs
+        grad_input = grad_step = jnp.zeros((packs, LANES), f32)
         new_states, new_rates = [], []
         for n in range(STATE):
-            state, in_map = states_ref[n, t], wide_ref[n, t]
-            grad_state = grad * wide_ref[STATE + n, t] + grad_states[n]
-            out_sum_ref[n, t] += grad * state
-            in_sum_ref[n, t] += grad_state * inputs
-            grad_input = grad_input + grad_state * in_map
-            through = grad_state * (state - in_map * inputs)
-            grad_step = grad_step + through * rate[n]
+            decayed, rate = decayed_ref[n, t], rates_ref[n]
+            grad_state = grad * wide_ref[STATE + n, at] + grad_states[n]
+            out_sum_ref[n, at] += grad * decayed
+            in_sum_ref[n, at] += grad_state * inputs
+            grad_input = grad_input + grad_state * wide_ref[n, at]
+            through = grad_state * decayed
+            grad_step = grad_step + through * rate
             new_rates.append(grad_rates[n] + through * step)
-            new_states.append(jnp.exp2(decay_step * rate2[n]) * grad_state)
+            new_states.append(jnp.exp2(decay_step * rate) * grad_state)
         grad_input_ref[t] = grad_input
         grad_step_ref[t] = grad_step
         return (tuple(new_states), tuple(new_rates))
 
-    _, grad_rates = lax.fori_loop(0, count, backward, ((zero,) * STATE, (zero,) * STATE))
+    carried = (
+        tuple(carry_ref[n] for n in range(STATE)),
+        tuple(carry_ref[STATE + n] for n in range(STATE)),
+    )
+    grad_states, grad_rates = lax.fori_loop(0, count, backward, carried)
     for n in range(STATE):
-        grad_rate_ref[n : n + 1, :] = jnp.sum(grad_rates[n], axis=0, keepdims=True)
-
-    @pl.when(at == pl.num_programs(1) - 1)
+        carry_ref[n] = grad_states[n]
+        carry_ref[STATE + n] = grad_rates[n]
+
+    @pl.when(chunk == pl.num_programs(2) - 1)
+    def _():
+        for n in range(STATE):
+            grad_rate_ref[n : n + 1, :] = jnp.sum(grad_rates[n], axis=0, keepdims=True)
+
+    @pl.when(tile == pl.num_programs(1) - 1)
     def _():
         column = lax.broadcasted_iota(jnp.int32, (LANES, LANES), 1)
-        total = jnp.zeros((count * packs, LANES), f32)
+        here = pl.ds(start, count)
+
+        def summed(value, place):
+            return jnp.dot(
+                value.reshape(count * packs, LANES).astype(bf16),
+                (column == place).astype(bf16),
+                preferred_element_type=f32,
+            )
+
+        total = summed(both_sum_ref[here], 2 * STATE)
         for n in range(STATE):
-            for sums, place in ((in_sum_ref, n), (out_sum_ref, STATE + n)):
-                total = total + jnp.dot(
-                    sums[n].reshape(count * packs, LANES).astype(bf16),
-                    (column == place).astype(bf16),
-                    preferred_element_type=f32,
-                )
-        grad_maps_ref[...] = total.reshape(count, packs, LANES)
-
-
-def scan_backward(decay_step, step, inputs, maps, grad, rate2, rate):
+            total = total + summed(in_sum_ref[n, here], n)
+            total = total + summed(out_sum_ref[n, here], STATE + n)
+        grad_maps_ref[here] = total.reshape(count, packs, LANES)
+
+
+def scan_backward(decay_step, step, inputs, maps, grad, decayed, rate, rep, collective_id, beside):
     count, packs, channels = inputs.shape
-    groups = packs // PACKS
-    wide = pl.BlockSpec((count, PACKS, LANES), lambda g, i: (0, g, i))
-    row = pl.BlockSpec((STATE, LANES), lambda g, i: (0, i))
-    scratch = pltpu.VMEM((STATE, count, PACKS, LANES), f32)
-    grad_inputs, grad_step, grad_rate, grad_maps = pl.pallas_call(
-        functools.partial(scan_back_kernel, channels),
-        grid=(groups, pl.cdiv(channels, LANES)),
+    groups, chunks = packs // PACKS, 4
+    part = count // chunks
+    wide = pl.BlockSpec((part, PACKS, LANES), lambda g, i, c: (chunks - 1 - c, g, i))
+    row = pl.BlockSpec((STATE, LANES), lambda g, i, c: (0, i))
+    sums = pltpu.VMEM((STATE, count, PACKS, LANES), f32)
+    grad_inputs, grad_step, grad_rate, grad_maps, all_beside = pl.pallas_call(
+        functools.partial(scan_back_kernel, rep, channels),
+        grid=(groups, pl.cdiv(channels, LANES), chunks),
         in_specs=[
             wide,
             wide,
             wide,
-            pl.BlockSpec((count, PACKS, 2 * STATE), lambda g, i: (0, g, 0)),
+            pl.BlockSpec((part, PACKS, 2 * STATE), lambda g, i, c: (chunks - 1 - c, g, 0)),
             wide,
+            pl.BlockSpec(
+                (STATE, part, PACKS, LANES), lambda g, i, c: (0, chunks - 1 - c, g, i)
+            ),
             row,
-            row,
+            hbm_spec(),
         ],
         out_specs=[
             wide,
             wide,
-            pl.BlockSpec((STATE, LANES), lambda g, i: (g, i)),
-            pl.BlockSpec((count, PACKS, LANES), lambda g, i: (0, g, 0)),
+            pl.BlockSpec((STATE, LANES), lambda g, i, c: (g, i)),
+            pl.BlockSpec((count, PACKS, LANES), lambda g, i, c: (0, g, 0)),
+            hbm_spec(),
         ],
         out_shape=[
             jax.ShapeDtypeStruct(inputs.shape, f32),
             jax.ShapeDtypeStruct(inputs.shape, f32),
             jax.ShapeDtypeStruct((groups * STATE, channels), f32),
             jax.ShapeDtypeStruct((count, packs, LANES), f32),
+            jax.ShapeDtypeStruct((rep,) + beside.shape, beside.dtype),
         ],
         scratch_shapes=[
-            scratch,
-            scratch,
-            scratch,
+            pltpu.VMEM((2 * STATE, PACKS, LANES), f32),
+            pltpu.VMEM((STATE, PACKS, LANES), f32),
+            sums,
+            sums,
+            pltpu.VMEM((count, PACKS, LANES), f32),
             pltpu.VMEM((2 * STATE, count, PACKS, LANES), f32),
+            pltpu.SemaphoreType.DMA,
+            pltpu.SemaphoreType.DMA((2, rep // 2)),
+            pltpu.SemaphoreType.DMA((2, rep // 2)),
         ],
-        compiler_params=pltpu.CompilerParams(vmem_limit_bytes=58 * 1024 * 1024),
+        compiler_params=pltpu.CompilerParams(
+            collective_id=collective_id,
+            has_side_effects=True,
+            vmem_limit_bytes=52 * 1024 * 1024,
+        ),
         cost_estimate=SMALL_COST,
-    )(decay_step, step, inputs, maps, grad, rate2, rate)
+    )(decay_step, step, inputs, maps, grad, decayed, rate, beside)
     grad_rate = jnp.sum(grad_rate.reshape(groups, STATE, channels), axis=0)
-    return grad_inputs, grad_step, grad_rate, grad_maps.reshape(count * packs, LANES)
+    in_maps, both = grad_maps[:, :, :STATE], grad_maps[:, :, 2 * STATE : 2 * STATE + 1]
+    out_maps = grad_maps[:, :, STATE : 2 * STATE] + maps[:, :, :STATE] * both
+    grad_maps = jnp.concatenate([in_maps, out_maps], axis=2).reshape(count * packs, 2 * STATE)
+    return grad_inputs, grad_step, grad_rate, grad_maps, all_beside
 
 
 def split_heads(qkv_low):
@@ -714,6 +1027,10 @@
 
 def tied(value, *others):
     return lax.optimization_barrier((value,) + others)[0]
+
+
+def by_row(value):
+    return with_layout_constraint(value, Layout(major_to_minor=(0, 1)))
 
 
 def silu_and_slope(value):
@@ -814,7 +1131,7 @@
     w_gate, w_up, part_mout, part_mix, part_down, received = lax.optimization_barrier(
         (w_gate, w_up, part_mout, part_mix, part_down, received)
     )
-    full_mout, half_mix = line_gather(part_mout), line_gather(part_mix)
+    mout_mix = line_gather(jnp.concatenate([part_mout, part_mix], axis=0))
     part_gate_up = by_rows(
         functools.partial(part_gate_up_kernel, rep, fsdp), (w_gate, w_up), 2 * ff_part
     )
@@ -850,7 +1167,6 @@
     part_x_proj, part_dt_proj = my_part(x_proj, 0), my_part(dt_proj, 1)
     part_dt_bias, part_skip = my_part(dt_bias, 0), my_part(d_skip, 0)
     rate = -jnp.exp(my_part(a_log, 1))
-    rate2 = rate * LOG2_E
     conv_sum = xs * conv_w[CONV - 1] + conv_b
     for k in range(1, CONV):
         earlier = jnp.where(in_seq_all >= k, shift_down(xs, k * rep), 0.0)
@@ -866,20 +1182,25 @@
     maps = proj[:, :, DT_RANK:]
     dt_sum = dot(dt_in, part_dt_proj, high) + part_dt_bias
     step = jax.nn.softplus(dt_sum)
-    decay_step = jnp.where(in_seq_all == 0.0, 1e30, step)
+    decay_step = jnp.where(in_seq_all == 0.0, 1e30, step * LOG2_E)
     inputs = step * act
     cube = (count, rep, channels)
-    scanned = scan_forward(decay_step.reshape(cube), inputs.reshape(cube), maps, rate2)
+    scanned, decayed, mout_mix = scan_forward(
+        decay_step.reshape(cube), inputs.reshape(cube), maps, rate, mout_mix
+    )
     scanned = scanned.reshape(group, channels)
+    mout_mix = mout_mix.reshape(fsdp, -1, width)
+    full_mout = mout_mix[:, : part_mout.shape[0]].reshape(-1, width)
+    half_mix = mout_mix[:, part_mout.shape[0] :]
     silu_z, z_slope = silu_and_slope(gate_z)
     before_gate = scanned + part_skip * act
     mixer_low = swapped((before_gate * silu_z).astype(bf16).reshape(cube))
-    ssm_part = dot(mixer_low, full_mout).astype(bf16).reshape(rep, count, width)
+    ssm_part = by_row(dot(mixer_low, full_mout).astype(bf16)).reshape(rep, count, width)
     (ssm_out,) = rep_exchange(rep, 3, sums=(ssm_part,))
 
     attended_values, log_total = attention_forward(qkv_low, allowed)
     half_mix, qkv_low = lax.optimization_barrier((half_mix, qkv_low))
-    full_mix = pair_gather(9, half_mix.reshape(fsdp, half, width)).reshape(width, width)
+    full_mix = pair_gather(9, half_mix).reshape(width, width)
     mixed, mix_pull = jax.vjp(mix_branches, attended_values, ssm_out, norm_attn, norm_ssm)
     mixed_low = mixed.astype(bf16)
     middle = hidden_in + dot(mixed_low, full_mix)
@@ -892,14 +1213,18 @@
     hidden_low = hidden.astype(bf16)
     grad_hidden = dot_right_t(cot_all, full_down)
     grad_gate_up = jnp.concatenate(swiglu_pull(grad_hidden), axis=1).astype(bf16)
-    ffn_sent = dot_right_t(grad_gate_up, full_gate_up).astype(bf16).reshape(rep, count, width)
-    down_sent = dot(hidden_low, full_down).astype(bf16).reshape(rep, count, width)
-    grad_ffn, down_out = rep_exchange(rep, 5, sums=(ffn_sent, down_sent))
+    part_gate_up = dot_left_t(ffn_all, grad_gate_up).astype(bf16)
+    own_gate_up = line_scatter(part_gate_up)
+    grad_gate_up = tied(grad_gate_up, part_gate_up)
+    ffn_sent = by_row(dot_right_t(grad_gate_up, full_gate_up).astype(bf16))
+    part_down = dot_left_t(hidden_low, cot_all).astype(bf16)
+    own_down = line_scatter(part_down)
+    down_sent = by_row(dot(tied(hidden_low, part_down), full_down).astype(bf16))
+    blocks = (rep, count, width)
+    grad_ffn, down_out = rep_exchange(
+        rep, 5, sums=(ffn_sent.reshape(blocks), down_sent.reshape(blocks))
+    )
     result = middle + down_out
-    part_gate_up = dot_left_t(ffn_all, grad_gate_up).astype(bf16)
-    part_down = dot_left_t(hidden_low, cot_all).astype(bf16)
-    grad_ffn = tied(grad_ffn, part_gate_up, part_down)
-    own_gate_up, own_down = line_scatter(part_gate_up), line_scatter(part_down)
 
     grad_middle_norm, grad_norm_ffn = ffn_pull(grad_ffn)
     grad_middle = cot_rows + grad_middle_norm
@@ -913,7 +1238,7 @@
         rep, 6, gathers=(grad_ssm.astype(bf16),), trades=(middle_sent, qkv_grad)
     )
     qkv_cols = qkv_cols.reshape(group, qkv_part)
-    ssm_all = ssm_all.reshape(group, width)
+    ssm_all = tied(ssm_all, own_gate_up).reshape(group, width)
     grad_mixer = dot_right_t(ssm_all, full_mout).reshape(rep, count, channels)
     grad_mixer = swapped(grad_mixer)
     part_mout = dot_left_t(mixer_low, ssm_all).astype(bf16)
@@ -924,17 +1249,20 @@
     spare = early_width - qkv_part - channels
     early_grad = jnp.concatenate([qkv_cols, jnp.zeros((group, spare), bf16), grad_z], axis=1)
     part_early = dot_left_t(normed_all, early_grad).astype(bf16)
-    grad_mixer = tied(grad_mixer, part_mout, part_mix, part_early)
+    grad_mixer = tied(grad_mixer, part_mout, part_mix, part_early, own_down)
     own_mout, own_mix = line_scatter(part_mout), line_scatter(part_mix)
     own_early = line_scatter(part_early)
     grad_before = grad_mixer * silu_z
     grad_skip = jnp.sum(grad_before * act, axis=0)
-    grad_inputs, grad_step, grad_rate, grad_maps = scan_backward(
+    grad_inputs, grad_step, grad_rate, grad_maps, all_gate_up = scan_backward(
         *(item.reshape(cube) for item in (decay_step, step, inputs)),
         maps,
         grad_before.reshape(cube),
-        rate2,
+        decayed,
         rate,
+        rep,
+        7,
+        own_gate_up,
     )
     grad_inputs = grad_inputs.reshape(group, channels)
     grad_step = grad_step.reshape(group, channels)
@@ -944,12 +1272,12 @@
     grad_dt_bias = jnp.sum(grad_dt, axis=0)
     grad_dt_proj = dot_left_t(dt_in, grad_dt)
     proj_sent = jnp.concatenate(
-        [dot_right_t(grad_dt, part_dt_proj), grad_maps[:, : 2 * STATE]], axis=1
+        [dot_right_t(grad_dt, part_dt_proj), grad_maps], axis=1
     )
     proj_sent = proj_sent.reshape(count, rep, -1).transpose(1, 0, 2)
-    (grad_proj,) = rep_exchange(rep, 7, alls=(proj_sent,))
-    grad_proj = swapped(grad_proj)
-    grad_x_proj = dot_left_t(act, grad_proj)
+    (grad_proj,) = rep_exchange(rep, 11, alls=(proj_sent,))
+    grad_proj = swapped(tied(grad_proj, own_mout, own_mix))
+    grad_x_proj = dot_left_t(grad_proj, act)
     grad_act = grad_before * part_skip + grad_inputs * step + dot_right_t(grad_proj, part_x_proj)
     grad_conv = grad_act * act_slope
     grad_conv_b = jnp.sum(grad_conv, axis=0)
@@ -961,15 +1289,16 @@
         grad_xs = grad_xs + shift_up(reached, k * rep) * conv_w[CONV - 1 - k]
     small = jnp.concatenate(
         [jnp.stack(grad_conv_w), grad_conv_b[None], grad_dt_bias[None], grad_skip[None]]
-        + [grad_a_log, grad_dt_proj],
+        + [grad_a_log, grad_dt_proj, grad_x_proj],
         axis=0,
     )
-    small = jnp.pad(small, ((0, up16(small.shape[0]) - small.shape[0]), (0, 0))).astype(bf16)
+    n_small = fsdp * up16(-(-small.shape[0] // fsdp))
+    small = jnp.pad(small, ((0, n_small - small.shape[0]), (0, 0))).astype(bf16)
     grad_xs = swapped(grad_xs.astype(bf16).reshape(cube))
     gap = jnp.zeros((group, gate_at - channels - qkv_part), bf16)
     end = jnp.zeros((group, in_width - gate_at - channels), bf16)
     in_grad = jnp.concatenate([grad_xs, qkv_cols, gap, grad_z, end], axis=1)
-    normed_part = dot_right_t(in_grad, full_in).astype(bf16).reshape(rep, count, width)
+    normed_part = by_row(dot_right_t(in_grad, full_in).astype(bf16)).reshape(blocks)
     own_late = line_scatter(dot_left_t(normed_all, grad_xs).astype(bf16))
     (grad_normed,) = rep_exchange(rep, 8, sums=(normed_part,))
     grad_hidden_norm, grad_norm_in = norm_in_pull(grad_normed)
@@ -980,25 +1309,27 @@
 
     gains = jnp.stack([grad_norm_in, grad_norm_attn, grad_norm_ssm, grad_norm_ffn])
     gains = jnp.concatenate([gains, jnp.zeros((4, width), f32)], axis=0)
-    gains, small, x_small, mixed_out, grad_tokens = line_exchange(
+    (
+        all_mout,
+        all_mix,
+        all_early,
+        all_late,
+        all_down,
+        small,
+        gains,
+        mixed_out,
+        grad_tokens,
+    ) = last_exchange(
+        rep,
         fsdp,
         10,
-        gathers=(gains, small, grad_x_proj.astype(bf16)),
-        trades=(given_back(result), given_back(grad_hidden_in)),
-    )
-    gains, small, x_small = (
-        jnp.sum(item.astype(f32), axis=0) for item in (gains, small, x_small)
-    )
-
-    own_gate_up = tied(own_gate_up, mixed_out)
-    all_down, all_gate_up, all_mout, all_mix, all_early = rep_exchange(
-        rep, 11, gathers=(own_down, own_gate_up, own_mout, own_mix, own_early)
-    )
-    own_late = tied(own_late, all_down)
-    all_late, small, x_small, gains = rep_exchange(
-        rep, 12, gathers=(own_late, small, x_small, gains)
-    )
-    gains = jnp.sum(gains, axis=0)
+        (own_mout, own_mix, own_early, own_late, own_down),
+        small.reshape(fsdp, -1, channels),
+        gains,
+        (given_back(result), given_back(grad_hidden_in)),
+    )
+    gains, small = jnp.sum(gains, axis=0), small.reshape(rep, n_small, channels)
+    all_gate_up = tied(all_gate_up, all_late)
     sum_gate, sum_up = join_columns(
         rep,
         (all_gate_up,),
@@ -1015,12 +1346,12 @@
             ((2, 0, width // rep, 0, 1),),
         ),
     )
-    (sum_down,) = join_rows(rep, (all_down,), (w_down.shape[0],))
-    (sum_mout,) = join_rows(rep, (all_mout,), (w_mamba_out.shape[0],))
-
-    (sum_x_proj,) = join_rows(rep, (x_small,), (x_proj.shape[0],), fsdp)
+    sum_down = join_rows(rep, all_down, w_down.shape[0], width, flip=True).T
+    sum_mout = join_rows(rep, all_mout, w_mamba_out.shape[0], width)
+
     (small,) = join_columns(rep, (small,), (INNER,), (((0, 0, piece, 0, fsdp),),))
     ends = [CONV, CONV + 1, CONV + 2, CONV + 3, CONV + 3 + STATE, CONV + 3 + STATE + DT_RANK]
+    ends.append(ends[-1] + x_proj.shape[1])
     return (
         mixed_out.reshape(count, width),
         grad_tokens.reshape(count, width),
@@ -1029,7 +1360,7 @@
         sum_mamba_in,
         small[: ends[0]],
         small[ends[0]],
-        sum_x_proj,
+        small[ends[5] : ends[6]].T,
         small[ends[4] : ends[5]],
         small[ends[1]],
         small[ends[3] : ends[4]],

time: 979 us -> 837 us (0.85)
  Pallas kernels: 595 us -> 506 us
  local copies, waits for them, and re-layouts: 154 us -> 121 us
  waiting for transfers between devices: 43.9 us -> 19.5 us
    pallas_call x10 -> x8, Pallas kernels: 367 us -> 226 us  [rep_exchange(): pl.pallas_call(functools.partial(rep_kernel, rep, counts, square), out_sh...]
    pallas_call x7 -> x6, Pallas kernels: 191 us -> 243 us  [the longest x1 104 us: last_exchange(): pl.pallas_call(functools.partial(last_kernel, rep, fsdp, rep == 8, n_gath...]
    unnamed x306 -> x327, local copies, waits for them, and re-layouts: 81.6 us -> 53.4 us
    convert_element_type x5 -> x0, local copies, waits for them, and re-layouts: 23.1 us -> none  [the longest x1 5.85 us: per_device(): dot(hidden_low, full_down).astype(bf16).reshape(rep, count, width)]
    all_gather x5 -> x4, waiting for transfers between devices: 41.7 us -> 18.8 us  [line_gather(): return lax.all_gather(value, 'fsdp', axis=0, tiled=True)]
  transfers between devices with their start and end apart: 11 -> 10, of which waited for: 2 -> 2; matrix products, arithmetic and copies ran while one was open for 23% -> 26% of each run, Pallas kernels for 54% -> 44%
where the time goes in v2:
time: 837 us; the launch traced here: 831 us
  Pallas kernels  506 us (60%)
  matrix products  124 us (15%)
  local copies, waits for them, and re-layouts  121 us (14%)
  other arithmetic  43.9 us (5%)
  waiting for transfers between devices  19.5 us (2%)
  between operations  16.5 us (2%)
    pallas_call x8, Pallas kernels, rep_exchange(): pl.pallas_call(functools.partial(rep_kernel, rep, counts, square), out_sh...  226 us
    pallas_call x1, Pallas kernels, last_exchange(): pl.pallas_call(functools.partial(last_kernel, rep, fsdp, rep == 8, n_gath...  104 us
    pallas_call x1, Pallas kernels, scan_backward(): pl.pallas_call(functools.partial(scan_back_kernel, rep, channels), grid=(...  59.3 us
    unnamed x327, local copies, waits for them, and re-layouts  53.4 us
    dot_general x7, matrix products, dot_right_t(): lax.dot_general(left, right, (((1,), (1,)), ((), ())), preferred_element_...  42 us
    pallas_call x1, Pallas kernels, line_exchange(): pl.pallas_call(functools.partial(line_kernel, count, (len(gathers), len(a...  41.3 us
    dot_general x10, matrix products, dot_left_t(): lax.dot_general(left, right, (((0,), (0,)), ((), ())), preferred_element_...  40 us
    dot_general x9, matrix products, dot(): return jnp.dot(left, right, precision=precision, preferred_element_type=f32)  36.2 us
  transfers between devices with their start and end apart: 10, of which 2 were waited for; matrix products, arithmetic and copies ran while one was open for 26% of the time, Pallas kernels for 44%

profile of v2, /device:TPU:0, one launch (start us, length us, event | category | flops | bytes accessed | tf_op | source)
XLA Modules:
  0.0 831.3 jit_solution(15577824314434048442)
XLA Ops:
  22.5 41.3 %shard_map.366 = (bf16[4,32,1600]{2,1,0:T(8,128)(2,1)}, bf16[4,32,1600]{2,1,0:T(8,128)(2,1)}) custom-call(bf16[4,32,1600]{2,1,0:T(8,128)(2,1)} %bitcast.312, bf16[4,32,1600]{2,1,0:T(8,128)(2,1)} %bitcast.313), custom_call_target="tpu_custom_call" | custom-call | bytes 10000 | tf_op jit(solution)/shard_map/pallas_call | solution.py:337
  76.8 32.6 %shard_map.367 = (bf16[8,128,1664]{2,1,0:T(8,128)(2,1)S(1)}, bf16[8,128,1600]{2,1,0:T(8,128)(2,1)S(1)}) custom-call(bf16[128,1664]{1,0:T(8,128)(2,1)S(1)} %pad_maximum_fusion.3.refs_0_, bf16[128,1600]{1,0:T(8,128)(2,1)S(1)} %copy.280.refs_1_), custom_call_target="tpu_custom_call" | custom-call | bytes 10000 | tf_op jit(solution)/shard_map/pallas_call | solution.py:270
  126.5 9.2 %fusion = f32[1024,1280]{1,0:T(8,128)S(1)} fusion(bf16[1600,1280]{1,0:T(8,128)(2,1)} %all-gather.5.cloned.1.call-done, bf16[128,8,1600]{2,0,1:T(8,128)(2,1)} %get-tuple-element.260), kind=kOutput, calls=%fused_computation.7 | convolution fusion | flops 4194304000 | bytes 12615680 | tf_op jit(solution)/shard_map/dot_general | solution.py:29
  142.7 27.3 %shard_map.368 = (f32[8,128,132]{2,1,0:T(8,128)S(1)}, bf16[8,128,280]{2,1,0:T(8,128)(2,1)S(1)}) custom-call(f32[8,128,132]{2,1,0:T(8,128)S(1)} %bitcast.264, bf16[8,128,280]{2,1,0:T(8,128)(2,1)S(1)} %bitcast.269), custom_call_target="tpu_custom_call" | custom-call | bytes 10000 | tf_op jit(solution)/shard_map/pallas_call | solution.py:270
  177.7 18.5 %all-gather.7.cloned.1.call-done._handed_ref = bf16[1248,1600]{1,0:T(8,128)(2,1)} async-done(((bf16[312,1600]{1,0:T(8,128)(2,1)}), bf16[1248,1600]{1,0:T(8,128)(2,1)}) %all-gather.7.cloned.1.call-update) | async-done | bytes 3993616 | tf_op jit(solution)/shard_map/all_gather | solution.py:1101
  196.2 28.1 %shard_map.369 = (f32[128,8,448]{2,1,0:T(8,128)S(1)}, f32[16,128,8,512]{3,2,1,0:T(8,128)}, bf16[1248,1600]{1,0:T(8,128)(2,1)}) custom-call(f32[128,8,448]{2,1,0:T(8,128)S(1)} %get-tuple-element.263.decay_step_ref, f32[128,8,448]{2,1,0:T(8,128)} %get-tuple-element.262.input_ref, f32[128,8,32]{2,1,0:T(8,128)S(1)} %copy.291.maps_ref, ...), custom_call_target="tpu_custom_call", output_to_operand_aliasing={{2}: (4, {})} | custom-call | bytes 10000 | tf_op jit(solution)/shard_map/pallas_call | solution.py:695
  233.3 7.0 shard_map.371
  252.0 22.3 %shard_map.370 = f32[128,1600]{1,0:T(8,128)S(1)} custom-call(bf16[8,128,1600]{2,1,0:T(8,128)(2,1)S(1)} %bitcast.266), custom_call_target="tpu_custom_call" | custom-call | bytes 10000 | tf_op jit(solution)/shard_map/pallas_call | solution.py:270
  286.9 32.3 %shard_map.372 = (bf16[8,128,1600]{2,1,0:T(8,128)(2,1)S(1)}, bf16[8,128,1600]{2,1,0:T(8,128)(2,1)S(1)}) custom-call(bf16[128,1600]{1,0:T(8,128)(2,1)S(1)} %multiply_convert_fusion.4.refs_0_, bf16[128,1600]{1,0:T(8,128)(2,1)S(1)} %multiply_convert_fusion.5.refs_1_), custom_call_target="tpu_custom_call" | custom-call | bytes 10000 | tf_op jit(solution)/shard_map/pallas_call | solution.py:270
  322.7 10.0 %fusion.107 = f32[1024,1408]{0,1:T(8,128)} fusion(bf16[1024,1600]{1,0:T(8,128)(2,1)} %bitcast.284, bf16[1600,1408]{1,0:T(8,128)(2,1)} %all-gather.11.cloned.1.call-done), kind=kOutput, calls=%fused_computation.292 | convolution fusion | flops 4613734400 | bytes 13549568 | tf_op jit(solution)/shard_map/dot_general | solution.py:29
  333.0 9.4 %fusion.6 = (bf16[1024,704]{0,1:T(8,128)(2,1)S(1)}, bf16[1024,704]{0,1:T(8,128)(2,1)S(1)}, bf16[1024,704]{0,1:T(8,128)(2,1)}) fusion(f32[1024,1408]{0,1:T(8,128)} %fusion.107, bf16[1024,1600]{1,0:T(8,128)(2,1)} %bitcast.282, bf16[704,1600]{1,0:T(8,128)(2,1)} %all-gather.9.cloned.1.call-done), kind=kOutput, calls=%fused_computation.17 | convolution fusion | flops 2318401536 | bytes 15622144 | tf_op jit(solution)/shard_map/dot_general | solution.py:33
  344.0 7.9 convolution_convert_fusion
  360.3 6.6 convolution_convert_fusion.6
  369.2 5.3 convolution_convert_fusion.1
  374.5 6.1 convolution_convert_fusion.2
  380.7 36.1 %shard_map.374 = (f32[128,1600]{1,0:T(8,128)S(1)}, f32[128,1600]{1,0:T(8,128)S(1)}) custom-call(bf16[8,128,1600]{2,1,0:T(8,128)(2,1)S(1)} %bitcast.268, bf16[8,128,1600]{2,1,0:T(8,128)(2,1)S(1)} %bitcast.267), custom_call_target="tpu_custom_call" | custom-call | bytes 10000 | tf_op jit(solution)/shard_map/pallas_call | solution.py:270
  424.1 5.5 multiply_reduce_fusion.7
  443.6 33.6 %shard_map.375 = (bf16[8,128,1600]{2,1,0:T(8,128)(2,1)S(1)}, bf16[8,128,200]{2,1,0:T(8,128)(2,1)S(1)}, bf16[8,128,280]{2,1,0:T(8,128)(2,1)S(1)}) custom-call(bf16[128,1600]{1,0:T(8,128)(2,1)S(1)} %copy-done.17, bf16[8,128,200]{2,1,0:T(8,128)(2,1)S(1)} %bitcast.271, bf16[8,128,280]{2,1,0:T(8,128)(2,1)S(1)} %bitcast.270), custom_call_target="tpu_custom_call" | custom-call | bytes 10000 | tf_op jit(solution)/shard_map/pallas_call | solution.py:270
  484.0 5.4 fusion.3
  490.6 5.6 convolution_bitcast_fusion.2
  499.2 5.2 fusion.34
  507.9 6.4 convolution_convert_fusion.5
  524.0 59.3 %shard_map.376 = (f32[128,8,448]{2,1,0:T(8,128)}, f32[128,8,448]{2,1,0:T(8,128)}, f32[16,448]{1,0:T(8,128)S(1)}, f32[128,8,128]{2,1,0:T(8,128)S(1)}, bf16[8,400,1408]{2,1,0:T(8,128)(2,1)}) custom-call(f32[128,8,448]{2,1,0:T(8,128)} %copy-done.2, f32[128,8,448]{2,1,0:T(8,128)} %get-tuple-element.261.step_ref, f32[128,8,448]{2,1,0:T(8,128)} %get-tuple-element.262.input_ref, ...), custom_call_target="tpu_custom_call" | custom-call | bytes 10000 | tf_op jit(solution)/shard_map/pallas_call | solution.py:909
  592.9 19.8 %shard_map.377 = f32[8,128,132]{2,1,0:T(8,128)S(1)} custom-call(f32[8,128,132]{2,1,0:T(8,128)S(1)} %maximum_bitcast_fusion.refs_0_), custom_call_target="tpu_custom_call" | custom-call | bytes 10000 | tf_op jit(solution)/shard_map/pallas_call | solution.py:270
  613.8 9.3 %multiply_reduce_fusion = (bf16[448]{0:T(512)(128)(2,1)S(1)}, bf16[448]{0:T(512)(128)(2,1)S(1)}, bf16[448]{0:T(512)(128)(2,1)S(1)}, bf16[448]{0:T(512)(128)(2,1)...) fusion(f32[1024,448]{1,0:T(8,128)} %bitcast.289, ...), kind=kOutput, calls=%fused_computation.36 | convolution fusion | flops 140181888 | bytes 24532992 | tf_op jit(solution)/shard_map/dot_general | solution.py:33
  627.3 5.1 bitcast_convert_fusion
  635.1 5.5 convolution_convert_fusion.4
  640.7 22.1 %shard_map.378 = f32[128,1600]{1,0:T(8,128)S(1)} custom-call(bf16[8,128,1600]{2,1,0:T(8,128)(2,1)S(1)} %bitcast.265), custom_call_target="tpu_custom_call" | custom-call | bytes 10000 | tf_op jit(solution)/shard_map/pallas_call | solution.py:270
  671.7 103.6 %shard_map.379 = (bf16[8,112,1600]{2,1,0:T(8,128)(2,1)S(1)}, bf16[8,400,200]{2,1,0:T(8,128)(2,1)S(1)}, bf16[8,400,768]{2,1,0:T(8,128)(2,1)}, bf16[8,400,448]{2,1...) custom-call(bf16[112,1600]{1,0:T(8,128)(2,1)S(1)} %copy-done.31, ...), custom_call_target="tpu_custom_call" | custom-call | bytes 10000 | tf_op jit(solution)/shard_map/pallas_call | solution.py:472
  786.3 11.7 %shard_map.383 = (f32[400,5504]{1,0:T(8,128)}, f32[400,5504]{1,0:T(8,128)}) custom-call(bf16[8,400,1408]{2,1,0:T(8,128)(2,1)} %get-tuple-element.116.refs_0_), custom_call_target="tpu_custom_call" | custom-call | bytes 10000 | tf_op jit(solution)/shard_map/pallas_call | solution.py:622
  798.0 6.7 shard_map.384
  814.5 9.7 %shard_map.380 = (f32[400,6400]{1,0:T(8,128)}, f32[400,2240]{1,0:T(8,128)}, f32[400,1600]{1,0:T(8,128)}) custom-call(bf16[8,400,448]{2,1,0:T(8,128)(2,1)S(1)} %copy-done.14, bf16[8,400,768]{2,1,0:T(8,128)(2,1)} %get-tuple-element.108.refs_1_, bf16[8,400,200]{2,1,0:T(8,128)(2,1)S(1)} %copy-done.19), custom_call_target="tpu_custom_call" | custom-call | bytes 10000 | tf_op jit(solution)/shard_map/pallas_call | solution.py:622
  (510 shorter events, 200.2 us)
Async XLA Ops:
  7.2 119.3 %all-gather.5.cloned.1.call-start = ((), (), s32[]{:S(2)}) async-start(), calls=%async_computation.6 | async-start | bytes 5120000 | tf_op jit(solution)/shard_map/all_gather | solution.py:1101
  15.5 180.7 %all-gather.7.cloned.1.call-start = ((), (), s32[]{:S(2)}) async-start(), calls=%async_computation.7 | async-start | bytes 5191680 | tf_op jit(solution)/shard_map/all_gather | solution.py:1101
  18.4 45.4 %copy-start.74 = (bf16[400,1600]{1,0:T(8,128)(2,1)S(1)}, bf16[400,1600]{1,0:T(8,128)(2,1)}, u32[]{:S(2)}) copy-start(bf16[400,1600]{1,0:T(8,128)(2,1)} %param.39) | copy-start | bytes 3840004
  65.0 257.8 %all-gather.11.cloned.1.call-start = ((), (), s32[]{:S(2)}) async-start(), calls=%async_computation.9 | async-start | bytes 5632000 | tf_op jit(solution)/shard_map/all_gather | solution.py:1101
  73.2 259.9 %all-gather.9.cloned.1.call-start = ((), (), s32[]{:S(2)}) async-start(), calls=%async_computation.8 | async-start | bytes 2928640 | tf_op jit(solution)/shard_map/all_gather | solution.py:1101
  73.7 410.2 %reduce-scatter.7.cloned.1.call-start = ((), (), s32[]{:S(2)}) async-start(), calls=%async_computation.10 | async-start | bytes 5632000 | tf_op jit(solution)/shard_map/reduce_scatter | solution.py:1104
  121.7 49.5 %copy-start.76 = (f32[100,100]{1,0:T(8,128)}, f32[100,100]{1,0:T(8,128)S(1)}, u32[]{:S(2)}) copy-start(f32[100,100]{1,0:T(8,128)S(1)} %get-tuple-element.274) | copy-start | bytes 120004
  121.7 49.5 %copy-start.78 = (f32[100,100]{1,0:T(8,128)}, f32[100,100]{1,0:T(8,128)S(1)}, u32[]{:S(2)}) copy-start(f32[100,100]{1,0:T(8,128)S(1)} %get-tuple-element.275) | copy-start | bytes 120004
  140.8 32.0 %copy-start.40 = (f32[1024,448]{1,0:T(8,128)}, f32[1024,448]{1,0:T(8,128)S(1)}, u32[]{:S(2)}) copy-start(f32[1024,448]{1,0:T(8,128)S(1)} %multiply_add_fusion) | copy-start | bytes 5505028
  177.7 46.6 %copy-start.2 = (f32[128,8,448]{2,1,0:T(8,128)}, f32[128,8,448]{2,1,0:T(8,128)S(1)}, u32[]{:S(2)}) copy-start(f32[128,8,448]{2,1,0:T(8,128)S(1)} %get-tuple-element.263.decay_step_ref) | copy-start | bytes 5505028
  252.0 22.4 %copy-start.66 = (bf16[128,1600]{0,1:T(8,128)(2,1)S(1)}, bf16[128,1600]{0,1:T(8,128)(2,1)}, u32[]{:S(2)}) copy-start(bf16[128,1600]{0,1:T(8,128)(2,1)} %slice.200) | copy-start | bytes 1228804
  252.0 22.4 %copy-start.75 = (bf16[128,320]{0,1:T(8,128)(2,1)S(1)}, bf16[128,320]{0,1:T(8,128)(2,1)}, u32[]{:S(2)}) copy-start(bf16[128,320]{0,1:T(8,128)(2,1)} %get-tuple-element.282) | copy-start | bytes 245764
  252.0 22.3 %copy-start.84 = (pred[128,128]{0,1:T(8,128)(4,1)S(1)}, pred[128,128]{0,1:T(8,128)(4,1)}, u32[]{:S(2)}) copy-start(pred[128,128]{0,1:T(8,128)(4,1)} %fusion.70) | copy-start | bytes 49156
  351.9 168.0 %reduce-scatter.15.cloned.1.call-start = ((), (), s32[]{:S(2)}) async-start(), calls=%async_computation.14 | async-start | bytes 2928640 | tf_op jit(solution)/shard_map/reduce_scatter | solution.py:1104
  380.6 37.0 %copy-start.47 = (f32[128,1600]{1,0:T(8,128)S(1)}, f32[128,1600]{1,0:T(8,128)}, u32[]{:S(2)}) copy-start(f32[128,1600]{1,0:T(8,128)} %copy-done.46) | copy-start | bytes 2457604
  380.6 37.0 %copy-start.133 = (f32[128]{0:T(128)S(1)}, f32[128]{0:T(128)}, u32[]{:S(2)}) copy-start(f32[128]{0:T(128)} %copy-done.132) | copy-start | bytes 1540
  380.6 37.8 %copy-start.150 = (f32[128]{0:T(128)S(1)}, f32[128]{0:T(128)}, u32[]{:S(2)}) copy-start(f32[128]{0:T(128)} %copy-done.149) | copy-start | bytes 1540
  419.0 194.7 %reduce-scatter.11.cloned.1.call-start = ((), (), s32[]{:S(2)}) async-start(), calls=%async_computation.12 | async-start | bytes 1024000 | tf_op jit(solution)/shard_map/reduce_scatter | solution.py:1104
  483.9 129.9 %reduce-scatter.9.cloned.1.call-start = ((), (), s32[]{:S(2)}) async-start(), calls=%async_computation.11 | async-start | bytes 1863680 | tf_op jit(solution)/shard_map/reduce_scatter | solution.py:1104
  489.4 178.1 %reduce-scatter.13.cloned.1.call-start = ((), (), s32[]{:S(2)}) async-start(), calls=%async_computation.13 | async-start | bytes 3072000 | tf_op jit(solution)/shard_map/reduce_scatter | solution.py:1104
  514.3 153.3 %reduce-scatter.17.cloned.1.call-start = ((), (), s32[]{:S(2)}) async-start(), calls=%async_computation.15 | async-start | bytes 2048000 | tf_op jit(solution)/shard_map/reduce_scatter | solution.py:1104
  524.0 59.7 %copy-start.50 = (f32[1024,448]{1,0:T(8,128)S(1)}, f32[1024,448]{1,0:T(8,128)}, u32[]{:S(2)}) copy-start(f32[1024,448]{1,0:T(8,128)} %copy-done.49) | copy-start | bytes 5505028
  592.1 21.1 %copy-start.96 = (f32[16,100]{1,0:T(8,128)S(1)}, f32[16,100]{1,0:T(8,128)}, u32[]{:S(2)}) copy-start(f32[16,100]{1,0:T(8,128)} %copy-done.95) | copy-start | bytes 19204
  592.1 21.1 %copy-start.98 = (f32[16,100]{1,0:T(8,128)S(1)}, f32[16,100]{1,0:T(8,128)}, u32[]{:S(2)}) copy-start(f32[16,100]{1,0:T(8,128)} %copy-done.97) | copy-start | bytes 19204
  592.1 21.1 %copy-start.100 = (f32[16,100]{1,0:T(8,128)S(1)}, f32[16,100]{1,0:T(8,128)}, u32[]{:S(2)}) copy-start(f32[16,100]{1,0:T(8,128)} %copy-done.99) | copy-start | bytes 19204
  592.1 21.2 %copy-start.59 = (f32[128,8,132]{2,1,0:T(8,128)S(1)}, f32[128,8,132]{2,1,0:T(8,128)}, u32[]{:S(2)}) copy-start(f32[128,8,132]{2,1,0:T(8,128)} %copy-done.58) | copy-start | bytes 1622020
  592.2 21.2 %copy-start.61 = (bf16[1024,448]{1,0:T(8,128)(2,1)S(1)}, bf16[1024,448]{1,0:T(8,128)(2,1)}, u32[]{:S(2)}) copy-start(bf16[1024,448]{1,0:T(8,128)(2,1)} %copy-done.60) | copy-start | bytes 2752516
  640.6 22.1 %copy-start.45 = (f32[128,1600]{1,0:T(8,128)S(1)}, f32[128,1600]{1,0:T(8,128)}, u32[]{:S(2)}) copy-start(f32[128,1600]{1,0:T(8,128)} %copy-done.43) | copy-start | bytes 2457604
  640.6 22.1 %copy-start.90 = (f32[1600]{0:T(1024)S(1)}, f32[1600]{0:T(1024)}, u32[]{:S(2)}) copy-start(f32[1600]{0:T(1024)} %param.26) | copy-start | bytes 19204
  640.6 22.1 %copy-start.131 = (f32[128]{0:T(128)S(1)}, f32[128]{0:T(128)}, u32[]{:S(2)}) copy-start(f32[128]{0:T(128)} %copy-done.130) | copy-start | bytes 1540
  640.6 22.4 %copy-start.146 = (f32[128]{0:T(128)S(1)}, f32[128]{0:T(128)}, u32[]{:S(2)}) copy-start(f32[128]{0:T(128)} %copy-done.145) | copy-start | bytes 1540
  640.6 22.4 %copy-start.63 = (f32[128,1600]{1,0:T(8,128)S(1)}, f32[128,1600]{1,0:T(8,128)}, u32[]{:S(2)}) copy-start(f32[128,1600]{1,0:T(8,128)} %get-tuple-element.255) | copy-start | bytes 2457604
  (137 other events, 751.6 us)
Sparse Core Ops, SparseCore 0:
  15.7 98.6 all-gather.4
  116.5 79.7 all-gather.6
  198.4 84.4 all-gather.10
  284.3 48.6 all-gather.8
  352.0 80.7 reduce-scatter.6
  435.1 48.4 reduce-scatter.14
  486.0 23.0 reduce-scatter.10
  512.2 33.4 reduce-scatter.8
  548.6 48.5 reduce-scatter.12
  632.5 34.9 reduce-scatter.16

commit v3 on v2

--- a/solution.py
+++ b/solution.py
@@ -350,173 +350,244 @@
     )(*arrays)
 
 
-def last_kernel(rep, fsdp, square, n_gather, *refs):
-    chips = rep // 2
+def remote_copy(src, dst, sems, axis, target):
+    return pltpu.make_async_remote_copy(
+        src_ref=src,
+        dst_ref=dst,
+        send_sem=sems[0],
+        recv_sem=sems[1],
+        device_id={axis: target},
+        device_id_type=pl.DeviceIdType.MESH,
+    )
+
+
+class Gathers:
+    def __init__(self, rep):
+        chips, self.square = rep // 2, rep == 8
+        self.me = lax.axis_index("rep")
+        self.core = lax.rem(self.me, 2)
+        chip = (self.me - self.core) // 2
+        self.partner = 2 * chip + 1 - self.core
+        if self.square:
+            along_x, along_y = chip + 1 - 2 * lax.rem(chip, 2), lax.rem(chip + 2, 4)
+            first = along_x + self.core * (along_y - along_x)
+            second = along_y + self.core * (along_x - along_y)
+            hops, sources = [first, second], [first, second, 3 - chip]
+        else:
+            hops = [lax.rem(chip + k, chips) for k in range(1, chips)]
+            sources = [lax.rem(chip + chips - k, chips) for k in range(1, chips)]
+        self.hops = [2 * hop + self.core for hop in hops]
+        self.sources = [2 * source + self.core for source in sources]
+
+    def plan(self, source, out, far, near, local, i):
+        blocks = [out.at[origin] for origin in self.sources]
+
+        def over(sems, src, dst, k, target):
+            return remote_copy(src, dst, (sems.at[0, i, k], sems.at[1, i, k]), "rep", target)
+
+        own = [over(far, source, out.at[self.me], k, hop) for k, hop in enumerate(self.hops)]
+        if self.square:
+            own.append(over(far, blocks[0], blocks[0], 2, self.hops[1]))
+        across = [over(near, block, block, k, self.partner) for k, block in enumerate(blocks)]
+        across.append(over(near, source, out.at[self.me], len(blocks), self.partner))
+        return own, across, pltpu.make_async_copy(source, out.at[self.me], local.at[i])
+
+    def begin(self, plan):
+        own, across, keep = plan
+        for copy in own[: len(self.hops)]:
+            copy.start()
+        across[-1].start()
+        keep.start()
+
+    def first_hop(self, plan):
+        own, across, _ = plan
+        own[0].wait_recv()
+        if self.square:
+            own[2].start()
+        across[0].start()
+
+    def second_hop(self, plan):
+        own, across, _ = plan
+        for k in range(1, len(self.hops)):
+            own[k].wait_recv()
+            across[k].start()
+
+    def relayed(self, plan):
+        own, across, _ = plan
+        if self.square:
+            own[2].wait_recv()
+            across[2].start()
+
+    def end(self, plan):
+        own, across, keep = plan
+        for copy in across:
+            copy.wait()
+        for copy in own:
+            copy.wait_send()
+        keep.wait()
+
+
+def last_kernel(rep, fsdp, square, n_gather, layout, down_rows, *refs):
+    parts_gate_up, parts_down, refs = refs[0], refs[1], refs[2:]
     gathers, refs = refs[:n_gather], refs[n_gather:]
     small, gains, trades, refs = refs[0], refs[1], refs[2:4], refs[4:]
+    joined_gate, joined_up, joined_down, refs = refs[0], refs[1], refs[2], refs[3:]
     gathered, refs = refs[:n_gather], refs[n_gather:]
     small_out, gains_out, traded, refs = refs[0], refs[1], refs[2:4], refs[4:]
-    arrived, total, lined, gains_in, gains_sum, local, far, near, remote = refs
-
-    me, line = lax.axis_index("rep"), lax.axis_index("fsdp")
-    core = lax.rem(me, 2)
-    chip = (me - core) // 2
-    partner = 2 * chip + 1 - core
-    if square:
-        along_x, along_y = chip + 1 - 2 * lax.rem(chip, 2), lax.rem(chip + 2, 4)
-        first = along_x + core * (along_y - along_x)
-        second = along_y + core * (along_x - along_y)
-        hops, sources = [first, second], [first, second, 3 - chip]
-    else:
-        hops = [lax.rem(chip + k, chips) for k in range(1, chips)]
-        sources = [lax.rem(chip + chips - k, chips) for k in range(1, chips)]
+    arrived, total, lined, gains_in, gains_sum, local, far, near, keeping, remote = refs
+
+    line = lax.axis_index("fsdp")
     others = [lax.rem(line + k, fsdp) for k in range(1, fsdp)]
-    barrier = pltpu.get_barrier_semaphore()
-    for axis, indices in (("rep", [2 * hop + core for hop in hops] + [partner]), ("fsdp", others)):
-        for index in indices:
+    along = Gathers(rep)
+
+    def push(block, out, slot):
+        return [
+            remote_copy(
+                block(other), out, (remote.at[0, slot, k], remote.at[1, slot, k]), "fsdp", other
+            )
+            for k, other in enumerate(others)
+        ]
+
+    gains_plan = along.plan(gains, gains_in, far, near, local, 0)
+    plans = [
+        along.plan(gathers[i], gathered[i], far, near, local, 1 + i) for i in range(n_gather)
+    ]
+    small_plan = along.plan(lined, small_out, far, near, local, 1 + n_gather)
+    small_in = push(lambda other: small.at[other], arrived.at[line], 0)
+    small_back = push(lambda other: total, lined.at[line], 3)
+    gains_push = push(lambda other: gains_sum, gains_out.at[line], 4)
+    gains_keep = pltpu.make_async_copy(gains_sum, gains_out.at[line], keeping.at[2])
+    traffic = []
+    for i in range(2):
+        source = trades[i]
+        traffic += push(lambda other: source.at[other], traded[i].at[line], 1 + i)
+        traffic.append(
+            pltpu.make_async_copy(source.at[line], traded[i].at[line], keeping.at[i])
+        )
+    step, steps = pl.program_id(0), pl.num_programs(0)
+
+    @pl.when(step == 0)
+    def _():
+        barrier = pltpu.get_barrier_semaphore()
+        met = [("rep", index) for index in (*along.hops, along.partner)]
+        met += [("fsdp", index) for index in others]
+        for axis, index in met:
             pl.semaphore_signal(
                 barrier, inc=1, device_id={axis: index}, device_id_type=pl.DeviceIdType.MESH
             )
-    pl.semaphore_wait(barrier, len(hops) + 1 + len(others))
-
-    kept, sent, waited = [], [], []
-
-    def keep(src, dst):
-        copy = pltpu.make_async_copy(src, dst, local.at[len(kept)])
-        copy.start()
-        kept.append(copy)
-
-    def push(block, out, slot):
-        copies = [
-            send(block(other), out, (remote.at[0, slot, k], remote.at[1, slot, k]), "fsdp", other)
-            for k, other in enumerate(others)
-        ]
-        return copies
-
-    def hop_send(src, dst, slot, k, target):
-        copy = send(src, dst, (far.at[0, slot, k], far.at[1, slot, k]), "rep", 2 * target + core)
-        sent.append(copy)
-        return copy
-
-    def cross_send(src, dst, slot, k):
-        copy = send(src, dst, (near.at[0, slot, k], near.at[1, slot, k]), "rep", partner)
-        sent.append(copy)
-        waited.append(copy)
-
-    def start_gather(source, out, slot):
-        far_copies = [
-            hop_send(source, out.at[me], slot, k, hop) for k, hop in enumerate(hops)
-        ]
-        cross_send(source, out.at[me], slot, chips - 1)
-        keep(source, out.at[me])
-        return out, slot, far_copies
-
-    def pass_on(state):
-        out, slot, far_copies = state
-        for k, source in enumerate(sources):
-            block = out.at[2 * source + core]
-            far_copies[k].wait_recv()
-            if square and k == 0:
-                far_copies.append(hop_send(block, block, slot, 2, second))
-            cross_send(block, block, slot, k)
-
-    small_copies = push(lambda other: small.at[other], arrived.at[line], 0)
-    states = [start_gather(gains, gains_in, 0)]
-    for i in range(n_gather):
-        states.append(start_gather(gathers[i], gathered[i], 1 + i))
-    for i in range(2):
-        keep(trades[i].at[line], traded[i].at[line])
-        waited += push(lambda other: trades[i].at[other], traded[i].at[line], 1 + i)
-        sent += waited[-len(others) :]
-    for copy in small_copies:
-        copy.wait()
-    value = small[line].astype(f32)
-    for other in others:
-        value = value + arrived[other].astype(f32)
-    total[...] = value.astype(total.dtype)
-    small_copies = push(lambda other: total, lined.at[line], 3)
-    lined[line] = total[...]
-
-    gains_state, states = states[0], states[1:]
-    crossed = len(waited)
-    pass_on(gains_state)
-    for copy in waited[crossed:]:
-        copy.wait_recv()
-    for state in states:
-        pass_on(state)
-    for copy in small_copies:
-        copy.wait()
-    small_state = start_gather(lined, small_out, 1 + n_gather)
-    kept[0].wait()
-    waited.pop(0).wait_recv()
-    gains_sum[...] = jnp.sum(gains_in[...], axis=0)
-    keep(gains_sum, gains_out.at[line])
-    gains_copies = push(lambda other: gains_sum, gains_out.at[line], 4)
-    pass_on(small_state)
-    for copy in waited[: crossed - 1] + waited[crossed - 1 + chips - 1 :]:
-        copy.wait_recv()
-    for copy in sent:
-        copy.wait_send()
-    for copy in gains_copies:
-        copy.wait()
-    for copy in kept[1:]:
-        copy.wait()
-
-
-def last_exchange(rep, fsdp, collective_id, gathers, small, gains, trades):
+        pl.semaphore_wait(barrier, len(met))
+        for copy in small_in:
+            copy.start()
+        along.begin(gains_plan)
+        for plan in plans:
+            along.begin(plan)
+        for copy in traffic:
+            copy.start()
+
+    join_kernel(rep, layout, parts_gate_up, joined_gate, joined_up)
+    join_rows_kernel(rep, down_rows, True, parts_down, joined_down)
+
+    @pl.when(step == steps - 1)
+    def _():
+        for copy in small_in:
+            copy.wait()
+        value = small[line].astype(f32)
+        for other in others:
+            value = value + arrived[other].astype(f32)
+        total[...] = value.astype(total.dtype)
+        for copy in small_back:
+            copy.start()
+        lined[line] = total[...]
+        for plan in (gains_plan, *plans):
+            along.first_hop(plan)
+        for plan in (gains_plan, *plans):
+            along.second_hop(plan)
+        along.relayed(gains_plan)
+        along.end(gains_plan)
+        gains_sum[...] = jnp.sum(gains_in[...], axis=0)
+        for copy in gains_push:
+            copy.start()
+        gains_keep.start()
+        for copy in small_back:
+            copy.wait()
+        along.begin(small_plan)
+        for plan in plans:
+            along.relayed(plan)
+        along.first_hop(small_plan)
+        along.second_hop(small_plan)
+        along.relayed(small_plan)
+        for plan in (*plans, small_plan):
+            along.end(plan)
+        for copy in (*traffic, *gains_push, gains_keep):
+            copy.wait()
+
+
+def last_exchange(rep, fsdp, collective_id, ffn, gathers, small, gains, trades):
     n_gather, chips = len(gathers), rep // 2
-    out_shape = [jax.ShapeDtypeStruct((rep,) + x.shape, x.dtype) for x in gathers]
+    parts_gate_up, parts_down, ff_width, ff_rows = ffn
+    rows, ff_part, width = parts_gate_up.shape[1], parts_gate_up.shape[2] // 2, gains.shape[1]
+    block, columns = next(n for n in (80, 40, 64, rows) if rows % n == 0), 2 * LANES
+    steps, row_steps = pl.cdiv(width, columns), rows // block
+    rest = ff_width // rep // fsdp
+    layout = (((0, 0, rest, 0, fsdp),), ((0, ff_part, rest, 0, fsdp),))
+
+    def row_at(i):
+        return lax.div(i * row_steps, steps)
+
+    out_shape = [jax.ShapeDtypeStruct((rows, ff_width), bf16)] * 2
+    out_shape.append(jax.ShapeDtypeStruct((width, ff_rows), bf16))
+    out_shape += [jax.ShapeDtypeStruct((rep,) + x.shape, x.dtype) for x in gathers]
     out_shape.append(jax.ShapeDtypeStruct((rep,) + small.shape, small.dtype))
     out_shape.append(jax.ShapeDtypeStruct((fsdp,) + gains.shape, gains.dtype))
     out_shape += [jax.ShapeDtypeStruct(x.shape, x.dtype) for x in trades]
     return pl.pallas_call(
-        functools.partial(last_kernel, rep, fsdp, rep == 8, n_gather),
+        functools.partial(
+            last_kernel, rep, fsdp, rep == 8, n_gather, layout, ff_rows // rep
+        ),
+        grid=(steps,),
         out_shape=out_shape,
-        in_specs=[vmem_spec()] * (n_gather + 4),
-        out_specs=[hbm_spec()] * (n_gather + 4),
+        in_specs=[
+            pl.BlockSpec((rep, block, 2 * ff_part), lambda i: (0, row_at(i), 0)),
+            pl.BlockSpec((rep, parts_down.shape[1], columns), lambda i: (0, 0, i)),
+        ]
+        + [vmem_spec()] * (n_gather + 4),
+        out_specs=[pl.BlockSpec((block, ff_width), lambda i: (row_at(i), 0))] * 2
+        + [pl.BlockSpec((columns, ff_rows), lambda i: (i, 0))]
+        + [hbm_spec()] * (n_gather + 4),
         scratch_shapes=[
             pltpu.VMEM(small.shape, small.dtype),
             pltpu.VMEM(small.shape[1:], small.dtype),
             pltpu.VMEM(small.shape, small.dtype),
             pltpu.VMEM((rep,) + gains.shape, gains.dtype),
             pltpu.VMEM(gains.shape, gains.dtype),
-            pltpu.SemaphoreType.DMA((n_gather + 5,)),
+            pltpu.SemaphoreType.DMA((n_gather + 2,)),
             pltpu.SemaphoreType.DMA((2, n_gather + 2, chips)),
             pltpu.SemaphoreType.DMA((2, n_gather + 2, chips)),
+            pltpu.SemaphoreType.DMA((3,)),
             pltpu.SemaphoreType.DMA((2, 5, fsdp)),
         ],
         compiler_params=pltpu.CompilerParams(
             collective_id=collective_id,
             has_side_effects=True,
-            vmem_limit_bytes=40 * 1024 * 1024,
+            vmem_limit_bytes=48 * 1024 * 1024,
         ),
         cost_estimate=SMALL_COST,
-    )(*gathers, small, gains, *trades)
-
-
-def pair_kernel(own_ref, out_ref, local, send_sem, recv_sem):
-    me = lax.axis_index("rep")
-    core = lax.rem(me, 2)
-    partner = me + 1 - 2 * core
-    meet("rep", [partner])
-    keep = pltpu.make_async_copy(own_ref, out_ref.at[:, core], local)
-    keep.start()
-    copy = send(own_ref, out_ref.at[:, core], (send_sem, recv_sem), "rep", partner)
-    copy.wait()
-    keep.wait()
-
-
-def pair_gather(collective_id, own):
-    groups, rows, width = own.shape
+    )(parts_gate_up, parts_down, *gathers, small, gains, *trades)
+
+
+def hand_kernel(_value, _after, _out):
+    pass
+
+
+def hand_on(value, after):
     return pl.pallas_call(
-        pair_kernel,
-        out_shape=jax.ShapeDtypeStruct((groups, 2, rows, width), own.dtype),
-        in_specs=[vmem_spec()],
+        hand_kernel,
+        out_shape=jax.ShapeDtypeStruct(value.shape, value.dtype),
+        in_specs=[hbm_spec()] * 2,
         out_specs=hbm_spec(),
-        scratch_shapes=[pltpu.SemaphoreType.DMA] * 3,
-        compiler_params=pltpu.CompilerParams(collective_id=collective_id, has_side_effects=True),
+        input_output_aliases={0: 0},
         cost_estimate=SMALL_COST,
-    )(own)
+    )(value, after)
 
 
 def windows(width, pieces, start, step, rest):
@@ -587,13 +658,13 @@
                 for r in range(rep):
                     at = place + (i * rep + r) * rest
                     piece = sources[index][r, :, start : start + rest]
-                    out[:, at : at + rest] = piece.astype(f32)
+                    out[:, at : at + rest] = piece.astype(out.dtype)
 
 
 def join_rows_kernel(rep, rows, flip, source, out):
     for r in range(rep):
         if flip:
-            out[:, r * rows : (r + 1) * rows] = source[r].astype(f32).T[:, :rows]
+            out[:, r * rows : (r + 1) * rows] = source[r].astype(f32).T[:, :rows].astype(out.dtype)
         else:
             out[r * rows : (r + 1) * rows, :] = source[r, :rows, :].astype(f32)
 
@@ -632,6 +703,35 @@
     )(*sources)
 
 
+def spread_beside(rep, steps, pairs, local, far, near):
+    along = Gathers(rep)
+    plans = [along.plan(*pair, far, near, local, i) for i, pair in enumerate(pairs)]
+
+    @pl.when(steps[0])
+    def _():
+        meet("rep", [*along.hops, along.partner])
+        for plan in plans:
+            along.begin(plan)
+
+    @pl.when(steps[1])
+    def _():
+        for plan in plans:
+            along.first_hop(plan)
+
+    @pl.when(steps[2])
+    def _():
+        for plan in plans:
+            along.second_hop(plan)
+
+    def finish():
+        for plan in plans:
+            along.relayed(plan)
+        for plan in plans:
+            along.end(plan)
+
+    return finish
+
+
 def spread_maps(maps_ref, wide_ref, start):
     count, packs, columns = maps_ref.shape
 
@@ -647,16 +747,20 @@
 
 
 def scan_kernel(
+    rep,
     channels,
     decay_step_ref,
     input_ref,
     maps_ref,
     rate_ref,
-    _handed_ref,
+    beside_ref,
     out_ref,
     decayed_ref,
-    _handed_on_ref,
+    beside_out_ref,
     wide_ref,
+    local,
+    far,
+    near,
 ):
     count, packs, _ = decay_step_ref.shape
     valid = (
@@ -664,6 +768,10 @@
         < channels - pl.program_id(1) * LANES
     )
     rate = jnp.where(valid[:1], rate_ref[...], 0.0)
+    at = pl.program_id(0) * pl.num_programs(1) + pl.program_id(1)
+    last = pl.num_programs(0) * pl.num_programs(1) - 1
+    steps = [at == step for step in (0, 2 * last // 3, last)]
+    finish = spread_beside(rep, steps, [(beside_ref, beside_out_ref)], local, far, near)
 
     @pl.when(pl.program_id(1) == 0)
     def _():
@@ -687,13 +795,14 @@
         return states
 
     lax.fori_loop(0, count // 2, step, (jnp.zeros((packs, LANES), f32),) * STATE)
-
-
-def scan_forward(decay_step, inputs, maps, rate, handed):
+    pl.when(at == last)(finish)
+
+
+def scan_forward(decay_step, inputs, maps, rate, rep, collective_id, beside):
     count, packs, channels = inputs.shape
     wide = pl.BlockSpec((count, PACKS, LANES), lambda g, i: (0, g, i))
     return pl.pallas_call(
-        functools.partial(scan_kernel, channels),
+        functools.partial(scan_kernel, rep, channels),
         grid=(packs // PACKS, pl.cdiv(channels, LANES)),
         in_specs=[
             wide,
@@ -707,86 +816,26 @@
             pl.BlockSpec((STATE, count, PACKS, LANES), lambda g, i: (0, 0, g, i)),
             hbm_spec(),
         ],
-        input_output_aliases={4: 2},
         out_shape=[
             jax.ShapeDtypeStruct(inputs.shape, f32),
             jax.ShapeDtypeStruct(
                 (STATE, count, packs, pl.cdiv(channels, LANES) * LANES), f32
             ),
-            jax.ShapeDtypeStruct(handed.shape, handed.dtype),
+            jax.ShapeDtypeStruct((rep,) + beside.shape, beside.dtype),
         ],
-        scratch_shapes=[pltpu.VMEM((2 * STATE, count, PACKS, LANES), f32)],
-        compiler_params=pltpu.CompilerParams(vmem_limit_bytes=48 * 1024 * 1024),
+        scratch_shapes=[
+            pltpu.VMEM((2 * STATE, count, PACKS, LANES), f32),
+            pltpu.SemaphoreType.DMA((1,)),
+            pltpu.SemaphoreType.DMA((2, 1, rep // 2)),
+            pltpu.SemaphoreType.DMA((2, 1, rep // 2)),
+        ],
+        compiler_params=pltpu.CompilerParams(
+            collective_id=collective_id,
+            has_side_effects=True,
+            vmem_limit_bytes=48 * 1024 * 1024,
+        ),
         cost_estimate=SMALL_COST,
-    )(decay_step, inputs, maps, rate, handed)
-
-
-def spread_beside(rep, steps, source, out, local, far, near):
-    chips, square = rep // 2, rep == 8
-    me = lax.axis_index("rep")
-    core = lax.rem(me, 2)
-    chip = (me - core) // 2
-    partner = 2 * chip + 1 - core
-    if square:
-        along_x, along_y = chip + 1 - 2 * lax.rem(chip, 2), lax.rem(chip + 2, 4)
-        first = along_x + core * (along_y - along_x)
-        second = along_y + core * (along_x - along_y)
-        hops, sources = [first, second], [first, second, 3 - chip]
-    else:
-        hops = [lax.rem(chip + k, chips) for k in range(1, chips)]
-        sources = [lax.rem(chip + chips - k, chips) for k in range(1, chips)]
-
-    def copy_to(src, dst, sems, k, target):
-        return pltpu.make_async_remote_copy(
-            src_ref=src,
-            dst_ref=dst,
-            send_sem=sems.at[0, k],
-            recv_sem=sems.at[1, k],
-            device_id={"rep": target},
-            device_id_type=pl.DeviceIdType.MESH,
-        )
-
-    def block(k):
-        return out.at[2 * sources[k] + core]
-
-    own = [copy_to(source, out.at[me], far, k, 2 * hop + core) for k, hop in enumerate(hops)]
-    if square:
-        own.append(copy_to(block(0), block(0), far, 2, 2 * second + core))
-    crossing = [copy_to(block(k), block(k), near, k, partner) for k in range(chips - 1)]
-    crossing.append(copy_to(source, out.at[me], near, chips - 1, partner))
-    keep = pltpu.make_async_copy(source, out.at[me], local)
-
-    @pl.when(steps[0])
-    def _():
-        meet("rep", [2 * hop + core for hop in hops] + [partner])
-        for copy in own[: len(hops)]:
-            copy.start()
-        crossing[-1].start()
-        keep.start()
-
-    @pl.when(steps[1])
-    def _():
-        own[0].wait_recv()
-        if square:
-            own[2].start()
-        crossing[0].start()
-
-    @pl.when(steps[2])
-    def _():
-        for k in range(1, len(hops)):
-            own[k].wait_recv()
-            crossing[k].start()
-
-    @pl.when(steps[3])
-    def _():
-        if square:
-            own[2].wait_recv()
-            crossing[2].start()
-        for copy in crossing:
-            copy.wait()
-        for copy in own:
-            copy.wait_send()
-        keep.wait()
+    )(decay_step, inputs, maps, rate, beside)
 
 
 def scan_back_kernel(
@@ -800,11 +849,13 @@
     decayed_ref,
     rate_ref,
     beside_ref,
+    beside2_ref,
     grad_input_ref,
     grad_step_ref,
     grad_rate_ref,
     grad_maps_ref,
     beside_out_ref,
+    beside2_out_ref,
     carry_ref,
     rates_ref,
     in_sum_ref,
@@ -819,8 +870,9 @@
     at = (pl.program_id(0) * pl.num_programs(1) + pl.program_id(1)) * pl.num_programs(2)
     at = at + pl.program_id(2)
     last = pl.num_programs(0) * pl.num_programs(1) * pl.num_programs(2) - 1
-    steps = [at == step for step in (0, 9 * last // 16, 11 * last // 16, last)]
-    spread_beside(rep, steps, beside_ref, beside_out_ref, local, far, near)
+    steps = [at == step for step in (0, 10 * last // 16, 14 * last // 16)]
+    pairs = [(beside_ref, beside_out_ref), (beside2_ref, beside2_out_ref)]
+    finish = spread_beside(rep, steps, pairs, local, far, near)
     tile, chunk = pl.program_id(1), pl.program_id(2)
     start = (pl.num_programs(2) - 1 - chunk) * count
     valid = lax.broadcasted_iota(jnp.int32, (packs, LANES), 1) < channels - tile * LANES
@@ -898,6 +950,8 @@
             total = total + summed(out_sum_ref[n, here], STATE + n)
         grad_maps_ref[here] = total.reshape(count, packs, LANES)
 
+    pl.when(at == last)(finish)
+
 
 def scan_backward(decay_step, step, inputs, maps, grad, decayed, rate, rep, collective_id, beside):
     count, packs, channels = inputs.shape
@@ -906,7 +960,7 @@
     wide = pl.BlockSpec((part, PACKS, LANES), lambda g, i, c: (chunks - 1 - c, g, i))
     row = pl.BlockSpec((STATE, LANES), lambda g, i, c: (0, i))
     sums = pltpu.VMEM((STATE, count, PACKS, LANES), f32)
-    grad_inputs, grad_step, grad_rate, grad_maps, all_beside = pl.pallas_call(
+    grad_inputs, grad_step, grad_rate, grad_maps, *all_beside = pl.pallas_call(
         functools.partial(scan_back_kernel, rep, channels),
         grid=(groups, pl.cdiv(channels, LANES), chunks),
         in_specs=[
@@ -919,22 +973,22 @@
                 (STATE, part, PACKS, LANES), lambda g, i, c: (0, chunks - 1 - c, g, i)
             ),
             row,
-            hbm_spec(),
-        ],
+        ]
+        + [hbm_spec()] * 2,
         out_specs=[
             wide,
             wide,
             pl.BlockSpec((STATE, LANES), lambda g, i, c: (g, i)),
             pl.BlockSpec((count, PACKS, LANES), lambda g, i, c: (0, g, 0)),
-            hbm_spec(),
-        ],
+        ]
+        + [hbm_spec()] * 2,
         out_shape=[
             jax.ShapeDtypeStruct(inputs.shape, f32),
             jax.ShapeDtypeStruct(inputs.shape, f32),
             jax.ShapeDtypeStruct((groups * STATE, channels), f32),
             jax.ShapeDtypeStruct((count, packs, LANES), f32),
-            jax.ShapeDtypeStruct((rep,) + beside.shape, beside.dtype),
-        ],
+        ]
+        + [jax.ShapeDtypeStruct((rep,) + x.shape, x.dtype) for x in beside],
         scratch_shapes=[
             pltpu.VMEM((2 * STATE, PACKS, LANES), f32),
             pltpu.VMEM((STATE, PACKS, LANES), f32),
@@ -942,9 +996,9 @@
             sums,
             pltpu.VMEM((count, PACKS, LANES), f32),
             pltpu.VMEM((2 * STATE, count, PACKS, LANES), f32),
-            pltpu.SemaphoreType.DMA,
-            pltpu.SemaphoreType.DMA((2, rep // 2)),
-            pltpu.SemaphoreType.DMA((2, rep // 2)),
+            pltpu.SemaphoreType.DMA((2,)),
+            pltpu.SemaphoreType.DMA((2, 2, rep // 2)),
+            pltpu.SemaphoreType.DMA((2, 2, rep // 2)),
         ],
         compiler_params=pltpu.CompilerParams(
             collective_id=collective_id,
@@ -952,7 +1006,7 @@
             vmem_limit_bytes=52 * 1024 * 1024,
         ),
         cost_estimate=SMALL_COST,
-    )(decay_step, step, inputs, maps, grad, decayed, rate, beside)
+    )(decay_step, step, inputs, maps, grad, decayed, rate, *beside)
     grad_rate = jnp.sum(grad_rate.reshape(groups, STATE, channels), axis=0)
     in_maps, both = grad_maps[:, :, :STATE], grad_maps[:, :, 2 * STATE : 2 * STATE + 1]
     out_maps = grad_maps[:, :, STATE : 2 * STATE] + maps[:, :, :STATE] * both
@@ -1116,8 +1170,10 @@
         in_width,
     )
     full_in = line_gather(part_in)
-    half = w_mix_out.shape[0] // 2
-    part_mix = lax.dynamic_slice_in_dim(w_mix_out, lax.rem(me, 2) * half, half, 0)
+    mix_part = width // rep
+    part_mix = lax.dynamic_slice_in_dim(w_mix_out, me * mix_part, mix_part, 1)
+    mix_size = part_mix.size
+    part_mix = jnp.pad(part_mix.reshape(-1), (0, -mix_size % (16 * width))).reshape(-1, width)
     part_mout, part_down = my_rows(w_mamba_out), my_rows(w_down)
 
     received, cot_received = line_exchange(
@@ -1159,6 +1215,11 @@
     in_seq_all = normed_sent[:, :, width].astype(f32).T.reshape(group, 1)
 
     in_out = dot(swapped(normed_all.reshape(rep, count, width)), full_in)
+    mout_mix = hand_on(mout_mix, in_out)
+    mout_mix = mout_mix.reshape(fsdp, -1, width)
+    full_mout = mout_mix[:, : part_mout.shape[0]].reshape(-1, width)
+    mix_t = mout_mix[:, part_mout.shape[0] :].reshape(fsdp, -1)[:, :mix_size]
+    mix_t = mix_t.reshape(width, mix_part).T
     xs, gate_z = in_out[:, :channels], in_out[:, gate_at : gate_at + channels]
     qkv_sent = in_out[:, channels : channels + qkv_part].astype(bf16)
     qkv_sent = swapped(qkv_sent.reshape(count, rep, qkv_part))
@@ -1185,13 +1246,11 @@
     decay_step = jnp.where(in_seq_all == 0.0, 1e30, step * LOG2_E)
     inputs = step * act
     cube = (count, rep, channels)
-    scanned, decayed, mout_mix = scan_forward(
-        decay_step.reshape(cube), inputs.reshape(cube), maps, rate, mout_mix
-    )
+    scanned, decayed, mix_t = scan_forward(
+        decay_step.reshape(cube), inputs.reshape(cube), maps, rate, rep, 9, mix_t
+    )
+    mix_t = mix_t.reshape(width, width)
     scanned = scanned.reshape(group, channels)
-    mout_mix = mout_mix.reshape(fsdp, -1, width)
-    full_mout = mout_mix[:, : part_mout.shape[0]].reshape(-1, width)
-    half_mix = mout_mix[:, part_mout.shape[0] :]
     silu_z, z_slope = silu_and_slope(gate_z)
     before_gate = scanned + part_skip * act
     mixer_low = swapped((before_gate * silu_z).astype(bf16).reshape(cube))
@@ -1199,11 +1258,9 @@
     (ssm_out,) = rep_exchange(rep, 3, sums=(ssm_part,))
 
     attended_values, log_total = attention_forward(qkv_low, allowed)
-    half_mix, qkv_low = lax.optimization_barrier((half_mix, qkv_low))
-    full_mix = pair_gather(9, half_mix).reshape(width, width)
     mixed, mix_pull = jax.vjp(mix_branches, attended_values, ssm_out, norm_attn, norm_ssm)
     mixed_low = mixed.astype(bf16)
-    middle = hidden_in + dot(mixed_low, full_mix)
+    middle = hidden_in + dot_right_t(mixed_low, mix_t)
     ffn_in, ffn_pull = jax.vjp(rms_norm, middle, norm_ffn)
     ffn_all, mixed_all = rep_exchange(rep, 4, gathers=(ffn_in.astype(bf16), mixed_low))
     ffn_all, mixed_all = ffn_all.reshape(group, width), mixed_all.reshape(group, width)
@@ -1229,7 +1286,7 @@
     grad_middle_norm, grad_norm_ffn = ffn_pull(grad_ffn)
     grad_middle = cot_rows + grad_middle_norm
     middle_low = grad_middle.astype(bf16)
-    grad_mixed = dot_right_t(middle_low, full_mix)
+    grad_mixed = dot(middle_low, mix_t)
     grad_attended, grad_ssm, grad_norm_attn, grad_norm_ssm = mix_pull(grad_mixed)
     middle_sent = middle_low.reshape(count, rep, -1).transpose(1, 0, 2)
     qkv_grad = attention_backward(qkv_low, grad_attended.astype(bf16), log_total, allowed)
@@ -1254,7 +1311,7 @@
     own_early = line_scatter(part_early)
     grad_before = grad_mixer * silu_z
     grad_skip = jnp.sum(grad_before * act, axis=0)
-    grad_inputs, grad_step, grad_rate, grad_maps, all_gate_up = scan_backward(
+    grad_inputs, grad_step, grad_rate, grad_maps, (all_gate_up, all_down) = scan_backward(
         *(item.reshape(cube) for item in (decay_step, step, inputs)),
         maps,
         grad_before.reshape(cube),
@@ -1262,7 +1319,7 @@
         rate,
         rep,
         7,
-        own_gate_up,
+        (own_gate_up, own_down),
     )
     grad_inputs = grad_inputs.reshape(group, channels)
     grad_step = grad_step.reshape(group, channels)
@@ -1310,11 +1367,13 @@
     gains = jnp.stack([grad_norm_in, grad_norm_attn, grad_norm_ssm, grad_norm_ffn])
     gains = jnp.concatenate([gains, jnp.zeros((4, width), f32)], axis=0)
     (
+        sum_gate,
+        sum_up,
+        sum_down,
         all_mout,
         all_mix,
         all_early,
         all_late,
-        all_down,
         small,
         gains,
         mixed_out,
@@ -1323,19 +1382,13 @@
         rep,
         fsdp,
         10,
-        (own_mout, own_mix, own_early, own_late, own_down),
+        (all_gate_up, all_down, w_gate.shape[1], w_down.shape[0]),
+        (own_mout, own_mix, own_early, own_late),
         small.reshape(fsdp, -1, channels),
         gains,
         (given_back(result), given_back(grad_hidden_in)),
     )
     gains, small = jnp.sum(gains, axis=0), small.reshape(rep, n_small, channels)
-    all_gate_up = tied(all_gate_up, all_late)
-    sum_gate, sum_up = join_columns(
-        rep,
-        (all_gate_up,),
-        (w_gate.shape[1], w_up.shape[1]),
-        (((0, 0, ff_piece, 0, fsdp),), ((0, ff_part, ff_piece, 0, fsdp),)),
-    )
     sum_mamba_in, sum_qkv, sum_mix = join_columns(
         rep,
         (all_late, all_early, all_mix),
@@ -1346,7 +1399,6 @@
             ((2, 0, width // rep, 0, 1),),
         ),
     )
-    sum_down = join_rows(rep, all_down, w_down.shape[0], width, flip=True).T
     sum_mout = join_rows(rep, all_mout, w_mamba_out.shape[0], width)
 
     (small,) = join_columns(rep, (small,), (INNER,), (((0, 0, piece, 0, fsdp),),))
@@ -1370,9 +1422,9 @@
         gains[2],
         sum_mix,
         gains[3],
-        sum_gate,
-        sum_up,
-        sum_down,
+        sum_gate.astype(f32),
+        sum_up.astype(f32),
+        sum_down.astype(f32).T,
     )
 
 

time: 837 us -> 785 us (0.938)
  Pallas kernels: 506 us -> 463 us
  waiting for transfers between devices: 19.5 us -> 7.72 us
    pallas_call x1, Pallas kernels: 104 us -> 72 us  [last_exchange(): pl.pallas_call(functools.partial(last_kernel, rep, fsdp, rep == 8, n_gath...]
    all_gather x4, waiting for transfers between devices: 18.8 us -> 0.03 us  [line_gather(): return lax.all_gather(value, 'fsdp', axis=0, tiled=True)]
    pallas_call x3 -> x2, Pallas kernels: 22.8 us -> 11.1 us  [join_columns(): pl.pallas_call(functools.partial(join_kernel, rep, layout), grid=(rows //...]
    unnamed x327 -> x287, local copies, waits for them, and re-layouts: 53.4 us -> 50.7 us
  transfers between devices with their start and end apart: 10 -> 10, of which waited for: 2 -> 1; matrix products, arithmetic and copies ran while one was open for 26% -> 27% of each run, Pallas kernels for 44% -> 48%
where the time goes in v3:
time: 785 us; the launch traced here: 779 us
  Pallas kernels  463 us (59%)
  matrix products  125 us (16%)
  local copies, waits for them, and re-layouts  117 us (15%)
  other arithmetic  48.4 us (6%)
  between operations  16.4 us (2%)
    pallas_call x8, Pallas kernels, rep_exchange(): pl.pallas_call(functools.partial(rep_kernel, rep, counts, square), out_sh...  226 us
    pallas_call x1, Pallas kernels, last_exchange(): pl.pallas_call(functools.partial(last_kernel, rep, fsdp, rep == 8, n_gath...  72 us
    pallas_call x1, Pallas kernels, scan_backward(): pl.pallas_call(functools.partial(scan_back_kernel, rep, channels), grid=(...  66.8 us
    unnamed x287, local copies, waits for them, and re-layouts  50.7 us
    dot_general x7, matrix products, dot_right_t(): lax.dot_general(left, right, (((1,), (1,)), ((), ())), preferred_element_...  43.3 us
    pallas_call x1, Pallas kernels, line_exchange(): pl.pallas_call(functools.partial(line_kernel, count, (len(gathers), len(a...  41 us
    dot_general x10, matrix products, dot_left_t(): lax.dot_general(left, right, (((0,), (0,)), ((), ())), preferred_element_...  39.7 us
    dot_general x9, matrix products, dot(): return jnp.dot(left, right, precision=precision, preferred_element_type=f32)  37.6 us
  transfers between devices with their start and end apart: 10, of which 1 were waited for; matrix products, arithmetic and copies ran while one was open for 27% of the time, Pallas kernels for 48%

profile of v3, /device:TPU:0, one launch (start us, length us, event | category | flops | bytes accessed | tf_op | source)
XLA Modules:
  0.0 778.8 jit_solution(14500944236928101766)
XLA Ops:
  24.3 41.0 %shard_map.366 = (bf16[4,32,1600]{2,1,0:T(8,128)(2,1)}, bf16[4,32,1600]{2,1,0:T(8,128)(2,1)}) custom-call(bf16[4,32,1600]{2,1,0:T(8,128)(2,1)} %bitcast.295, bf16[4,32,1600]{2,1,0:T(8,128)(2,1)} %bitcast.296), custom_call_target="tpu_custom_call" | custom-call | bytes 10000 | tf_op jit(solution)/shard_map/pallas_call | solution.py:337
  77.9 33.1 %shard_map.367 = (bf16[8,128,1664]{2,1,0:T(8,128)(2,1)S(1)}, bf16[8,128,1600]{2,1,0:T(8,128)(2,1)S(1)}) custom-call(bf16[128,1664]{1,0:T(8,128)(2,1)S(1)} %pad_maximum_fusion.3.refs_0_, bf16[128,1600]{1,0:T(8,128)(2,1)S(1)} %copy.283.refs_1_), custom_call_target="tpu_custom_call" | custom-call | bytes 10000 | tf_op jit(solution)/shard_map/pallas_call | solution.py:270
  125.6 9.2 %fusion._after = f32[1024,1280]{1,0:T(8,128)S(1)} fusion(bf16[1600,1280]{1,0:T(8,128)(2,1)} %all-gather.5.cloned.1.call-done, bf16[128,8,1600]{2,0,1:T(8,128)(2,1)} %get-tuple-element.256), kind=kOutput, calls=%fused_computation.8 | convolution fusion | flops 4194304000 | bytes 12615680 | tf_op jit(solution)/shard_map/dot_general | solution.py:29
  141.8 27.2 %shard_map.368 = (f32[8,128,132]{2,1,0:T(8,128)S(1)}, bf16[8,128,280]{2,1,0:T(8,128)(2,1)S(1)}) custom-call(f32[8,128,132]{2,1,0:T(8,128)S(1)} %bitcast.245, bf16[8,128,280]{2,1,0:T(8,128)(2,1)S(1)} %bitcast.250), custom_call_target="tpu_custom_call" | custom-call | bytes 10000 | tf_op jit(solution)/shard_map/pallas_call | solution.py:270
  192.4 36.3 %shard_map.370 = (f32[128,8,448]{2,1,0:T(8,128)S(1)}, f32[16,128,8,512]{3,2,1,0:T(8,128)}, bf16[8,200,1600]{2,1,0:T(8,128)(2,1)}) custom-call(f32[128,8,448]{2,1,0:T(8,128)S(1)} %get-tuple-element.259.decay_step_ref, f32[128,8,448]{2,1,0:T(8,128)} %get-tuple-element.257.input_ref, f32[128,8,32]{2,1,0:T(8,128)S(1)} %copy.325.maps_ref, ...), custom_call_target="tpu_custom_call" | custom-call | bytes 10000 | tf_op jit(solution)/shard_map/pallas_call | solution.py:804
  237.8 22.1 %shard_map.371 = f32[128,1600]{1,0:T(8,128)S(1)} custom-call(bf16[8,128,1600]{2,1,0:T(8,128)(2,1)S(1)} %bitcast.247), custom_call_target="tpu_custom_call" | custom-call | bytes 10000 | tf_op jit(solution)/shard_map/pallas_call | solution.py:270
  264.4 4.4 multiply_reduce_fusion.13
  269.9 31.8 %shard_map.372 = (bf16[8,128,1600]{2,1,0:T(8,128)(2,1)S(1)}, bf16[8,128,1600]{2,1,0:T(8,128)(2,1)S(1)}) custom-call(bf16[128,1600]{1,0:T(8,128)(2,1)S(1)} %multiply_convert_fusion.4.refs_0_, bf16[128,1600]{1,0:T(8,128)(2,1)S(1)} %multiply_convert_fusion.5.refs_1_), custom_call_target="tpu_custom_call" | custom-call | bytes 10000 | tf_op jit(solution)/shard_map/pallas_call | solution.py:270
  305.2 10.2 %fusion.106 = f32[1024,1408]{0,1:T(8,128)} fusion(bf16[1024,1600]{1,0:T(8,128)(2,1)} %bitcast.266, bf16[1600,1408]{1,0:T(8,128)(2,1)} %all-gather.11.cloned.1.call-done), kind=kOutput, calls=%fused_computation.291 | convolution fusion | flops 4613734400 | bytes 13549568 | tf_op jit(solution)/shard_map/dot_general | solution.py:29
  315.4 9.4 %fusion.6 = (bf16[1024,704]{0,1:T(8,128)(2,1)S(1)}, bf16[1024,704]{0,1:T(8,128)(2,1)S(1)}, bf16[1024,704]{0,1:T(8,128)(2,1)}) fusion(f32[1024,1408]{0,1:T(8,128)} %fusion.106, bf16[1024,1600]{1,0:T(8,128)(2,1)} %bitcast.264, bf16[704,1600]{1,0:T(8,128)(2,1)} %all-gather.7.cloned.1.call-done), kind=kOutput, calls=%fused_computation.18 | convolution fusion | flops 2318401536 | bytes 15622144 | tf_op jit(solution)/shard_map/dot_general | solution.py:33
  326.4 7.7 convolution_convert_fusion
  336.5 6.5 convolution_convert_fusion.6
  346.8 6.0 convolution_convert_fusion.1
  352.9 8.6 %convolution_convert_fusion.2 = bf16[1024,1600]{1,0:T(8,128)(2,1)S(1)} fusion(bf16[1024,1408]{0,1:T(8,128)(2,1)S(1)} %copy-done.69, bf16[1600,1408]{1,0:T(8,128)(2,1)} %all-gather.11.cloned.1.call-done), kind=kOutput, calls=%fused_computation.5 | convolution fusion | flops 4615372800 | bytes 10665984 | tf_op jit(solution)/shard_map/dot_general | solution.py:33
  361.5 35.9 %shard_map.374 = (f32[128,1600]{1,0:T(8,128)S(1)}, f32[128,1600]{1,0:T(8,128)S(1)}) custom-call(bf16[8,128,1600]{2,1,0:T(8,128)(2,1)S(1)} %bitcast.249, bf16[8,128,1600]{2,1,0:T(8,128)(2,1)S(1)} %bitcast.248), custom_call_target="tpu_custom_call" | custom-call | bytes 10000 | tf_op jit(solution)/shard_map/pallas_call | solution.py:270
  402.2 4.4 multiply_reduce_fusion.7
  413.0 33.5 %shard_map.375 = (bf16[8,128,1600]{2,1,0:T(8,128)(2,1)S(1)}, bf16[8,128,200]{2,1,0:T(8,128)(2,1)S(1)}, bf16[8,128,280]{2,1,0:T(8,128)(2,1)S(1)}) custom-call(bf16[128,1600]{1,0:T(8,128)(2,1)S(1)} %get-tuple-element.275.refs_0_, bf16[8,128,200]{2,1,0:T(8,128)(2,1)S(1)} %bitcast.253, bf16[8,128,280]{2,1,0:T(8,128)(2,1)S(1)} %bitcast.251), custom_call_target="tpu_custom_call" | custom-call | bytes 10000 | tf_op jit(solution)/shard_map/pallas_call | solution.py:270
  448.3 4.2 fusion.8
  453.0 5.0 fusion.3
  458.3 5.5 convolution_bitcast_fusion.2
  467.1 5.3 fusion.33
  475.6 6.4 convolution_convert_fusion.5
  490.1 66.8 %shard_map.376 = (f32[128,8,448]{2,1,0:T(8,128)}, f32[128,8,448]{2,1,0:T(8,128)}, f32[16,448]{1,0:T(8,128)S(1)}, f32[128,8,128]{2,1,0:T(8,128)S(1)}, bf16[8,400,...) custom-call(f32[128,8,448]{2,1,0:T(8,128)} %copy-done.2, f32[128,8,448]{2,1,0:T(8,128)} %get-tuple-element.258.step_ref, ...), custom_call_target="tpu_custom_call" | custom-call | bytes 10000 | tf_op jit(solution)/shard_map/pallas_call | solution.py:963
  566.4 20.0 %shard_map.377 = f32[8,128,132]{2,1,0:T(8,128)S(1)} custom-call(f32[8,128,132]{2,1,0:T(8,128)S(1)} %maximum_bitcast_fusion.refs_0_), custom_call_target="tpu_custom_call" | custom-call | bytes 10000 | tf_op jit(solution)/shard_map/pallas_call | solution.py:270
  587.1 9.3 %multiply_reduce_fusion = (bf16[448]{0:T(512)(128)(2,1)S(1)}, bf16[448]{0:T(512)(128)(2,1)S(1)}, bf16[448]{0:T(512)(128)(2,1)S(1)}, bf16[448]{0:T(512)(128)(2,1)...) fusion(f32[1024,448]{1,0:T(8,128)} %bitcast.271, ...), kind=kOutput, calls=%fused_computation.37 | convolution fusion | flops 140181888 | bytes 24532992 | tf_op jit(solution)/shard_map/dot_general | solution.py:33
  602.5 5.4 bitcast_convert_fusion
  610.6 5.5 convolution_convert_fusion.4
  616.2 22.0 %shard_map.378 = f32[128,1600]{1,0:T(8,128)S(1)} custom-call(bf16[8,128,1600]{2,1,0:T(8,128)(2,1)S(1)} %bitcast.246), custom_call_target="tpu_custom_call" | custom-call | bytes 10000 | tf_op jit(solution)/shard_map/pallas_call | solution.py:270
  644.0 6.9 reduce-scatter.17.cloned.1.call-done.refs_5_
  656.7 72.0 %shard_map.379 = (bf16[400,5504]{1,0:T(8,128)(2,1)}, bf16[400,5504]{1,0:T(8,128)(2,1)}, bf16[1600,1376]{1,0:T(8,128)(2,1)}, bf16[8,112,1600]{2,1,0:T(8,128)(2,1)...) custom-call(bf16[8,400,1408]{2,1,0:T(8,128)(2,1)} %get-tuple-element, ...), custom_call_target="tpu_custom_call" | custom-call | bytes 10000 | tf_op jit(solution)/shard_map/pallas_call | solution.py:543
  739.6 4.4 convert_bitcast_fusion
  762.0 9.7 %shard_map.380 = (f32[400,6400]{1,0:T(8,128)}, f32[400,2240]{1,0:T(8,128)}, f32[400,1600]{1,0:T(8,128)}) custom-call(bf16[8,400,448]{2,1,0:T(8,128)(2,1)S(1)} %copy-done.12, bf16[8,400,768]{2,1,0:T(8,128)(2,1)} %get-tuple-element.106.refs_1_, bf16[8,400,200]{2,1,0:T(8,128)(2,1)S(1)} %copy-done.17), custom_call_target="tpu_custom_call" | custom-call | bytes 10000 | tf_op jit(solution)/shard_map/pallas_call | solution.py:693
  (475 shorter events, 186.6 us)
Async XLA Ops:
  7.2 118.4 %all-gather.5.cloned.1.call-start = ((), (), s32[]{:S(2)}) async-start(), calls=%async_computation.6 | async-start | bytes 5120000 | tf_op jit(solution)/shard_map/all_gather | solution.py:1155
  15.5 156.1 %all-gather.9.cloned.1.call-start = ((), (), s32[]{:S(2)}) async-start(), calls=%async_computation.8 | async-start | bytes 2928640 | tf_op jit(solution)/shard_map/all_gather | solution.py:1155
  66.1 239.1 %all-gather.11.cloned.1.call-start = ((), (), s32[]{:S(2)}) async-start(), calls=%async_computation.9 | async-start | bytes 5632000 | tf_op jit(solution)/shard_map/all_gather | solution.py:1155
  74.3 241.1 %all-gather.7.cloned.1.call-start = ((), (), s32[]{:S(2)}) async-start(), calls=%async_computation.7 | async-start | bytes 2928640 | tf_op jit(solution)/shard_map/all_gather | solution.py:1155
  74.9 378.0 %reduce-scatter.7.cloned.1.call-start = ((), (), s32[]{:S(2)}) async-start(), calls=%async_computation.10 | async-start | bytes 5632000 | tf_op jit(solution)/shard_map/reduce_scatter | solution.py:1158
  75.8 188.6 %copy-start.44 = (f32[128,1600]{1,0:T(8,128)}, f32[128,1600]{1,0:T(8,128)S(1)}, u32[]{:S(2)}) copy-start(f32[128,1600]{1,0:T(8,128)S(1)} %copy.282) | copy-start | bytes 2457604
  125.6 103.1 %copy-start.110 = (f32[448]{0:T(512)}, f32[448]{0:T(512)S(1)}, u32[]{:S(2)}) copy-start(f32[448]{0:T(512)S(1)} %select_maximum_fusion.12) | copy-start | bytes 5380
  177.5 82.5 %copy-start.73 = (bf16[128,320]{0,1:T(8,128)(2,1)}, bf16[128,320]{0,1:T(8,128)(2,1)S(1)}, u32[]{:S(2)}) copy-start(bf16[128,320]{0,1:T(8,128)(2,1)S(1)} %get-tuple-element.276) | copy-start | bytes 245764
  192.4 36.3 %copy-start.2 = (f32[128,8,448]{2,1,0:T(8,128)}, f32[128,8,448]{2,1,0:T(8,128)S(1)}, u32[]{:S(2)}) copy-start(f32[128,8,448]{2,1,0:T(8,128)S(1)} %get-tuple-element.259.decay_step_ref) | copy-start | bytes 5505028
  237.8 22.1 %copy-start.64 = (bf16[128,1600]{0,1:T(8,128)(2,1)S(1)}, bf16[128,1600]{0,1:T(8,128)(2,1)}, u32[]{:S(2)}) copy-start(bf16[128,1600]{0,1:T(8,128)(2,1)} %slice.194) | copy-start | bytes 1228804
  334.2 151.7 %reduce-scatter.9.cloned.1.call-start = ((), (), s32[]{:S(2)}) async-start(), calls=%async_computation.11 | async-start | bytes 2928640 | tf_op jit(solution)/shard_map/reduce_scatter | solution.py:1158
  346.7 240.2 %reduce-scatter.13.cloned.1.call-start = ((), (), s32[]{:S(2)}) async-start(), calls=%async_computation.13 | async-start | bytes 1024000 | tf_op jit(solution)/shard_map/reduce_scatter | solution.py:1158
  361.5 36.0 %copy-start.47 = (f32[128,1600]{1,0:T(8,128)S(1)}, f32[128,1600]{1,0:T(8,128)}, u32[]{:S(2)}) copy-start(f32[128,1600]{1,0:T(8,128)} %copy-done.46) | copy-start | bytes 2457604
  452.5 134.5 %reduce-scatter.11.cloned.1.call-start = ((), (), s32[]{:S(2)}) async-start(), calls=%async_computation.12 | async-start | bytes 1863680 | tf_op jit(solution)/shard_map/reduce_scatter | solution.py:1158
  458.0 186.0 %reduce-scatter.15.cloned.1.call-start = ((), (), s32[]{:S(2)}) async-start(), calls=%async_computation.14 | async-start | bytes 3072000 | tf_op jit(solution)/shard_map/reduce_scatter | solution.py:1158
  482.1 168.9 %reduce-scatter.17.cloned.1.call-start = ((), (), s32[]{:S(2)}) async-start(), calls=%async_computation.15 | async-start | bytes 2048000 | tf_op jit(solution)/shard_map/reduce_scatter | solution.py:1158
  490.1 67.2 %copy-start.50 = (f32[1024,448]{1,0:T(8,128)S(1)}, f32[1024,448]{1,0:T(8,128)}, u32[]{:S(2)}) copy-start(f32[1024,448]{1,0:T(8,128)} %copy-done.49) | copy-start | bytes 5505028
  565.7 20.8 %copy-start.92 = (f32[16,100]{1,0:T(8,128)S(1)}, f32[16,100]{1,0:T(8,128)}, u32[]{:S(2)}) copy-start(f32[16,100]{1,0:T(8,128)} %copy-done.91) | copy-start | bytes 19204
  565.7 20.8 %copy-start.94 = (f32[16,100]{1,0:T(8,128)S(1)}, f32[16,100]{1,0:T(8,128)}, u32[]{:S(2)}) copy-start(f32[16,100]{1,0:T(8,128)} %copy-done.93) | copy-start | bytes 19204
  565.7 20.8 %copy-start.96 = (f32[16,100]{1,0:T(8,128)S(1)}, f32[16,100]{1,0:T(8,128)}, u32[]{:S(2)}) copy-start(f32[16,100]{1,0:T(8,128)} %copy-done.95) | copy-start | bytes 19204
  565.7 20.8 %copy-start.98 = (f32[16,100]{1,0:T(8,128)S(1)}, f32[16,100]{1,0:T(8,128)}, u32[]{:S(2)}) copy-start(f32[16,100]{1,0:T(8,128)} %copy-done.97) | copy-start | bytes 19204
  565.7 20.9 %copy-start.59 = (f32[128,8,132]{2,1,0:T(8,128)S(1)}, f32[128,8,132]{2,1,0:T(8,128)}, u32[]{:S(2)}) copy-start(f32[128,8,132]{2,1,0:T(8,128)} %copy.401) | copy-start | bytes 1622020
  565.7 20.9 %copy-start.63 = (bf16[1024,448]{1,0:T(8,128)(2,1)S(1)}, bf16[1024,448]{1,0:T(8,128)(2,1)}, u32[]{:S(2)}) copy-start(bf16[1024,448]{1,0:T(8,128)(2,1)} %copy-done.62) | copy-start | bytes 2752516
  566.3 20.7 %copy-start.100 = (f32[100,132]{0,1:T(8,128)S(1)}, f32[100,132]{0,1:T(8,128)}, u32[]{:S(2)}) copy-start(f32[100,132]{0,1:T(8,128)} %copy-done.99) | copy-start | bytes 158404
  566.3 20.7 %copy-start.102 = (f32[100,132]{0,1:T(8,128)S(1)}, f32[100,132]{0,1:T(8,128)}, u32[]{:S(2)}) copy-start(f32[100,132]{0,1:T(8,128)} %copy-done.101) | copy-start | bytes 158404
  566.4 20.7 %copy-start.104 = (f32[100,132]{0,1:T(8,128)S(1)}, f32[100,132]{0,1:T(8,128)}, u32[]{:S(2)}) copy-start(f32[100,132]{0,1:T(8,128)} %copy-done.103) | copy-start | bytes 158404
  566.4 20.7 %copy-start.106 = (f32[100,132]{0,1:T(8,128)S(1)}, f32[100,132]{0,1:T(8,128)}, u32[]{:S(2)}) copy-start(f32[100,132]{0,1:T(8,128)} %copy-done.105) | copy-start | bytes 158404
  616.1 22.0 %copy-start.45 = (f32[128,1600]{1,0:T(8,128)S(1)}, f32[128,1600]{1,0:T(8,128)}, u32[]{:S(2)}) copy-start(f32[128,1600]{1,0:T(8,128)} %copy-done.44) | copy-start | bytes 2457604
  616.1 22.0 %copy-start.90 = (f32[1600]{0:T(1024)S(1)}, f32[1600]{0:T(1024)}, u32[]{:S(2)}) copy-start(f32[1600]{0:T(1024)} %param.26) | copy-start | bytes 19204
  616.2 22.0 %copy-start.123 = (f32[128]{0:T(128)S(1)}, f32[128]{0:T(128)}, u32[]{:S(2)}) copy-start(f32[128]{0:T(128)} %copy-done.122) | copy-start | bytes 1540
  616.2 22.3 %copy-start.132 = (f32[128]{0:T(128)S(1)}, f32[128]{0:T(128)}, u32[]{:S(2)}) copy-start(f32[128]{0:T(128)} %copy-done.131) | copy-start | bytes 1540
  616.2 22.3 %copy-start.67 = (f32[128,1600]{1,0:T(8,128)S(1)}, f32[128,1600]{1,0:T(8,128)}, u32[]{:S(2)}) copy-start(f32[128,1600]{1,0:T(8,128)} %get-tuple-element.251) | copy-start | bytes 2457604
  (117 other events, 607.9 us)
Sparse Core Ops, SparseCore 0:
  15.7 99.8 all-gather.4
  117.7 48.6 all-gather.8
  168.5 84.7 all-gather.10
  254.7 48.6 all-gather.6
  334.3 89.4 reduce-scatter.6
  426.0 48.4 reduce-scatter.8
  476.9 23.1 reduce-scatter.12
  503.1 33.4 reduce-scatter.10
  539.5 48.5 reduce-scatter.14
  608.0 42.9 reduce-scatter.16

commit v4 on v3

--- a/solution.py
+++ b/solution.py
@@ -232,7 +232,7 @@
         for k in (1, 3) if square else range(1, chips):
             crossed[i][k - 1].wait_recv()
             total = total + arrived[k - 1].astype(f32)
-        totals[i][...] = total
+        totals[i][...] = total.astype(totals[i].dtype)
         if i >= n_sum:
             states.append(start_gather(totals[i], all_summed[i - n_sum], n_all + i))
     pass_on(states)
@@ -251,14 +251,13 @@
     reduced = (*sums, *alls)
     out_shape = [jax.ShapeDtypeStruct((rep,) + x.shape, x.dtype) for x in gathers]
     out_shape += [jax.ShapeDtypeStruct(x.shape[1:], f32) for x in sums]
-    out_shape += [jax.ShapeDtypeStruct(x.shape, f32) for x in alls]
-    out_shape += [jax.ShapeDtypeStruct(x.shape, x.dtype) for x in trades]
+    out_shape += [jax.ShapeDtypeStruct(x.shape, x.dtype) for x in (*alls, *trades)]
     scratch = []
     for x in reduced:
         scratch += [
             pltpu.VMEM((n,) + x.shape[1:], x.dtype) for n in (chips - 1, chips, chips - 1)
         ]
-    scratch += [pltpu.VMEM(x.shape[1:], f32) for x in alls]
+    scratch += [pltpu.VMEM(x.shape[1:], x.dtype) for x in alls]
     n_local = sum(counts) - len(sums) + 1
     n_slots = len(reduced) + len(alls) + len(gathers) + 1
     scratch += [
@@ -1215,11 +1214,6 @@
     in_seq_all = normed_sent[:, :, width].astype(f32).T.reshape(group, 1)
 
     in_out = dot(swapped(normed_all.reshape(rep, count, width)), full_in)
-    mout_mix = hand_on(mout_mix, in_out)
-    mout_mix = mout_mix.reshape(fsdp, -1, width)
-    full_mout = mout_mix[:, : part_mout.shape[0]].reshape(-1, width)
-    mix_t = mout_mix[:, part_mout.shape[0] :].reshape(fsdp, -1)[:, :mix_size]
-    mix_t = mix_t.reshape(width, mix_part).T
     xs, gate_z = in_out[:, :channels], in_out[:, gate_at : gate_at + channels]
     qkv_sent = in_out[:, channels : channels + qkv_part].astype(bf16)
     qkv_sent = swapped(qkv_sent.reshape(count, rep, qkv_part))
@@ -1233,12 +1227,18 @@
         earlier = jnp.where(in_seq_all >= k, shift_down(xs, k * rep), 0.0)
         conv_sum = conv_sum + earlier * conv_w[CONV - 1 - k]
     act, act_slope = silu_and_slope(conv_sum)
-    proj_sent = dot(act, part_x_proj, high).reshape(count, rep, -1).transpose(1, 0, 2)
+    proj_sent = dot(act, part_x_proj, high).astype(bf16).reshape(count, rep, -1)
+    proj_sent = proj_sent.transpose(1, 0, 2)
     proj, qkv_back = rep_exchange(
         rep, 2, alls=(proj_sent,), trades=(qkv_sent.reshape(rep, count, qkv_part),)
     )
+    mout_mix = hand_on(mout_mix, proj)
+    mout_mix = mout_mix.reshape(fsdp, -1, width)
+    full_mout = mout_mix[:, : part_mout.shape[0]].reshape(-1, width)
+    mix_t = mout_mix[:, part_mout.shape[0] :].reshape(fsdp, -1)[:, :mix_size]
+    mix_t = mix_t.reshape(width, mix_part).T
     qkv_low = qkv_back.transpose(1, 0, 2).reshape(count, rep * qkv_part)
-    proj = proj.transpose(1, 0, 2)
+    proj = proj.transpose(1, 0, 2).astype(f32)
     dt_in = proj.reshape(group, -1)[:, :DT_RANK]
     maps = proj[:, :, DT_RANK:]
     dt_sum = dot(dt_in, part_dt_proj, high) + part_dt_bias
@@ -1296,8 +1296,8 @@
     )
     qkv_cols = qkv_cols.reshape(group, qkv_part)
     ssm_all = tied(ssm_all, own_gate_up).reshape(group, width)
-    grad_mixer = dot_right_t(ssm_all, full_mout).reshape(rep, count, channels)
-    grad_mixer = swapped(grad_mixer)
+    grad_mixer = dot_right_t(ssm_all, full_mout).astype(bf16).reshape(rep, count, channels)
+    grad_mixer = swapped(grad_mixer).astype(f32)
     part_mout = dot_left_t(mixer_low, ssm_all).astype(bf16)
     part_mix = dot_left_t(mixed_all, middle_cols.reshape(group, -1)).astype(bf16)
 
@@ -1331,7 +1331,7 @@
     proj_sent = jnp.concatenate(
         [dot_right_t(grad_dt, part_dt_proj), grad_maps], axis=1
     )
-    proj_sent = proj_sent.reshape(count, rep, -1).transpose(1, 0, 2)
+    proj_sent = proj_sent.astype(bf16).reshape(count, rep, -1).transpose(1, 0, 2)
     (grad_proj,) = rep_exchange(rep, 11, alls=(proj_sent,))
     grad_proj = swapped(tied(grad_proj, own_mout, own_mix))
     grad_x_proj = dot_left_t(grad_proj, act)

time: 785 us -> 777 us (0.990)
  Pallas kernels: 463 us -> 452 us
    pallas_call x8, Pallas kernels: 226 us -> 214 us  [rep_exchange(): pl.pallas_call(functools.partial(rep_kernel, rep, counts, square), out_sh...]
    unnamed x287 -> x290, local copies, waits for them, and re-layouts: 50.7 us -> 51.2 us
  transfers between devices with their start and end apart: 10 -> 10, of which waited for: 1 -> 1; matrix products, arithmetic and copies ran while one was open for 27% -> 28% of each run, Pallas kernels for 48% -> 47%
where the time goes in v4:
time: 777 us; the launch traced here: 771 us
  Pallas kernels  452 us (58%)
  matrix products  124 us (16%)
  local copies, waits for them, and re-layouts  123 us (16%)
  other arithmetic  47.4 us (6%)
  between operations  16.4 us (2%)
  waiting for transfers between devices  7.91 us (1%)
    pallas_call x8, Pallas kernels, rep_exchange(): pl.pallas_call(functools.partial(rep_kernel, rep, counts, square), out_sh...  214 us
    pallas_call x1, Pallas kernels, last_exchange(): pl.pallas_call(functools.partial(last_kernel, rep, fsdp, rep == 8, n_gath...  71.9 us
    pallas_call x1, Pallas kernels, scan_backward(): pl.pallas_call(functools.partial(scan_back_kernel, rep, channels), grid=(...  66.8 us
    unnamed x290, local copies, waits for them, and re-layouts  51.2 us
    dot_general x7, matrix products, dot_right_t(): lax.dot_general(left, right, (((1,), (1,)), ((), ())), preferred_element_...  42.1 us
    pallas_call x1, Pallas kernels, line_exchange(): pl.pallas_call(functools.partial(line_kernel, count, (len(gathers), len(a...  41 us
    dot_general x10, matrix products, dot_left_t(): lax.dot_general(left, right, (((0,), (0,)), ((), ())), preferred_element_...  39.2 us
    dot_general x9, matrix products, dot(): return jnp.dot(left, right, precision=precision, preferred_element_type=f32)  38.2 us
  transfers between devices with their start and end apart: 10, of which 1 were waited for; matrix products, arithmetic and copies ran while one was open for 28% of the time, Pallas kernels for 47%

profile of v4, /device:TPU:0, one launch (start us, length us, event | category | flops | bytes accessed | tf_op | source)
XLA Modules:
  0.0 770.8 jit_solution(6256557919190482112)
XLA Ops:
  24.3 41.0 %shard_map.366 = (bf16[4,32,1600]{2,1,0:T(8,128)(2,1)}, bf16[4,32,1600]{2,1,0:T(8,128)(2,1)}) custom-call(bf16[4,32,1600]{2,1,0:T(8,128)(2,1)} %bitcast.299, bf16[4,32,1600]{2,1,0:T(8,128)(2,1)} %bitcast.300), custom_call_target="tpu_custom_call" | custom-call | bytes 10000 | tf_op jit(solution)/shard_map/pallas_call | solution.py:336
  77.9 33.1 %shard_map.367 = (bf16[8,128,1664]{2,1,0:T(8,128)(2,1)S(1)}, bf16[8,128,1600]{2,1,0:T(8,128)(2,1)S(1)}) custom-call(bf16[128,1664]{1,0:T(8,128)(2,1)S(1)} %pad_maximum_fusion.3.refs_0_, bf16[128,1600]{1,0:T(8,128)(2,1)S(1)} %copy.279.refs_1_), custom_call_target="tpu_custom_call" | custom-call | bytes 10000 | tf_op jit(solution)/shard_map/pallas_call | solution.py:269
  125.6 9.2 %fusion = f32[1024,1280]{1,0:T(8,128)S(1)} fusion(bf16[1600,1280]{1,0:T(8,128)(2,1)} %all-gather.5.cloned.1.call-done, bf16[128,8,1600]{2,0,1:T(8,128)(2,1)} %get-tuple-element.256), kind=kOutput, calls=%fused_computation.8 | convolution fusion | flops 4194304000 | bytes 12615680 | tf_op jit(solution)/shard_map/dot_general | solution.py:29
  145.0 21.5 %shard_map.368 = (bf16[8,128,132]{2,1,0:T(8,128)(2,1)S(1)}, bf16[8,128,280]{2,1,0:T(8,128)(2,1)S(1)}) custom-call(bf16[8,128,132]{2,1,0:T(8,128)(2,1)S(1)} %bitcast.254, bf16[8,128,280]{2,1,0:T(8,128)(2,1)S(1)} %bitcast.250), custom_call_target="tpu_custom_call" | custom-call | bytes 10000 | tf_op jit(solution)/shard_map/pallas_call | solution.py:269
  191.8 36.3 %shard_map.370 = (f32[128,8,448]{2,1,0:T(8,128)S(1)}, f32[16,128,8,512]{3,2,1,0:T(8,128)}, bf16[8,200,1600]{2,1,0:T(8,128)(2,1)}) custom-call(f32[128,8,448]{2,1,0:T(8,128)S(1)} %get-tuple-element.259.decay_step_ref, f32[128,8,448]{2,1,0:T(8,128)} %get-tuple-element.257.input_ref, f32[128,8,32]{2,1,0:T(8,128)S(1)} %copy.320.maps_ref, ...), custom_call_target="tpu_custom_call" | custom-call | bytes 10000 | tf_op jit(solution)/shard_map/pallas_call | solution.py:803
  237.3 22.1 %shard_map.371 = f32[128,1600]{1,0:T(8,128)S(1)} custom-call(bf16[8,128,1600]{2,1,0:T(8,128)(2,1)S(1)} %bitcast.247), custom_call_target="tpu_custom_call" | custom-call | bytes 10000 | tf_op jit(solution)/shard_map/pallas_call | solution.py:269
  263.9 4.4 multiply_reduce_fusion.13
  269.4 31.8 %shard_map.372 = (bf16[8,128,1600]{2,1,0:T(8,128)(2,1)S(1)}, bf16[8,128,1600]{2,1,0:T(8,128)(2,1)S(1)}) custom-call(bf16[128,1600]{1,0:T(8,128)(2,1)S(1)} %multiply_convert_fusion.4.refs_0_, bf16[128,1600]{1,0:T(8,128)(2,1)S(1)} %multiply_convert_fusion.5.refs_1_), custom_call_target="tpu_custom_call" | custom-call | bytes 10000 | tf_op jit(solution)/shard_map/pallas_call | solution.py:269
  304.7 10.2 %fusion.106 = f32[1024,1408]{0,1:T(8,128)} fusion(bf16[1024,1600]{1,0:T(8,128)(2,1)} %bitcast.268, bf16[1600,1408]{1,0:T(8,128)(2,1)} %all-gather.11.cloned.1.call-done), kind=kOutput, calls=%fused_computation.294 | convolution fusion | flops 4613734400 | bytes 13549568 | tf_op jit(solution)/shard_map/dot_general | solution.py:29
  314.9 9.4 %fusion.6 = (bf16[1024,704]{0,1:T(8,128)(2,1)S(1)}, bf16[1024,704]{0,1:T(8,128)(2,1)S(1)}, bf16[1024,704]{0,1:T(8,128)(2,1)}) fusion(f32[1024,1408]{0,1:T(8,128)} %fusion.106, bf16[1024,1600]{1,0:T(8,128)(2,1)} %bitcast.265, bf16[704,1600]{1,0:T(8,128)(2,1)} %all-gather.7.cloned.1.call-done), kind=kOutput, calls=%fused_computation.18 | convolution fusion | flops 2318401536 | bytes 15622144 | tf_op jit(solution)/shard_map/dot_general | solution.py:33
  325.9 7.7 %convolution_convert_fusion = bf16[1600,1408]{1,0:T(8,128)(2,1)} fusion(bf16[1024,1600]{1,0:T(8,128)(2,1)S(1)} %bitcast.269, bf16[1024,704]{0,1:T(8,128)(2,1)S(1)} %get-tuple-element.253, bf16[1024,704]{0,1:T(8,128)(2,1)S(1)} %get-tuple-element.252), kind=kOutput, calls=%fused_computation.1 | convolution fusion | flops 4621754368 | bytes 10665984 | tf_op jit(solution)/shard_map/dot_general | solution.py:37
  336.0 6.5 convolution_convert_fusion.6
  346.3 6.1 convolution_convert_fusion.1
  352.4 8.6 %convolution_convert_fusion.2 = bf16[1024,1600]{1,0:T(8,128)(2,1)S(1)} fusion(bf16[1024,1408]{0,1:T(8,128)(2,1)S(1)} %copy-done.69, bf16[1600,1408]{1,0:T(8,128)(2,1)} %all-gather.11.cloned.1.call-done), kind=kOutput, calls=%fused_computation.5 | convolution fusion | flops 4615372800 | bytes 10665984 | tf_op jit(solution)/shard_map/dot_general | solution.py:33
  361.0 35.8 %shard_map.374 = (f32[128,1600]{1,0:T(8,128)S(1)}, f32[128,1600]{1,0:T(8,128)S(1)}) custom-call(bf16[8,128,1600]{2,1,0:T(8,128)(2,1)S(1)} %bitcast.249, bf16[8,128,1600]{2,1,0:T(8,128)(2,1)S(1)} %bitcast.248), custom_call_target="tpu_custom_call" | custom-call | bytes 10000 | tf_op jit(solution)/shard_map/pallas_call | solution.py:269
  401.5 4.4 multiply_reduce_fusion.7
  412.4 33.7 %shard_map.375 = (bf16[8,128,1600]{2,1,0:T(8,128)(2,1)S(1)}, bf16[8,128,200]{2,1,0:T(8,128)(2,1)S(1)}, bf16[8,128,280]{2,1,0:T(8,128)(2,1)S(1)}) custom-call(bf16[128,1600]{1,0:T(8,128)(2,1)S(1)} %get-tuple-element.275.refs_0_, bf16[8,128,200]{2,1,0:T(8,128)(2,1)S(1)} %bitcast.253, bf16[8,128,280]{2,1,0:T(8,128)(2,1)S(1)} %bitcast.251), custom_call_target="tpu_custom_call" | custom-call | bytes 10000 | tf_op jit(solution)/shard_map/pallas_call | solution.py:269
  452.5 5.0 fusion.3
  457.8 4.3 convert_bitcast_fusion.1
  467.0 5.2 fusion.31
  475.6 6.4 convolution_convert_fusion.5
  485.8 4.2 fusion.91.grad_ref
  490.0 66.8 %shard_map.376 = (f32[128,8,448]{2,1,0:T(8,128)}, f32[128,8,448]{2,1,0:T(8,128)}, f32[16,448]{1,0:T(8,128)S(1)}, f32[128,8,128]{2,1,0:T(8,128)S(1)}, bf16[8,400,...) custom-call(f32[128,8,448]{2,1,0:T(8,128)} %copy-done.2, f32[128,8,448]{2,1,0:T(8,128)} %get-tuple-element.258.step_ref, ...), custom_call_target="tpu_custom_call" | custom-call | bytes 10000 | tf_op jit(solution)/shard_map/pallas_call | solution.py:962
  566.6 14.0 %shard_map.377 = bf16[8,128,132]{2,1,0:T(8,128)(2,1)S(1)} custom-call(bf16[8,128,132]{2,1,0:T(8,128)(2,1)S(1)} %maximum_bitcast_fusion.refs_0_), custom_call_target="tpu_custom_call" | custom-call | bytes 10000 | tf_op jit(solution)/shard_map/pallas_call | solution.py:269
  581.2 9.4 %multiply_reduce_fusion = (bf16[448]{0:T(512)(128)(2,1)S(1)}, bf16[448]{0:T(512)(128)(2,1)S(1)}, bf16[448]{0:T(512)(128)(2,1)S(1)}, bf16[448]{0:T(512)(128)(2,1)...) fusion(f32[1024,448]{1,0:T(8,128)} %bitcast.273, ...), kind=kOutput, calls=%fused_computation.37 | convolution fusion | flops 140181888 | bytes 24262656 | tf_op jit(solution)/shard_map/dot_general | solution.py:33
  594.7 5.1 bitcast_convert_fusion
  602.6 5.5 convolution_convert_fusion.4
  608.1 22.1 %shard_map.378 = f32[128,1600]{1,0:T(8,128)S(1)} custom-call(bf16[8,128,1600]{2,1,0:T(8,128)(2,1)S(1)} %bitcast.246), custom_call_target="tpu_custom_call" | custom-call | bytes 10000 | tf_op jit(solution)/shard_map/pallas_call | solution.py:269
  636.0 7.1 reduce-scatter.17.cloned.1.call-done.refs_5_
  648.9 71.9 %shard_map.379 = (bf16[400,5504]{1,0:T(8,128)(2,1)}, bf16[400,5504]{1,0:T(8,128)(2,1)}, bf16[1600,1376]{1,0:T(8,128)(2,1)}, bf16[8,112,1600]{2,1,0:T(8,128)(2,1)...) custom-call(bf16[8,400,1408]{2,1,0:T(8,128)(2,1)} %get-tuple-element, ...), custom_call_target="tpu_custom_call" | custom-call | bytes 10000 | tf_op jit(solution)/shard_map/pallas_call | solution.py:542
  731.6 4.4 convert_bitcast_fusion
  754.0 9.7 %shard_map.380 = (f32[400,6400]{1,0:T(8,128)}, f32[400,2240]{1,0:T(8,128)}, f32[400,1600]{1,0:T(8,128)}) custom-call(bf16[8,400,448]{2,1,0:T(8,128)(2,1)S(1)} %copy-done.12, bf16[8,400,768]{2,1,0:T(8,128)(2,1)} %get-tuple-element.106.refs_1_, bf16[8,400,200]{2,1,0:T(8,128)(2,1)S(1)} %copy-done.17), custom_call_target="tpu_custom_call" | custom-call | bytes 10000 | tf_op jit(solution)/shard_map/pallas_call | solution.py:692
  (482 shorter events, 191.5 us)
Async XLA Ops:
  7.2 118.4 %all-gather.5.cloned.1.call-start = ((), (), s32[]{:S(2)}) async-start(), calls=%async_computation.6 | async-start | bytes 5120000 | tf_op jit(solution)/shard_map/all_gather | solution.py:1154
  15.5 151.1 %all-gather.9.cloned.1.call-start = ((), (), s32[]{:S(2)}) async-start(), calls=%async_computation.8 | async-start | bytes 2928640 | tf_op jit(solution)/shard_map/all_gather | solution.py:1154
  66.1 238.6 %all-gather.11.cloned.1.call-start = ((), (), s32[]{:S(2)}) async-start(), calls=%async_computation.9 | async-start | bytes 5632000 | tf_op jit(solution)/shard_map/all_gather | solution.py:1154
  74.3 240.6 %all-gather.7.cloned.1.call-start = ((), (), s32[]{:S(2)}) async-start(), calls=%async_computation.7 | async-start | bytes 2928640 | tf_op jit(solution)/shard_map/all_gather | solution.py:1154
  74.9 377.5 %reduce-scatter.7.cloned.1.call-start = ((), (), s32[]{:S(2)}) async-start(), calls=%async_computation.10 | async-start | bytes 5632000 | tf_op jit(solution)/shard_map/reduce_scatter | solution.py:1157
  75.8 188.1 %copy-start.44 = (f32[128,1600]{1,0:T(8,128)}, f32[128,1600]{1,0:T(8,128)S(1)}, u32[]{:S(2)}) copy-start(f32[128,1600]{1,0:T(8,128)S(1)} %copy.278) | copy-start | bytes 2457604
  117.6 19.9 %copy-start.113 = (f32[1,448]{1,0:T(1,128)}, f32[1,448]{1,0:T(1,128)S(1)}, u32[]{:S(2)}) copy-start(f32[1,448]{1,0:T(1,128)S(1)} %get-tuple-element.298) | copy-start | bytes 5380
  117.6 19.9 %copy-start.115 = (f32[1,448]{1,0:T(1,128)}, f32[1,448]{1,0:T(1,128)S(1)}, u32[]{:S(2)}) copy-start(f32[1,448]{1,0:T(1,128)S(1)} %get-tuple-element.299) | copy-start | bytes 5380
  117.7 19.9 %copy-start.117 = (f32[1,448]{1,0:T(1,128)}, f32[1,448]{1,0:T(1,128)S(1)}, u32[]{:S(2)}) copy-start(f32[1,448]{1,0:T(1,128)S(1)} %get-tuple-element.300) | copy-start | bytes 5380
  117.7 19.9 %copy-start.119 = (f32[1,448]{1,0:T(1,128)}, f32[1,448]{1,0:T(1,128)S(1)}, u32[]{:S(2)}) copy-start(f32[1,448]{1,0:T(1,128)S(1)} %get-tuple-element.301) | copy-start | bytes 5380
  118.8 18.8 %copy-start.125 = (pred[1024]{0:T(1024)(128)(4,1)}, pred[1024]{0:T(1024)(128)(4,1)S(1)}, u32[]{:S(2)}) copy-start(pred[1024]{0:T(1024)(128)(4,1)S(1)} %ge.86) | copy-start | bytes 3076
  120.6 19.6 %copy-start.100 = (f32[100,132]{0,1:T(8,128)}, f32[100,132]{0,1:T(8,128)S(1)}, u32[]{:S(2)}) copy-start(f32[100,132]{0,1:T(8,128)S(1)} %get-tuple-element.266) | copy-start | bytes 158404
  120.6 19.6 %copy-start.102 = (f32[100,132]{0,1:T(8,128)}, f32[100,132]{0,1:T(8,128)S(1)}, u32[]{:S(2)}) copy-start(f32[100,132]{0,1:T(8,128)S(1)} %get-tuple-element.267) | copy-start | bytes 158404
  120.6 19.6 %copy-start.104 = (f32[100,132]{0,1:T(8,128)}, f32[100,132]{0,1:T(8,128)S(1)}, u32[]{:S(2)}) copy-start(f32[100,132]{0,1:T(8,128)S(1)} %get-tuple-element.268) | copy-start | bytes 158404
  120.6 19.6 %copy-start.106 = (f32[100,132]{0,1:T(8,128)}, f32[100,132]{0,1:T(8,128)S(1)}, u32[]{:S(2)}) copy-start(f32[100,132]{0,1:T(8,128)S(1)} %get-tuple-element.269) | copy-start | bytes 158404
  125.6 102.5 %copy-start.111 = (f32[448]{0:T(512)}, f32[448]{0:T(512)S(1)}, u32[]{:S(2)}) copy-start(f32[448]{0:T(512)S(1)} %select_maximum_fusion.12) | copy-start | bytes 5380
  166.6 19.8 %copy-start.58 = (f32[128,8,132]{2,0,1:T(8,128)}, f32[128,8,132]{2,0,1:T(8,128)S(1)}, u32[]{:S(2)}) copy-start(f32[128,8,132]{2,0,1:T(8,128)S(1)} %bitcast_convert_fusion.1) | copy-start | bytes 1622020
  176.6 82.8 %copy-start.74 = (bf16[128,320]{0,1:T(8,128)(2,1)}, bf16[128,320]{0,1:T(8,128)(2,1)S(1)}, u32[]{:S(2)}) copy-start(bf16[128,320]{0,1:T(8,128)(2,1)S(1)} %get-tuple-element.276) | copy-start | bytes 245764
  191.8 36.3 %copy-start.2 = (f32[128,8,448]{2,1,0:T(8,128)}, f32[128,8,448]{2,1,0:T(8,128)S(1)}, u32[]{:S(2)}) copy-start(f32[128,8,448]{2,1,0:T(8,128)S(1)} %get-tuple-element.259.decay_step_ref) | copy-start | bytes 5505028
  237.2 22.2 %copy-start.64 = (bf16[128,1600]{0,1:T(8,128)(2,1)S(1)}, bf16[128,1600]{0,1:T(8,128)(2,1)}, u32[]{:S(2)}) copy-start(bf16[128,1600]{0,1:T(8,128)(2,1)} %slice.195) | copy-start | bytes 1228804
  333.7 152.1 %reduce-scatter.9.cloned.1.call-start = ((), (), s32[]{:S(2)}) async-start(), calls=%async_computation.11 | async-start | bytes 2928640 | tf_op jit(solution)/shard_map/reduce_scatter | solution.py:1157
  346.2 234.8 %reduce-scatter.13.cloned.1.call-start = ((), (), s32[]{:S(2)}) async-start(), calls=%async_computation.13 | async-start | bytes 1024000 | tf_op jit(solution)/shard_map/reduce_scatter | solution.py:1157
  361.0 35.8 %copy-start.47 = (f32[128,1600]{1,0:T(8,128)S(1)}, f32[128,1600]{1,0:T(8,128)}, u32[]{:S(2)}) copy-start(f32[128,1600]{1,0:T(8,128)} %copy-done.46) | copy-start | bytes 2457604
  452.0 129.1 %reduce-scatter.11.cloned.1.call-start = ((), (), s32[]{:S(2)}) async-start(), calls=%async_computation.12 | async-start | bytes 1863680 | tf_op jit(solution)/shard_map/reduce_scatter | solution.py:1157
  457.5 178.5 %reduce-scatter.15.cloned.1.call-start = ((), (), s32[]{:S(2)}) async-start(), calls=%async_computation.14 | async-start | bytes 3072000 | tf_op jit(solution)/shard_map/reduce_scatter | solution.py:1157
  482.0 161.1 %reduce-scatter.17.cloned.1.call-start = ((), (), s32[]{:S(2)}) async-start(), calls=%async_computation.15 | async-start | bytes 2048000 | tf_op jit(solution)/shard_map/reduce_scatter | solution.py:1157
  490.0 67.2 %copy-start.50 = (f32[1024,448]{1,0:T(8,128)S(1)}, f32[1024,448]{1,0:T(8,128)}, u32[]{:S(2)}) copy-start(f32[1024,448]{1,0:T(8,128)} %copy-done.49) | copy-start | bytes 5505028
  608.1 22.2 %copy-start.45 = (f32[128,1600]{1,0:T(8,128)S(1)}, f32[128,1600]{1,0:T(8,128)}, u32[]{:S(2)}) copy-start(f32[128,1600]{1,0:T(8,128)} %copy-done.44) | copy-start | bytes 2457604
  608.1 22.2 %copy-start.91 = (f32[1600]{0:T(1024)S(1)}, f32[1600]{0:T(1024)}, u32[]{:S(2)}) copy-start(f32[1600]{0:T(1024)} %param.26) | copy-start | bytes 19204
  608.1 22.2 %copy-start.124 = (f32[128]{0:T(128)S(1)}, f32[128]{0:T(128)}, u32[]{:S(2)}) copy-start(f32[128]{0:T(128)} %copy-done.123) | copy-start | bytes 1540
  608.1 22.5 %copy-start.133 = (f32[128]{0:T(128)S(1)}, f32[128]{0:T(128)}, u32[]{:S(2)}) copy-start(f32[128]{0:T(128)} %copy-done.132) | copy-start | bytes 1540
  608.1 22.5 %copy-start.67 = (f32[128,1600]{1,0:T(8,128)S(1)}, f32[128,1600]{1,0:T(8,128)}, u32[]{:S(2)}) copy-start(f32[128,1600]{1,0:T(8,128)} %get-tuple-element.251) | copy-start | bytes 2457604
  (118 other events, 560.2 us)
Sparse Core Ops, SparseCore 0:
  15.7 99.8 all-gather.4
  117.7 48.6 all-gather.8
  168.5 84.6 all-gather.10
  254.7 48.6 all-gather.6
  333.8 89.5 reduce-scatter.6
  425.6 48.4 reduce-scatter.8
  476.5 23.1 reduce-scatter.12
  502.7 33.4 reduce-scatter.10
  539.1 48.5 reduce-scatter.14
  600.0 43.0 reduce-scatter.16

commit v5 on v4

--- a/solution.py
+++ b/solution.py
@@ -869,7 +869,7 @@
     at = (pl.program_id(0) * pl.num_programs(1) + pl.program_id(1)) * pl.num_programs(2)
     at = at + pl.program_id(2)
     last = pl.num_programs(0) * pl.num_programs(1) * pl.num_programs(2) - 1
-    steps = [at == step for step in (0, 10 * last // 16, 14 * last // 16)]
+    steps = [at == step for step in (0, 9 * last // 16, 12 * last // 16)]
     pairs = [(beside_ref, beside_out_ref), (beside2_ref, beside2_out_ref)]
     finish = spread_beside(rep, steps, pairs, local, far, near)
     tile, chunk = pl.program_id(1), pl.program_id(2)

time: 777 us -> 780 us (level)
  no operation moved by 1% of the time
where the time goes in v5:
time: 780 us; the launch traced here: 773 us
  Pallas kernels  454 us (58%)
  matrix products  124 us (16%)
  local copies, waits for them, and re-layouts  123 us (16%)
  other arithmetic  47.4 us (6%)
  between operations  16.4 us (2%)
  waiting for transfers between devices  7.99 us (1%)
    pallas_call x8, Pallas kernels, rep_exchange(): pl.pallas_call(functools.partial(rep_kernel, rep, counts, square), out_sh...  214 us
    pallas_call x1, Pallas kernels, last_exchange(): pl.pallas_call(functools.partial(last_kernel, rep, fsdp, rep == 8, n_gath...  71.8 us
    pallas_call x1, Pallas kernels, scan_backward(): pl.pallas_call(functools.partial(scan_back_kernel, rep, channels), grid=(...  69.2 us
    unnamed x290, local copies, waits for them, and re-layouts  51.1 us
    dot_general x7, matrix products, dot_right_t(): lax.dot_general(left, right, (((1,), (1,)), ((), ())), preferred_element_...  42.1 us
    pallas_call x1, Pallas kernels, line_exchange(): pl.pallas_call(functools.partial(line_kernel, count, (len(gathers), len(a...  41 us
    dot_general x10, matrix products, dot_left_t(): lax.dot_general(left, right, (((0,), (0,)), ((), ())), preferred_element_...  39.2 us
    dot_general x9, matrix products, dot(): return jnp.dot(left, right, precision=precision, preferred_element_type=f32)  38.2 us
  transfers between devices with their start and end apart: 10, of which 1 were waited for; matrix products, arithmetic and copies ran while one was open for 28% of the time, Pallas kernels for 47%

profile of v5, /device:TPU:0, one launch (start us, length us, event | category | flops | bytes accessed | tf_op | source)
XLA Modules:
  0.0 773.2 jit_solution(10033004143919429342)
XLA Ops:
  24.3 41.0 %shard_map.366 = (bf16[4,32,1600]{2,1,0:T(8,128)(2,1)}, bf16[4,32,1600]{2,1,0:T(8,128)(2,1)}) custom-call(bf16[4,32,1600]{2,1,0:T(8,128)(2,1)} %bitcast.299, bf16[4,32,1600]{2,1,0:T(8,128)(2,1)} %bitcast.300), custom_call_target="tpu_custom_call" | custom-call | bytes 10000 | tf_op jit(solution)/shard_map/pallas_call | solution.py:336
  77.9 33.1 %shard_map.367 = (bf16[8,128,1664]{2,1,0:T(8,128)(2,1)S(1)}, bf16[8,128,1600]{2,1,0:T(8,128)(2,1)S(1)}) custom-call(bf16[128,1664]{1,0:T(8,128)(2,1)S(1)} %pad_maximum_fusion.3.refs_0_, bf16[128,1600]{1,0:T(8,128)(2,1)S(1)} %copy.279.refs_1_), custom_call_target="tpu_custom_call" | custom-call | bytes 10000 | tf_op jit(solution)/shard_map/pallas_call | solution.py:269
  125.6 9.2 %fusion = f32[1024,1280]{1,0:T(8,128)S(1)} fusion(bf16[1600,1280]{1,0:T(8,128)(2,1)} %all-gather.5.cloned.1.call-done, bf16[128,8,1600]{2,0,1:T(8,128)(2,1)} %get-tuple-element.256), kind=kOutput, calls=%fused_computation.8 | convolution fusion | flops 4194304000 | bytes 12615680 | tf_op jit(solution)/shard_map/dot_general | solution.py:29
  145.0 21.5 %shard_map.368 = (bf16[8,128,132]{2,1,0:T(8,128)(2,1)S(1)}, bf16[8,128,280]{2,1,0:T(8,128)(2,1)S(1)}) custom-call(bf16[8,128,132]{2,1,0:T(8,128)(2,1)S(1)} %bitcast.254, bf16[8,128,280]{2,1,0:T(8,128)(2,1)S(1)} %bitcast.250), custom_call_target="tpu_custom_call" | custom-call | bytes 10000 | tf_op jit(solution)/shard_map/pallas_call | solution.py:269
  191.8 36.3 %shard_map.370 = (f32[128,8,448]{2,1,0:T(8,128)S(1)}, f32[16,128,8,512]{3,2,1,0:T(8,128)}, bf16[8,200,1600]{2,1,0:T(8,128)(2,1)}) custom-call(f32[128,8,448]{2,1,0:T(8,128)S(1)} %get-tuple-element.259.decay_step_ref, f32[128,8,448]{2,1,0:T(8,128)} %get-tuple-element.257.input_ref, f32[128,8,32]{2,1,0:T(8,128)S(1)} %copy.320.maps_ref, ...), custom_call_target="tpu_custom_call" | custom-call | bytes 10000 | tf_op jit(solution)/shard_map/pallas_call | solution.py:803
  237.3 22.1 %shard_map.371 = f32[128,1600]{1,0:T(8,128)S(1)} custom-call(bf16[8,128,1600]{2,1,0:T(8,128)(2,1)S(1)} %bitcast.247), custom_call_target="tpu_custom_call" | custom-call | bytes 10000 | tf_op jit(solution)/shard_map/pallas_call | solution.py:269
  263.9 4.4 multiply_reduce_fusion.13
  269.4 31.8 %shard_map.372 = (bf16[8,128,1600]{2,1,0:T(8,128)(2,1)S(1)}, bf16[8,128,1600]{2,1,0:T(8,128)(2,1)S(1)}) custom-call(bf16[128,1600]{1,0:T(8,128)(2,1)S(1)} %multiply_convert_fusion.4.refs_0_, bf16[128,1600]{1,0:T(8,128)(2,1)S(1)} %multiply_convert_fusion.5.refs_1_), custom_call_target="tpu_custom_call" | custom-call | bytes 10000 | tf_op jit(solution)/shard_map/pallas_call | solution.py:269
  304.7 10.2 %fusion.106 = f32[1024,1408]{0,1:T(8,128)} fusion(bf16[1024,1600]{1,0:T(8,128)(2,1)} %bitcast.268, bf16[1600,1408]{1,0:T(8,128)(2,1)} %all-gather.11.cloned.1.call-done), kind=kOutput, calls=%fused_computation.294 | convolution fusion | flops 4613734400 | bytes 13549568 | tf_op jit(solution)/shard_map/dot_general | solution.py:29
  314.9 9.4 %fusion.6 = (bf16[1024,704]{0,1:T(8,128)(2,1)S(1)}, bf16[1024,704]{0,1:T(8,128)(2,1)S(1)}, bf16[1024,704]{0,1:T(8,128)(2,1)}) fusion(f32[1024,1408]{0,1:T(8,128)} %fusion.106, bf16[1024,1600]{1,0:T(8,128)(2,1)} %bitcast.265, bf16[704,1600]{1,0:T(8,128)(2,1)} %all-gather.7.cloned.1.call-done), kind=kOutput, calls=%fused_computation.18 | convolution fusion | flops 2318401536 | bytes 15622144 | tf_op jit(solution)/shard_map/dot_general | solution.py:33
  325.9 7.7 convolution_convert_fusion
  336.0 6.5 convolution_convert_fusion.6
  346.3 6.1 convolution_convert_fusion.1
  352.4 8.6 %convolution_convert_fusion.2 = bf16[1024,1600]{1,0:T(8,128)(2,1)S(1)} fusion(bf16[1024,1408]{0,1:T(8,128)(2,1)S(1)} %copy-done.69, bf16[1600,1408]{1,0:T(8,128)(2,1)} %all-gather.11.cloned.1.call-done), kind=kOutput, calls=%fused_computation.5 | convolution fusion | flops 4615372800 | bytes 10665984 | tf_op jit(solution)/shard_map/dot_general | solution.py:33
  361.0 35.8 %shard_map.374 = (f32[128,1600]{1,0:T(8,128)S(1)}, f32[128,1600]{1,0:T(8,128)S(1)}) custom-call(bf16[8,128,1600]{2,1,0:T(8,128)(2,1)S(1)} %bitcast.249, bf16[8,128,1600]{2,1,0:T(8,128)(2,1)S(1)} %bitcast.248), custom_call_target="tpu_custom_call" | custom-call | bytes 10000 | tf_op jit(solution)/shard_map/pallas_call | solution.py:269
  401.5 4.4 multiply_reduce_fusion.7
  412.4 33.7 %shard_map.375 = (bf16[8,128,1600]{2,1,0:T(8,128)(2,1)S(1)}, bf16[8,128,200]{2,1,0:T(8,128)(2,1)S(1)}, bf16[8,128,280]{2,1,0:T(8,128)(2,1)S(1)}) custom-call(bf16[128,1600]{1,0:T(8,128)(2,1)S(1)} %get-tuple-element.275.refs_0_, bf16[8,128,200]{2,1,0:T(8,128)(2,1)S(1)} %bitcast.253, bf16[8,128,280]{2,1,0:T(8,128)(2,1)S(1)} %bitcast.251), custom_call_target="tpu_custom_call" | custom-call | bytes 10000 | tf_op jit(solution)/shard_map/pallas_call | solution.py:269
  452.5 5.0 fusion.3
  457.8 4.3 convert_bitcast_fusion.1
  467.0 5.2 fusion.31
  475.6 6.4 convolution_convert_fusion.5
  485.8 4.2 fusion.91.grad_ref
  490.0 69.2 %shard_map.376 = (f32[128,8,448]{2,1,0:T(8,128)}, f32[128,8,448]{2,1,0:T(8,128)}, f32[16,448]{1,0:T(8,128)S(1)}, f32[128,8,128]{2,1,0:T(8,128)S(1)}, bf16[8,400,...) custom-call(f32[128,8,448]{2,1,0:T(8,128)} %copy-done.2, f32[128,8,448]{2,1,0:T(8,128)} %get-tuple-element.258.step_ref, ...), custom_call_target="tpu_custom_call" | custom-call | bytes 10000 | tf_op jit(solution)/shard_map/pallas_call | solution.py:962
  569.0 14.2 %shard_map.377 = bf16[8,128,132]{2,1,0:T(8,128)(2,1)S(1)} custom-call(bf16[8,128,132]{2,1,0:T(8,128)(2,1)S(1)} %maximum_bitcast_fusion.refs_0_), custom_call_target="tpu_custom_call" | custom-call | bytes 10000 | tf_op jit(solution)/shard_map/pallas_call | solution.py:269
  583.8 9.4 %multiply_reduce_fusion = (bf16[448]{0:T(512)(128)(2,1)S(1)}, bf16[448]{0:T(512)(128)(2,1)S(1)}, bf16[448]{0:T(512)(128)(2,1)S(1)}, bf16[448]{0:T(512)(128)(2,1)...) fusion(f32[1024,448]{1,0:T(8,128)} %bitcast.273, ...), kind=kOutput, calls=%fused_computation.37 | convolution fusion | flops 140181888 | bytes 24262656 | tf_op jit(solution)/shard_map/dot_general | solution.py:33
  597.3 5.1 bitcast_convert_fusion
  605.2 5.5 convolution_convert_fusion.4
  610.7 21.8 %shard_map.378 = f32[128,1600]{1,0:T(8,128)S(1)} custom-call(bf16[8,128,1600]{2,1,0:T(8,128)(2,1)S(1)} %bitcast.246), custom_call_target="tpu_custom_call" | custom-call | bytes 10000 | tf_op jit(solution)/shard_map/pallas_call | solution.py:269
  638.3 7.2 reduce-scatter.17.cloned.1.call-done.refs_5_
  651.3 71.8 %shard_map.379 = (bf16[400,5504]{1,0:T(8,128)(2,1)}, bf16[400,5504]{1,0:T(8,128)(2,1)}, bf16[1600,1376]{1,0:T(8,128)(2,1)}, bf16[8,112,1600]{2,1,0:T(8,128)(2,1)...) custom-call(bf16[8,400,1408]{2,1,0:T(8,128)(2,1)} %get-tuple-element, ...), custom_call_target="tpu_custom_call" | custom-call | bytes 10000 | tf_op jit(solution)/shard_map/pallas_call | solution.py:542
  734.0 4.4 convert_bitcast_fusion
  756.4 9.7 %shard_map.380 = (f32[400,6400]{1,0:T(8,128)}, f32[400,2240]{1,0:T(8,128)}, f32[400,1600]{1,0:T(8,128)}) custom-call(bf16[8,400,448]{2,1,0:T(8,128)(2,1)S(1)} %copy-done.12, bf16[8,400,768]{2,1,0:T(8,128)(2,1)} %get-tuple-element.106.refs_1_, bf16[8,400,200]{2,1,0:T(8,128)(2,1)S(1)} %copy-done.17), custom_call_target="tpu_custom_call" | custom-call | bytes 10000 | tf_op jit(solution)/shard_map/pallas_call | solution.py:692
  (482 shorter events, 191.5 us)
Async XLA Ops:
  7.2 118.4 %all-gather.5.cloned.1.call-start = ((), (), s32[]{:S(2)}) async-start(), calls=%async_computation.6 | async-start | bytes 5120000 | tf_op jit(solution)/shard_map/all_gather | solution.py:1154
  15.5 151.1 %all-gather.9.cloned.1.call-start = ((), (), s32[]{:S(2)}) async-start(), calls=%async_computation.8 | async-start | bytes 2928640 | tf_op jit(solution)/shard_map/all_gather | solution.py:1154
  66.1 238.6 %all-gather.11.cloned.1.call-start = ((), (), s32[]{:S(2)}) async-start(), calls=%async_computation.9 | async-start | bytes 5632000 | tf_op jit(solution)/shard_map/all_gather | solution.py:1154
  74.3 240.6 %all-gather.7.cloned.1.call-start = ((), (), s32[]{:S(2)}) async-start(), calls=%async_computation.7 | async-start | bytes 2928640 | tf_op jit(solution)/shard_map/all_gather | solution.py:1154
  74.9 377.5 %reduce-scatter.7.cloned.1.call-start = ((), (), s32[]{:S(2)}) async-start(), calls=%async_computation.10 | async-start | bytes 5632000 | tf_op jit(solution)/shard_map/reduce_scatter | solution.py:1157
  75.8 188.1 %copy-start.44 = (f32[128,1600]{1,0:T(8,128)}, f32[128,1600]{1,0:T(8,128)S(1)}, u32[]{:S(2)}) copy-start(f32[128,1600]{1,0:T(8,128)S(1)} %copy.278) | copy-start | bytes 2457604
  117.6 19.9 %copy-start.113 = (f32[1,448]{1,0:T(1,128)}, f32[1,448]{1,0:T(1,128)S(1)}, u32[]{:S(2)}) copy-start(f32[1,448]{1,0:T(1,128)S(1)} %get-tuple-element.298) | copy-start | bytes 5380
  117.6 19.9 %copy-start.115 = (f32[1,448]{1,0:T(1,128)}, f32[1,448]{1,0:T(1,128)S(1)}, u32[]{:S(2)}) copy-start(f32[1,448]{1,0:T(1,128)S(1)} %get-tuple-element.299) | copy-start | bytes 5380
  117.7 19.9 %copy-start.117 = (f32[1,448]{1,0:T(1,128)}, f32[1,448]{1,0:T(1,128)S(1)}, u32[]{:S(2)}) copy-start(f32[1,448]{1,0:T(1,128)S(1)} %get-tuple-element.300) | copy-start | bytes 5380
  117.7 19.9 %copy-start.119 = (f32[1,448]{1,0:T(1,128)}, f32[1,448]{1,0:T(1,128)S(1)}, u32[]{:S(2)}) copy-start(f32[1,448]{1,0:T(1,128)S(1)} %get-tuple-element.301) | copy-start | bytes 5380
  118.8 18.8 %copy-start.125 = (pred[1024]{0:T(1024)(128)(4,1)}, pred[1024]{0:T(1024)(128)(4,1)S(1)}, u32[]{:S(2)}) copy-start(pred[1024]{0:T(1024)(128)(4,1)S(1)} %ge.86) | copy-start | bytes 3076
  120.6 19.6 %copy-start.100 = (f32[100,132]{0,1:T(8,128)}, f32[100,132]{0,1:T(8,128)S(1)}, u32[]{:S(2)}) copy-start(f32[100,132]{0,1:T(8,128)S(1)} %get-tuple-element.266) | copy-start | bytes 158404
  120.6 19.6 %copy-start.102 = (f32[100,132]{0,1:T(8,128)}, f32[100,132]{0,1:T(8,128)S(1)}, u32[]{:S(2)}) copy-start(f32[100,132]{0,1:T(8,128)S(1)} %get-tuple-element.267) | copy-start | bytes 158404
  120.6 19.6 %copy-start.104 = (f32[100,132]{0,1:T(8,128)}, f32[100,132]{0,1:T(8,128)S(1)}, u32[]{:S(2)}) copy-start(f32[100,132]{0,1:T(8,128)S(1)} %get-tuple-element.268) | copy-start | bytes 158404
  120.6 19.6 %copy-start.106 = (f32[100,132]{0,1:T(8,128)}, f32[100,132]{0,1:T(8,128)S(1)}, u32[]{:S(2)}) copy-start(f32[100,132]{0,1:T(8,128)S(1)} %get-tuple-element.269) | copy-start | bytes 158404
  125.6 102.5 %copy-start.111 = (f32[448]{0:T(512)}, f32[448]{0:T(512)S(1)}, u32[]{:S(2)}) copy-start(f32[448]{0:T(512)S(1)} %select_maximum_fusion.12) | copy-start | bytes 5380
  166.6 19.8 %copy-start.58 = (f32[128,8,132]{2,0,1:T(8,128)}, f32[128,8,132]{2,0,1:T(8,128)S(1)}, u32[]{:S(2)}) copy-start(f32[128,8,132]{2,0,1:T(8,128)S(1)} %bitcast_convert_fusion.1) | copy-start | bytes 1622020
  176.6 82.8 %copy-start.74 = (bf16[128,320]{0,1:T(8,128)(2,1)}, bf16[128,320]{0,1:T(8,128)(2,1)S(1)}, u32[]{:S(2)}) copy-start(bf16[128,320]{0,1:T(8,128)(2,1)S(1)} %get-tuple-element.276) | copy-start | bytes 245764
  191.8 36.3 %copy-start.2 = (f32[128,8,448]{2,1,0:T(8,128)}, f32[128,8,448]{2,1,0:T(8,128)S(1)}, u32[]{:S(2)}) copy-start(f32[128,8,448]{2,1,0:T(8,128)S(1)} %get-tuple-element.259.decay_step_ref) | copy-start | bytes 5505028
  237.2 22.2 %copy-start.64 = (bf16[128,1600]{0,1:T(8,128)(2,1)S(1)}, bf16[128,1600]{0,1:T(8,128)(2,1)}, u32[]{:S(2)}) copy-start(bf16[128,1600]{0,1:T(8,128)(2,1)} %slice.195) | copy-start | bytes 1228804
  333.7 152.1 %reduce-scatter.9.cloned.1.call-start = ((), (), s32[]{:S(2)}) async-start(), calls=%async_computation.11 | async-start | bytes 2928640 | tf_op jit(solution)/shard_map/reduce_scatter | solution.py:1157
  346.2 237.5 %reduce-scatter.13.cloned.1.call-start = ((), (), s32[]{:S(2)}) async-start(), calls=%async_computation.13 | async-start | bytes 1024000 | tf_op jit(solution)/shard_map/reduce_scatter | solution.py:1157
  361.0 35.8 %copy-start.47 = (f32[128,1600]{1,0:T(8,128)S(1)}, f32[128,1600]{1,0:T(8,128)}, u32[]{:S(2)}) copy-start(f32[128,1600]{1,0:T(8,128)} %copy-done.46) | copy-start | bytes 2457604
  452.0 131.8 %reduce-scatter.11.cloned.1.call-start = ((), (), s32[]{:S(2)}) async-start(), calls=%async_computation.12 | async-start | bytes 1863680 | tf_op jit(solution)/shard_map/reduce_scatter | solution.py:1157
  457.5 180.8 %reduce-scatter.15.cloned.1.call-start = ((), (), s32[]{:S(2)}) async-start(), calls=%async_computation.14 | async-start | bytes 3072000 | tf_op jit(solution)/shard_map/reduce_scatter | solution.py:1157
  482.0 163.5 %reduce-scatter.17.cloned.1.call-start = ((), (), s32[]{:S(2)}) async-start(), calls=%async_computation.15 | async-start | bytes 2048000 | tf_op jit(solution)/shard_map/reduce_scatter | solution.py:1157
  490.0 69.6 %copy-start.50 = (f32[1024,448]{1,0:T(8,128)S(1)}, f32[1024,448]{1,0:T(8,128)}, u32[]{:S(2)}) copy-start(f32[1024,448]{1,0:T(8,128)} %copy-done.49) | copy-start | bytes 5505028
  610.7 21.9 %copy-start.45 = (f32[128,1600]{1,0:T(8,128)S(1)}, f32[128,1600]{1,0:T(8,128)}, u32[]{:S(2)}) copy-start(f32[128,1600]{1,0:T(8,128)} %copy-done.44) | copy-start | bytes 2457604
  610.7 21.9 %copy-start.91 = (f32[1600]{0:T(1024)S(1)}, f32[1600]{0:T(1024)}, u32[]{:S(2)}) copy-start(f32[1600]{0:T(1024)} %param.26) | copy-start | bytes 19204
  610.7 21.9 %copy-start.124 = (f32[128]{0:T(128)S(1)}, f32[128]{0:T(128)}, u32[]{:S(2)}) copy-start(f32[128]{0:T(128)} %copy-done.123) | copy-start | bytes 1540
  610.7 22.2 %copy-start.133 = (f32[128]{0:T(128)S(1)}, f32[128]{0:T(128)}, u32[]{:S(2)}) copy-start(f32[128]{0:T(128)} %copy-done.132) | copy-start | bytes 1540
  610.7 22.2 %copy-start.67 = (f32[128,1600]{1,0:T(8,128)S(1)}, f32[128,1600]{1,0:T(8,128)}, u32[]{:S(2)}) copy-start(f32[128,1600]{1,0:T(8,128)} %get-tuple-element.251) | copy-start | bytes 2457604
  (118 other events, 563.5 us)
Sparse Core Ops, SparseCore 0:
  15.7 99.8 all-gather.4
  117.7 48.6 all-gather.8
  168.5 84.6 all-gather.10
  254.7 48.6 all-gather.6
  333.8 89.5 reduce-scatter.6
  425.6 48.4 reduce-scatter.8
  476.5 23.1 reduce-scatter.12
  502.7 33.4 reduce-scatter.10
  539.1 48.5 reduce-scatter.14
  602.6 42.8 reduce-scatter.16
